TPU v7x, 32 devices: a whole 2x2x4 slice. The times are simulated.
32 devices in a mesh: dp: 8 (over z, y), mp: 4 (over x, core).
Axes of the slice: x: 2, y: 2, z: 4, core: 2. Of those that a mesh axis runs over, the one named last changes fastest.
Arguments:
- frames: bfloat16 [8704, 84, 336], P(('dp', 'mp')), may hold values from -4 to 4
- send_rows: int32 [16384], P(('dp', 'mp')), may hold values from 0 to 271, as said below
- recv_counts: int32 [256], P(('dp', 'mp')), may hold values from 1 to 64, as said below
- actions: int32 [16384], P(('dp', 'mp')), may hold values from 0 to 17
- target_dist: float32 [16384, 51], P(('dp', 'mp')), may hold values from 0 to 1, as said below
- sample_weight: float32 [16384], P(('dp', 'mp')), may hold values from 0.1 to 1
- conv_first: float32 [256, 32], P('dp'), may hold values from -0.5 to 0.5
- conv_second: float32 [512, 64], P('dp'), may hold values from -0.5 to 0.5
- conv_third: float32 [576, 64], P('dp'), may hold values from -0.5 to 0.5
- hidden_mean: float32 [2, 3136, 512], P(None, None, ('mp', 'dp')), may hold values from -0.15625 to 0.15625
- hidden_spread: float32 [2, 3136, 512], P(None, None, ('mp', 'dp')), may hold values from -0.078125 to 0.078125
- hidden_bias: float32 [2, 512], P(None, ('mp', 'dp')), may hold values from -1.5 to 1.5
- feature_noise: float32 [2, 3136], replicated, may hold values from -4 to 4
- hidden_noise: float32 [2, 2, 512], P(None, None, ('mp', 'dp')), may hold values from -4 to 4
- value_mean: float32 [512, 51], P(('mp', 'dp')), may hold values from -0.75 to 0.75
- value_spread: float32 [512, 51], P(('mp', 'dp')), may hold values from -0.375 to 0.375
- advantage_mean: float32 [512, 918], P(('mp', 'dp')), may hold values from -0.75 to 0.75
- advantage_spread: float32 [512, 918], P(('mp', 'dp')), may hold values from -0.375 to 0.375
- output_noise: float32 [969], replicated, may hold values from -4 to 4
- output_bias: float32 [969], replicated, may hold values from -2.5 to 2.5
Outputs:
- mean_loss: float32 [], replicated
- conv_first_grad: float32 [256, 32], P('dp')
- conv_second_grad: float32 [512, 64], P('dp')
- conv_third_grad: float32 [576, 64], P('dp')
- hidden_mean_grad: float32 [2, 3136, 512], P(None, None, ('mp', 'dp'))
- hidden_spread_grad: float32 [2, 3136, 512], P(None, None, ('mp', 'dp'))
- hidden_bias_grad: float32 [2, 512], P(None, ('mp', 'dp'))
- value_mean_grad: float32 [512, 51], P(('mp', 'dp'))
- value_spread_grad: float32 [512, 51], P(('mp', 'dp'))
- advantage_mean_grad: float32 [512, 918], P(('mp', 'dp'))
- advantage_spread_grad: float32 [512, 918], P(('mp', 'dp'))
- output_bias_grad: float32 [969], replicated
- priorities: float32 [16384], P(('dp', 'mp'))
Inputs may be any that keep to these rules, and one draw needn't show every extreme that they name: `send_rows`: the 64 send slots that one replay shard sends to one learner name different rows of that shard; a row may go to several learners, and every row of a shard is sent. `recv_counts`: entry g * 8 + s: how many of the 64 slots that device s * 4 + (g % 4) sends to device g are used, always its first ones; in every draw some device uses all 64 slots from every source. `target_dist`: each row is positive and sums to one.
All inputs are finite; a program needn't handle non-finite values.
Results may differ from a plain program's by a relative error of at most 0.011.
Values may be sent and summed in bfloat16 or wider, within the bound.
A program may use at most 384 MiB of HBM per device.

v0:
```python
import jax
import jax.numpy as jnp
from jax import lax
from jax.sharding import PartitionSpec as P


def in_blocks(shard, dim, devices):
    before, after = (shard.shape[:dim], shard.shape[dim + 1 :])
    return jnp.moveaxis(shard.reshape(*before, devices, -1, *after), dim, 0)


def summed_on_arrival(shard, axis, dim):
    blocks = in_blocks(shard, dim, lax.axis_size(axis))
    arrived = lax.all_to_all(blocks, axis, split_axis=0, concat_axis=0, tiled=True)
    return arrived.astype(jnp.float32).sum(axis=0)


def side_by_side(arrays, axis, dim, along):
    both = jnp.concatenate(arrays, axis=along)
    result, at, outs = (summed_on_arrival(both, axis, dim), 0, [])
    for a in arrays:
        outs.append(lax.slice_in_dim(result, at, at + a.shape[along], axis=along))
        at += a.shape[along]
    return tuple(outs)


def silu_value(values):
    return values * jax.nn.sigmoid(values)


def silu_slope(values):
    logistic = jax.nn.sigmoid(values)
    return logistic * (1.0 + values * (1.0 - logistic))


def to_depth(values, factor):
    batch_rows, height, breadth, channels = values.shape
    moved = values.reshape(
        batch_rows, height // factor, factor, breadth // factor, factor, channels
    )
    moved = moved.transpose(0, 1, 3, 2, 4, 5)
    return moved.reshape(
        batch_rows, height // factor, breadth // factor, factor * factor * channels
    )


def from_depth(values, factor, channels):
    batch_rows, height, breadth = (values.shape[0], values.shape[1], values.shape[2])
    moved = values.reshape(batch_rows, height, breadth, factor, factor, channels).transpose(
        0, 1, 3, 2, 4, 5
    )
    return moved.reshape(batch_rows, height * factor, breadth * factor, channels)


def shifted_conv(source, kernel, extent, out_side):
    summed = jnp.zeros((source.shape[0], out_side, out_side, kernel.shape[3]), jnp.float32)
    for shift_row in range(extent):
        for shift_col in range(extent):
            window = source[
                :, shift_row : shift_row + out_side, shift_col : shift_col + out_side, :
            ]
            summed = summed + jnp.einsum(
                "npqc,cd->npqd",
                window,
                kernel[shift_row, shift_col],
                preferred_element_type=jnp.float32,
            )
    return summed


def kernel_grad(source, grad_out, extent):
    out_side = grad_out.shape[1]
    blocks = []
    for shift_row in range(extent):
        for shift_col in range(extent):
            window = source[
                :, shift_row : shift_row + out_side, shift_col : shift_col + out_side, :
            ]
            blocks.append(
                jnp.einsum("npqc,npqd->cd", window, grad_out, preferred_element_type=jnp.float32)
            )
    return jnp.stack(blocks).reshape(-1, grad_out.shape[3])


def input_grad(grad_out, kernel, extent, in_side):
    out_side = grad_out.shape[1]
    summed = jnp.zeros((grad_out.shape[0], in_side, in_side, kernel.shape[2]), jnp.float32)
    for shift_row in range(extent):
        for shift_col in range(extent):
            shifted_piece = jnp.einsum(
                "npqd,cd->npqc",
                grad_out,
                kernel[shift_row, shift_col],
                preferred_element_type=jnp.float32,
            )
            summed = summed + jnp.pad(
                shifted_piece,
                (
                    (0, 0),
                    (shift_row, in_side - out_side - shift_row),
                    (shift_col, in_side - out_side - shift_col),
                    (0, 0),
                ),
            )
    return summed


def torso_forward(frame_rows, kern_one, kern_two, kern_three):
    batch_rows, side_len = (frame_rows.shape[0], frame_rows.shape[1])
    depth_in = to_depth(frame_rows.reshape(batch_rows, side_len, side_len, 4), 4)
    side_one = depth_in.shape[1] - 1
    pre_one = shifted_conv(depth_in, kern_one.reshape(2, 2, depth_in.shape[3], -1), 2, side_one)
    act_one = silu_value(pre_one).astype(jnp.bfloat16)
    depth_two = to_depth(act_one, 2)
    side_two = depth_two.shape[1] - 1
    pre_two = shifted_conv(depth_two, kern_two.reshape(2, 2, depth_two.shape[3], -1), 2, side_two)
    act_two = silu_value(pre_two).astype(jnp.bfloat16)
    pre_three = shifted_conv(
        act_two, kern_three.reshape(3, 3, act_two.shape[3], -1), 3, side_two - 2
    )
    features = silu_value(pre_three).astype(jnp.bfloat16).reshape(batch_rows, -1)
    return (features, (depth_in, pre_one, depth_two, pre_two, act_two, pre_three))


def torso_backward(saved_acts, feat_grad, kern_two, kern_three):
    depth_in, pre_one, depth_two, pre_two, act_two, pre_three = saved_acts
    grad_three = feat_grad.astype(jnp.float32).reshape(pre_three.shape) * silu_slope(pre_three)
    grad_three = grad_three.astype(jnp.bfloat16)
    kern_grad_three = kernel_grad(act_two, grad_three, 3)
    back_two = input_grad(
        grad_three, kern_three.reshape(3, 3, act_two.shape[3], -1), 3, act_two.shape[1]
    )
    grad_two = (back_two * silu_slope(pre_two)).astype(jnp.bfloat16)
    kern_grad_two = kernel_grad(depth_two, grad_two, 2)
    back_depth = input_grad(
        grad_two, kern_two.reshape(2, 2, depth_two.shape[3], -1), 2, depth_two.shape[1]
    )
    back_one = from_depth(back_depth, 2, pre_one.shape[3])
    grad_first = (back_one * silu_slope(pre_one)).astype(jnp.bfloat16)
    kern_grad_one = kernel_grad(depth_in, grad_first, 2)
    return (kern_grad_one, kern_grad_two, kern_grad_three)


def on_device(
    frames,
    send_rows,
    recv_counts,
    actions,
    target_dist,
    sample_weight,
    conv_first,
    conv_second,
    conv_third,
    hidden_mean,
    hidden_spread,
    hidden_bias,
    feature_noise,
    hidden_noise,
    value_mean,
    value_spread,
    advantage_mean,
    advantage_spread,
    output_noise,
    output_bias,
):
    dp_count = lax.axis_size("dp")
    slot_count = send_rows.shape[0]
    capacity = slot_count // dp_count
    atom_count = value_mean.shape[1]
    action_count = advantage_mean.shape[1] // atom_count
    wide_one = hidden_mean + hidden_spread * feature_noise[:, :, None] * hidden_noise[0][:, None, :]
    wide_val = (
        value_mean + value_spread * hidden_noise[1, 0][:, None] * output_noise[None, :atom_count]
    )
    wide_adv = (
        advantage_mean
        + advantage_spread * hidden_noise[1, 1][:, None] * output_noise[None, atom_count:]
    )
    gathered = (
        lax.all_gather(conv_first.astype(jnp.bfloat16), "dp", axis=0, tiled=True),
        lax.all_gather(conv_second.astype(jnp.bfloat16), "dp", axis=0, tiled=True),
        lax.all_gather(conv_third.astype(jnp.bfloat16), "dp", axis=0, tiled=True),
        lax.all_gather(wide_one.astype(jnp.bfloat16), "dp", axis=2, tiled=True),
        lax.all_gather(hidden_bias.astype(jnp.bfloat16), "dp", axis=1, tiled=True),
        lax.all_gather(wide_val.astype(jnp.bfloat16), "dp", axis=0, tiled=True),
        lax.all_gather(wide_adv.astype(jnp.bfloat16), "dp", axis=0, tiled=True),
    )
    kern_one, kern_two, kern_three, head_one, head_bias, head_val, head_adv = gathered
    routed = lax.all_to_all(frames[send_rows], "dp", split_axis=0, concat_axis=0, tiled=True)
    features, saved_acts = torso_forward(routed, kern_one, kern_two, kern_three)
    inputs = lax.all_gather(features, "mp", axis=0, tiled=True)
    pre_hid = jnp.einsum("rf,ifh->rih", inputs, head_one, preferred_element_type=jnp.float32)
    pre_hid = pre_hid + head_bias.astype(jnp.float32)[None, :, :]
    hidden = silu_value(pre_hid).astype(jnp.bfloat16)
    row_block = hidden
    logit_sum = lax.psum_scatter(
        jnp.concatenate(
            [
                jnp.dot(row_block[:, 0], head_val, preferred_element_type=jnp.float32),
                jnp.dot(row_block[:, 1], head_adv, preferred_element_type=jnp.float32),
            ],
            axis=1,
        ).astype(jnp.bfloat16),
        "mp",
        scatter_dimension=0,
        tiled=True,
    ).astype(jnp.float32)
    logits = logit_sum + output_bias[None, :]
    value_part = logits[:, :atom_count]
    adv_part = logits[:, atom_count:].reshape(slot_count, action_count, atom_count)
    chosen_mask = (actions[:, None] == jnp.arange(action_count, dtype=jnp.int32)[None, :]).astype(
        jnp.float32
    )
    chosen = jnp.sum(chosen_mask[:, :, None] * adv_part, axis=1)
    q_atoms = value_part + chosen - jnp.mean(adv_part, axis=1)
    row_top = jnp.max(q_atoms, axis=1, keepdims=True)
    shifted = jnp.exp(q_atoms - row_top)
    total_exp = jnp.sum(shifted, axis=1, keepdims=True)
    log_prob = q_atoms - row_top - jnp.log(total_exp)
    cross = -jnp.sum(target_dist * log_prob, axis=1)
    is_valid = jnp.arange(capacity, dtype=jnp.int32)[None, :] < recv_counts[:, None]
    is_valid = is_valid.astype(jnp.float32).reshape(slot_count)
    loss_coeff = is_valid * sample_weight
    priority = is_valid * cross
    prio_back = lax.all_to_all(priority, "dp", split_axis=0, concat_axis=0, tiled=True)
    q_grad = loss_coeff[:, None] * (
        shifted / total_exp * jnp.sum(target_dist, axis=1, keepdims=True) - target_dist
    )
    adv_grad = chosen_mask[:, :, None] * q_grad[:, None, :] - q_grad[:, None, :] / action_count
    logit_grad = jnp.concatenate([q_grad, adv_grad.reshape(slot_count, -1)], axis=1).astype(
        jnp.bfloat16
    )
    grad_rows = lax.all_gather(logit_grad, "mp", axis=0, tiled=True)
    grad_val = jnp.einsum(
        "rh,rz->hz", hidden[:, 0], grad_rows[:, :atom_count], preferred_element_type=jnp.float32
    )
    grad_adv = jnp.einsum(
        "rh,rz->hz", hidden[:, 1], grad_rows[:, atom_count:], preferred_element_type=jnp.float32
    )
    hid_grad = jnp.stack(
        [
            jnp.einsum(
                "rz,hz->rh", grad_rows[:, :atom_count], head_val, preferred_element_type=jnp.float32
            ),
            jnp.einsum(
                "rz,hz->rh", grad_rows[:, atom_count:], head_adv, preferred_element_type=jnp.float32
            ),
        ],
        axis=1,
    )
    pre_grad = (hid_grad * silu_slope(pre_hid)).astype(jnp.bfloat16)
    grad_one = jnp.einsum("rf,rih->ifh", inputs, pre_grad, preferred_element_type=jnp.float32)
    grad_bias = jnp.sum(pre_grad.astype(jnp.float32), axis=0)
    row_block = pre_grad
    feat_grad = lax.psum_scatter(
        jnp.einsum("rih,ifh->rf", row_block, head_one, preferred_element_type=jnp.float32).astype(
            jnp.bfloat16
        ),
        "mp",
        scatter_dimension=0,
        tiled=True,
    ).astype(jnp.float32)
    feat_grad = feat_grad.astype(jnp.bfloat16)
    kern_grad_one, kern_grad_two, kern_grad_three = torso_backward(
        saved_acts, feat_grad, kern_two, kern_three
    )
    shard_sums = (
        summed_on_arrival(kern_grad_one.astype(jnp.bfloat16), "dp", 0),
        summed_on_arrival(kern_grad_two.astype(jnp.bfloat16), "dp", 0),
        summed_on_arrival(kern_grad_three.astype(jnp.bfloat16), "dp", 0),
        summed_on_arrival(grad_one.astype(jnp.bfloat16), "dp", 2),
        summed_on_arrival(grad_bias.astype(jnp.bfloat16), "dp", 1),
        *side_by_side((grad_val.astype(jnp.bfloat16), grad_adv.astype(jnp.bfloat16)), "dp", 0, 1),
    )
    conv_sums = lax.psum((shard_sums[0], shard_sums[1], shard_sums[2]), "mp")
    tail_total = lax.psum(
        (
            jnp.sum(loss_coeff * cross),
            jnp.sum(is_valid),
            jnp.sum(logit_grad.astype(jnp.float32), axis=0),
        ),
        ("dp", "mp"),
    )
    inverse = 1.0 / tail_total[1]
    mean_loss = tail_total[0] * inverse
    hidden_mean_grad = shard_sums[3] * inverse
    hidden_spread_grad = hidden_mean_grad * feature_noise[:, :, None] * hidden_noise[0][:, None, :]
    value_mean_grad = shard_sums[5] * inverse
    value_spread_grad = (
        value_mean_grad * hidden_noise[1, 0][:, None] * output_noise[None, :atom_count]
    )
    advantage_mean_grad = shard_sums[6] * inverse
    advantage_spread_grad = (
        advantage_mean_grad * hidden_noise[1, 1][:, None] * output_noise[None, atom_count:]
    )
    return (
        mean_loss,
        conv_sums[0] * inverse,
        conv_sums[1] * inverse,
        conv_sums[2] * inverse,
        hidden_mean_grad,
        hidden_spread_grad,
        shard_sums[4] * inverse,
        value_mean_grad,
        value_spread_grad,
        advantage_mean_grad,
        advantage_spread_grad,
        tail_total[2] * inverse,
        prio_back,
    )


def solution(mesh):
    return jax.shard_map(
        on_device,
        mesh=mesh,
        in_specs=(
            P(("dp", "mp"), None, None),
            P(("dp", "mp")),
            P(("dp", "mp")),
            P(("dp", "mp")),
            P(("dp", "mp"), None),
            P(("dp", "mp")),
            P("dp", None),
            P("dp", None),
            P("dp", None),
            P(None, None, ("mp", "dp")),
            P(None, None, ("mp", "dp")),
            P(None, ("mp", "dp")),
            P(),
            P(None, None, ("mp", "dp")),
            P(("mp", "dp"), None),
            P(("mp", "dp"), None),
            P(("mp", "dp"), None),
            P(("mp", "dp"), None),
            P(),
            P(),
        ),
        out_specs=(
            P(),
            P("dp", None),
            P("dp", None),
            P("dp", None),
            P(None, None, ("mp", "dp")),
            P(None, None, ("mp", "dp")),
            P(None, ("mp", "dp")),
            P(("mp", "dp"), None),
            P(("mp", "dp"), None),
            P(("mp", "dp"), None),
            P(("mp", "dp"), None),
            P(),
            P(("dp", "mp")),
        ),
        check_vma=False,
    )
```

profile of v0, /device:TPU:0, one launch (start us, length us, event | category | flops | bytes accessed | tf_op | source)
XLA Modules:
  0.0 1944.7 jit_solution(17856065479296526421)
XLA Ops:
  7.9 68.8 %gather_fusion = bf16[512,84,336]{2,0,1:T(8,128)(2,1)} fusion(bf16[272,84,336]{2,0,1:T(8,128)(2,1)} %param.20, s32[1024]{0:T(1024)S(1)} %pad_clamp_fusion), kind=kCustom, calls=%fused_computation | custom fusion | bytes 57804800 | tf_op jit(solution)/shard_map/gather | solution.py:189
  76.7 23.4 %copy.251 = bf16[512,84,336]{2,1,0:T(8,128)(2,1)} copy(bf16[512,84,336]{2,0,1:T(8,128)(2,1)} %gather_fusion) | data formatting | bytes 57802752 | tf_op jit(solution)/shard_map/gather | solution.py:189
  100.1 7.4 all-to-all-start
  109.1 784.5 %all-gather = bf16[8,72,64]{1,2,0:T(8,128)(2,1)S(1)} all-gather(bf16[1,72,64]{1,2,0:T(8,128)(2,1)S(1)} %convert_bitcast_fusion), channel_id=1, replica_groups=mesh['dp'=8,'mp'=4] {'dp'}, dimensions={0}, use_global_device_ids=true | all-gather | bytes 82944 | tf_op jit(solution)/shard_map/all_gather | solution.py:182
  894.3 30.5 %all_gather.27 = bf16[256,32]{1,0:T(8,128)(2,1)S(1)} all-gather(bf16[32,32]{1,0:T(8,128)(2,1)S(1)} %convert_element_type.148), channel_id=1, replica_groups=mesh['dp'=8,'mp'=4] {'dp'}, dimensions={0}, use_global_device_ids=true | all-gather | bytes 18432 | tf_op jit(solution)/shard_map/all_gather | solution.py:180
  924.8 32.7 %all_gather.28 = bf16[512,64]{1,0:T(8,128)(2,1)} all-gather(bf16[64,64]{1,0:T(8,128)(2,1)S(1)} %convert_element_type.150), channel_id=1, replica_groups=mesh['dp'=8,'mp'=4] {'dp'}, dimensions={0}, use_global_device_ids=true | all-gather | bytes 73728 | tf_op jit(solution)/shard_map/all_gather | solution.py:181
  957.6 41.6 %copy.252 = bf16[512,84,336]{0,2,1:T(8,128)(2,1)} copy(bf16[512,84,336]{2,1,0:T(8,128)(2,1)} %all-to-all-done) | data formatting | bytes 57802752 | tf_op jit(solution)/shard_map/all_to_all | solution.py:189
  999.1 47.6 %reshape_reshape.3 = bf16[512,21,4,21,4,4]{0,5,4,3,2,1:T(4,128)(2,1)} reshape(bf16[512,84,336]{0,2,1:T(8,128)(2,1)} %copy.252) | data formatting | bytes 57802752 | tf_op jit(solution)/shard_map/reshape;reshape | solution.py:38
  1046.7 20.4 %copy.253 = bf16[512,21,21,4,4,4]{0,5,4,3,2,1:T(4,128)(2,1)} copy(bf16[512,21,21,4,4,4]{0,5,4,2,3,1:T(4,128)(2,1)} %bitcast.555) | data formatting | bytes 57802752 | tf_op jit(solution)/shard_map/transpose | solution.py:41
  1067.1 45.4 %reshape.182 = bf16[512,21,21,64]{0,3,2,1:T(8,128)(2,1)} reshape(bf16[512,21,21,4,4,4]{0,5,4,3,2,1:T(4,128)(2,1)} %copy.253) | data formatting | bytes 57802752 | tf_op jit(solution)/shard_map/reshape | solution.py:42
  1112.5 19.0 fusion
  1131.5 19.1 fusion.2
  1150.6 20.1 %fusion.4 = f32[512,20,20,32]{0,3,2,1:T(8,128)} fusion(bf16[512,21,21,64]{0,3,2,1:T(8,128)(2,1)} %reshape.182, bf16[2,2,64,32]{3,2,1,0:T(8,128)(2,1)S(1)} %bitcast.592), kind=kOutput, calls=%fused_computation.5 | convolution fusion | flops 838860800 | bytes 52445184 | tf_op jit(solution)/shard_map/npqc,cd->npqd/dot_general | solution.py:62
  1170.7 47.0 %multiply_convert_fusion.1 = (bf16[512,20,20,32]{0,3,2,1:T(8,128)(2,1)}, f32[512,20,20,32]{0,3,2,1:T(8,128)}) fusion(f32[512,20,20,32]{0,3,2,1:T(8,128)} %fusion, f32[512,20,20,32]{0,3,2,1:T(8,128)} %fusion.2, f32[512,20,20,32]{0,3,2,1:T(8,128)} %fusion.4, bf16[512,21,21,64]{0,3,2,1:T(8,128)(2,1)} %reshape.182, bf16[2,2,64,32]{3,2,1,0:T(8,128)(2,1)S(1)} %bitcast.593), kind=kOutput, calls=%fused_computation.11 | convolution fusion | flops 891289600 | bytes 144195584 | tf_op jit(solution)/shard_map/npqc,cd->npqd/dot_general | solution.py:62
  1217.7 6.4 copy.259
  1229.5 5.8 fusion.141
  1240.1 22.3 %multiply_convert_fusion.3 = (bf16[512,9,9,64]{0,3,2,1:T(8,128)(2,1)}, f32[512,9,9,64]{0,3,2,1:T(8,128)}) fusion(bf16[512,10,10,128]{0,3,2,1:T(8,128)(2,1)} %bitcast.546, bf16[2,2,128,64]{3,2,1,0:T(8,128)(2,1)S(1)} %bitcast.583, f32[512,9,9,64]{0,3,2,1:T(8,128)} %fusion.143, f32[512,9,9,64]{0,3,2,1:T(8,128)} %fusion.139, f32[512,9,9,64]{0,3,2,1:T(8,128)} %fusion.141), kind=kOutput, calls=%fused_computation.28 | convolution fusion | flops 700710912 | bytes 60915712 | tf_op jit(solution)/shard_map/npqc,cd->npqd/dot_general | solution.py:62
  1289.3 18.1 multiply_convert_fusion.4
  1307.6 18.8 all-gather.1
  1326.6 30.4 %all_gather.33 = bf16[128,51]{1,0:T(8,128)(2,1)S(1)} all-gather(bf16[16,51]{1,0:T(8,128)(2,1)S(1)} %add_convert_fusion.2), channel_id=1, replica_groups=mesh['dp'=8,'mp'=4] {'dp'}, dimensions={0}, use_global_device_ids=true | all-gather | bytes 14688 | tf_op jit(solution)/shard_map/all_gather | solution.py:185
  1357.1 30.7 %all_gather.34 = bf16[128,918]{1,0:T(8,128)(2,1)S(1)} all-gather(bf16[16,918]{1,0:T(8,128)(2,1)S(1)} %add_convert_fusion.1), channel_id=1, replica_groups=mesh['dp'=8,'mp'=4] {'dp'}, dimensions={0}, use_global_device_ids=true | all-gather | bytes 264384 | tf_op jit(solution)/shard_map/all_gather | solution.py:186
  1390.5 8.4 multiply_convert_fusion.5
  1404.8 42.1 %reduce-scatter.3.cloned.1.call-done = bf16[512,969]{0,1:T(8,128)(2,1)} async-done(((bf16[2048,969]{0,1:T(8,128)(2,1)}), bf16[512,969]{0,1:T(8,128)(2,1)}) %reduce-scatter.3.cloned.1.call-update) | async-done | bytes 992272 | tf_op jit(solution)/shard_map/reduce_scatter | solution.py:196
  1460.8 33.5 %all-gather.10.cloned.1.call-done = bf16[2048,969]{0,1:T(8,128)(2,1)} async-done(((bf16[512,969]{0,1:T(8,128)(2,1)}), bf16[2048,969]{0,1:T(8,128)(2,1)}) %all-gather.10.cloned.1.call-update) | async-done | bytes 3969040 | tf_op jit(solution)/shard_map/all_gather | solution.py:233
  1500.2 6.6 bitcast_convert_fusion
  1535.3 9.8 fusion.26
  1549.3 5.9 all-to-all-start.4
  1556.2 55.3 %all-reduce.13 = (f32[]{:T(128)}, f32[]{:T(128)}, f32[969]{0:T(1024)S(1)}) all-reduce(f32[]{:T(128)} %get-tuple-element.85, f32[]{:T(128)} %convert_reduce_fusion.7, f32[969]{0:T(1024)S(1)} %convert_reduce_fusion.1), channel_id=1, replica_groups=mesh['dp'=8,'mp'=4] {'dp','mp'}, use_global_device_ids=true, to_apply=%region_7.0 | all-reduce | flops 971 | bytes 7768 | tf_op jit(solution)/shard_map/psum | solution.py:276
  1646.7 5.6 fusion.151
  1652.3 5.5 fusion.149
  1663.3 27.4 %multiply_convert_fusion.2 = bf16[512,9,9,64]{0,3,2,1:T(8,128)(2,1)} fusion(f32[512,9,9,64]{0,3,2,1:T(8,128)} %get-tuple-element.95, f32[512,9,9,64]{0,3,2,1:T(8,128)} %fusion.151, f32[512,7,7,64]{0,3,2,1:T(8,128)} %fusion.150, f32[512,9,9,64]{0,3,2,1:T(8,128)} %fusion.149, f32[512,9,9,64]{0,3,2,1:T(8,128)} %fusion.148, f32[512,7,7,64]{0,3,2,1:T(8,128)} %fusion.147, ...), kind=kOutput, calls=%fused_computation.27 | convolution fusion | flops 250642432 | bytes 83116032 | tf_op jit(solution)/shard_map/jit(_pad)/pad | solution.py:96
  1690.7 10.0 fusion.96
  1700.8 10.0 fusion.99
  1710.8 6.2 fusion.102
  1717.0 6.3 fusion.105
  1723.3 11.2 fusion.138
  1734.6 8.8 fusion.140
  1743.4 8.8 fusion.142
  1752.2 33.1 %add_add_fusion = f32[512,10,10,128]{0,3,2,1:T(8,128)} fusion(f32[512,9,9,128]{0,3,2,1:T(8,128)} %fusion.142, f32[512,9,9,128]{0,3,2,1:T(8,128)} %fusion.140, f32[512,9,9,128]{0,3,2,1:T(8,128)} %fusion.138, bf16[512,9,9,64]{0,3,2,1:T(8,128)(2,1)} %multiply_convert_fusion.2, bf16[2,2,128,64]{3,2,1,0:T(8,128)(2,1)S(1)} %bitcast.587), kind=kOutput, calls=%fused_computation.10 | convolution fusion | flops 699138048 | bytes 95256576 | tf_op jit(solution)/shard_map/jit(_pad)/pad | solution.py:96
  1785.3 10.0 copy.289
  1795.3 18.3 multiply_convert_fusion
  1813.7 15.7 fusion.130
  1829.4 15.8 fusion.131
  1845.2 15.9 fusion.132
  1861.1 16.2 fusion.133
  1895.8 5.5 all-to-all-done.1
  1916.2 7.1 all-to-all-done.3
  1923.4 11.1 all-reduce.14
  (248 shorter events, 176.9 us)
Async XLA Ops:
  100.1 857.5 %all-to-all-start = ((bf16[512,84,336]{2,1,0:T(8,128)(2,1)}), bf16[512,84,336]{2,1,0:T(8,128)(2,1)}, u32[]{:S(2)}, u32[]{:S(2)}) async-start(bf16[512,84,336]{2,1,0:T(8,128)(2,1)} %copy.251), calls=%async_computation | async-start | bytes 69206016 | tf_op jit(solution)/shard_map/all_to_all | solution.py:189
  107.5 1280.3 %all-gather.8.cloned.1.call-start = ((), (), s32[]{:S(2)}) async-start(), calls=%async_computation.11 | async-start | bytes 1843200 | tf_op jit(solution)/shard_map/all_gather | solution.py:183
  109.0 1281.5 %all-gather.6.cloned.1.call-start = ((), (), s32[]{:S(2)}) async-start(), calls=%async_computation.10 | async-start | bytes 16056320 | tf_op jit(solution)/shard_map/all_gather | solution.py:191
  1224.1 11.1 copy-start.2
  1240.1 22.3 %copy-start.6 = (bf16[8,72,64]{2,1,0:T(8,128)(2,1)S(1)}, bf16[8,72,64]{2,1,0:T(8,128)(2,1)}, u32[]{:S(2)}) copy-start(bf16[8,72,64]{2,1,0:T(8,128)(2,1)} %copy.269) | copy-start | bytes 221188
  1289.3 18.2 copy-start.35
  1289.3 18.3 copy-start.43
  1289.3 37.2 %copy-start.40 = (f32[2,2,16]{2,1,0:T(2,128)S(1)}, f32[2,2,16]{2,1,0:T(2,128)}, u32[]{:S(2)}) copy-start(f32[2,2,16]{2,1,0:T(2,128)} %param.33) | copy-start | bytes 772
  1289.3 37.2 %copy-start.28 = (f32[16,51]{1,0:T(8,128)S(1)}, f32[16,51]{1,0:T(8,128)}, u32[]{:S(2)}) copy-start(f32[16,51]{1,0:T(8,128)} %param.34) | copy-start | bytes 9796
  1289.3 37.2 %copy-start.29 = (f32[16,51]{1,0:T(8,128)S(1)}, f32[16,51]{1,0:T(8,128)}, u32[]{:S(2)}) copy-start(f32[16,51]{1,0:T(8,128)} %param.35) | copy-start | bytes 9796
  1289.3 67.7 %copy-start.15 = (f32[16,918]{1,0:T(8,128)S(1)}, f32[16,918]{1,0:T(8,128)}, u32[]{:S(2)}) copy-start(f32[16,918]{1,0:T(8,128)} %param.36) | copy-start | bytes 176260
  1289.3 67.7 %copy-start.16 = (f32[16,918]{1,0:T(8,128)S(1)}, f32[16,918]{1,0:T(8,128)}, u32[]{:S(2)}) copy-start(f32[16,918]{1,0:T(8,128)} %param.37) | copy-start | bytes 176260
  1307.4 139.5 %reduce-scatter.3.cloned.1.call-start = ((), (), s32[]{:S(2)}) async-start(), calls=%async_computation.12 | async-start | bytes 4997120 | tf_op jit(solution)/shard_map/reduce_scatter | solution.py:196
  1307.5 91.4 %copy-start.37 = (f32[51]{0:T(128)}, f32[51]{0:T(128)S(1)}, u32[]{:S(2)}) copy-start(f32[51]{0:T(128)S(1)} %slice.217) | copy-start | bytes 616
  1307.6 49.4 %copy-start.17 = (f32[918]{0:T(1024)}, f32[918]{0:T(1024)S(1)}, u32[]{:S(2)}) copy-start(f32[918]{0:T(1024)S(1)} %slice.220) | copy-start | bytes 11020
  1326.5 30.5 %copy-start.30 = (f32[16]{0:T(128)}, f32[16]{0:T(128)S(1)}, u32[]{:S(2)}) copy-start(f32[16]{0:T(128)S(1)} %get-tuple-element.91) | copy-start | bytes 196
  1326.5 72.4 %copy-start.32 = (f32[16]{0:T(128)}, f32[16]{0:T(128)S(1)}, u32[]{:S(2)}) copy-start(f32[16]{0:T(128)S(1)} %get-tuple-element.90) | copy-start | bytes 196
  1400.4 46.5 %copy-start.34 = (f32[969]{0:T(1024)S(1)}, f32[969]{0:T(1024)}, u32[]{:S(2)}) copy-start(f32[969]{0:T(1024)} %param.39) | copy-start | bytes 11632
  1403.5 90.8 %all-gather.10.cloned.1.call-start = ((), (), s32[]{:S(2)}) async-start(), calls=%async_computation.13 | async-start | bytes 4997120 | tf_op jit(solution)/shard_map/all_gather | solution.py:233
  1458.2 39.6 %copy-start.9 = (bf16[512,51]{0,1:T(8,128)(2,1)}, bf16[512,51]{0,1:T(8,128)(2,1)S(1)}, u32[]{:S(2)}) copy-start(bf16[512,51]{0,1:T(8,128)(2,1)S(1)} %get-tuple-element.83) | copy-start | bytes 156676
  1460.7 157.9 %reduce-scatter.5.cloned.1.call-start = ((), (), s32[]{:S(2)}) async-start(), calls=%async_computation.14 | async-start | bytes 16056320 | tf_op jit(solution)/shard_map/reduce_scatter | solution.py:255
  1508.1 11.9 all-to-all-start.7
  1520.0 11.9 all-to-all-start.5
  1531.9 17.4 all-to-all-start.6
  1545.1 10.8 copy-start.10
  1545.1 70.9 %copy-start.33 = (f32[16]{0:T(128)S(1)}, f32[16]{0:T(128)}, u32[]{:S(2)}) copy-start(f32[16]{0:T(128)} %copy-done.32) | copy-start | bytes 196
  1545.1 70.9 %copy-start.38 = (f32[51]{0:T(128)S(1)}, f32[51]{0:T(128)}, u32[]{:S(2)}) copy-start(f32[51]{0:T(128)} %copy-done.37) | copy-start | bytes 616
  1545.1 71.6 %copy-start.18 = (f32[918]{0:T(1024)S(1)}, f32[918]{0:T(1024)}, u32[]{:S(2)}) copy-start(f32[918]{0:T(1024)} %copy-done.17) | copy-start | bytes 11020
  1545.1 71.6 %copy-start.31 = (f32[16]{0:T(128)S(1)}, f32[16]{0:T(128)}, u32[]{:S(2)}) copy-start(f32[16]{0:T(128)} %copy-done.30) | copy-start | bytes 196
  1545.1 72.5 %copy-start.14 = (f32[2,3136]{1,0:T(2,128)S(1)}, f32[2,3136]{1,0:T(2,128)}, u32[]{:S(2)}) copy-start(f32[2,3136]{1,0:T(2,128)} %param.32) | copy-start | bytes 75268
  1545.1 72.5 %copy-start.27 = (f32[2,16]{1,0:T(2,128)S(1)}, f32[2,16]{1,0:T(2,128)}, u32[]{:S(2)}) copy-start(f32[2,16]{1,0:T(2,128)} %copy-done.26) | copy-start | bytes 388
  1549.3 68.1 %all-to-all-start.4 = ((bf16[8,2,3136,16]{2,3,1,0:T(8,128)(2,1)}), bf16[8,2,3136,16]{2,3,1,0:T(8,128)(2,1)S(1)}, u32[]{:S(2)}, u32[]{:S(2)}) async-start(bf16[8,2,3136,16]{2,3,1,0:T(8,128)(2,1)} %copy.299), calls=%async_computation.6 | async-start | bytes 3276800 | tf_op jit(solution)/shard_map/all_to_all | solution.py:14
  1623.8 39.5 %copy-start = (bf16[512,7,7,64]{0,3,2,1:T(8,128)(2,1)}, bf16[512,7,7,64]{0,3,2,1:T(8,128)(2,1)S(1)}, u32[]{:S(2)}) copy-start(bf16[512,7,7,64]{0,3,2,1:T(8,128)(2,1)S(1)} %fusion.22) | copy-start | bytes 9633796
  1690.7 20.0 %slice-start.4 = ((s8[13107200]{0:T(1024)(128)(4,1)}), s8[4194304]{0:T(1024)(128)(4,1)S(1)}, s32[]{:S(2)}) async-start(s8[13107200]{0:T(1024)(128)(4,1)} %bitcast.549), calls=%async_computation.19 | async-start | bytes 8388608
  1690.7 20.0 %slice-start.5 = ((s8[13107200]{0:T(1024)(128)(4,1)}), s8[4194304]{0:T(1024)(128)(4,1)S(1)}, s32[]{:S(2)}) async-start(s8[13107200]{0:T(1024)(128)(4,1)} %bitcast.549), calls=%async_computation.20 | async-start | bytes 8388608
  1700.8 10.0 slice-start.6
  1700.8 10.0 slice-start.7
  1717.0 17.5 slice-start.8
  1723.3 11.2 slice-start.9
  1845.2 32.1 %slice-start.2 = ((s8[5308416]{0:T(1024)(128)(4,1)}), s8[4194304]{0:T(1024)(128)(4,1)S(1)}, s32[]{:S(2)}) async-start(s8[5308416]{0:T(1024)(128)(4,1)} %bitcast.541), calls=%async_computation.17 | async-start | bytes 8388608
  1861.1 16.2 copy-start.1
  1861.1 16.2 slice-start.3
  1885.2 9.6 copy-start.23
  1885.2 9.6 copy-start.24
  1885.2 9.6 copy-start.25
  1889.3 12.1 all-to-all-start.1
  1901.4 10.2 all-to-all-start.2
  1911.6 11.7 all-to-all-start.3
  (19 other events, 104.5 us)
Sparse Core Ops, SparseCore 0:
  111.2 585.5 all-gather.7
  1307.6 82.8 all-gather.5
  1403.6 43.2 reduce-scatter.2
  1460.8 33.3 all-gather.9
  1506.9 101.6 reduce-scatter.4
where the time goes:
time: 1960 us; the launch traced here: 1940 us
  blocking collectives  994 us (51%)
  matrix products  464 us (24%)
  local copies, waits for them, and re-layouts  284 us (14%)
  waiting for transfers between devices  98.7 us (5%)
  other arithmetic  44.9 us (2%)
  starting transfers between devices  41.2 us (2%)
    all_gather x1, blocking collectives, on_device(): lax.all_gather(conv_third.astype(jnp.bfloat16), 'dp', axis=0, tiled=True)  784 us
    dot_general x17, matrix products, shifted_conv(): jnp.einsum('npqc,cd->npqd', window, kernel[shift_row, shift_col], preferr...  188 us
    dot_general x17, matrix products, kernel_grad(): jnp.einsum('npqc,npqd->cd', window, grad_out, preferred_element_type=jnp....  115 us
    gather x2, local copies, waits for them, and re-layouts, on_device(): frames[send_rows]  92.2 us
    pad x5, matrix products, input_grad(): jnp.pad(shifted_piece, ((0, 0), (shift_row, in_side - out_side - shift_ro...  77.1 us
    psum x1, blocking collectives, on_device(): lax.psum((jnp.sum(loss_coeff * cross), jnp.sum(is_valid), jnp.sum(logit_g...  55.3 us
    another operation x1, local copies, waits for them, and re-layouts, to_depth(): values.reshape(batch_rows, height // factor, factor, breadth // factor, f...  47.6 us
    dot_general x8, matrix products, input_grad(): jnp.einsum('npqd,cd->npqc', grad_out, kernel[shift_row, shift_col], prefe...  47.2 us
  transfers between devices with their start and end apart: 13, of which 8 were waited for; matrix products, arithmetic and copies ran while one was open for 20% of the time, Pallas kernels for 0%

commit v1 on v0

v1 whole, which is shorter than its diff:
```python
import functools

import jax
import jax.numpy as jnp
from jax import lax
from jax.experimental import pallas as pl
from jax.experimental.pallas import tpu as pltpu
from jax.sharding import PartitionSpec as P

F32 = jnp.float32
BF16 = jnp.bfloat16
VMEM_LIMIT = 60 * 1024 * 1024


def sigmoid(v):
    return 0.5 * jnp.tanh(0.5 * v) + 0.5


def silu_and_slope(v):
    s = sigmoid(v)
    a = v * s
    return a, s + a * (1.0 - s)


def dot(a, b):
    return lax.dot_general(a, b, (((1,), (0,)), ((), ())), preferred_element_type=F32)


def dot_nt(a, b):
    return lax.dot_general(a, b, (((1,), (1,)), ((), ())), preferred_element_type=F32)


def dot_tn(a, b):
    return lax.dot_general(a, b, (((0,), (0,)), ((), ())), preferred_element_type=F32)


def columns_of_one():
    return [7 * (g // 8) + g % 8 if g % 8 < 7 and 7 * (g // 8) + g % 8 < 20 else -9 for g in range(24)]


def band_one(kern):
    w = kern.reshape(2, 2, 4, 16, 32).transpose(0, 2, 1, 3, 4).reshape(8, 2, 1, 16, 1, 32)
    group = lax.broadcasted_iota(jnp.int32, (8, 16, 8, 32), 0)
    col = lax.broadcasted_iota(jnp.int32, (8, 16, 8, 32), 2)
    zero = jnp.zeros((), kern.dtype)
    band = jnp.where((group == col) & (col < 7), w[:, 0], zero) + jnp.where((group == col + 1) & (col < 7), w[:, 1], zero)
    return band.reshape(8 * 128, 256)


def band_two(kern):
    w = kern.reshape(2, 2, 2, 2, 32, 64).transpose(0, 2, 1, 3, 4, 5).reshape(4, 4, 1, 32, 1, 64)
    grp = lax.broadcasted_iota(jnp.int32, (24, 32, 10, 64), 0)
    inside = grp % 8
    source = jnp.where(inside < 7, 7 * (grp // 8) + inside, -9)
    col = lax.broadcasted_iota(jnp.int32, (24, 32, 10, 64), 2)
    zero = jnp.zeros((), kern.dtype)
    band = sum(jnp.where((source == 2 * col + v) & (col < 9), w[:, v], zero) for v in range(4))
    return band.reshape(4, 768, 640)


def band_three(kern):
    w = kern.reshape(3, 3, 1, 64, 1, 64)
    source = lax.broadcasted_iota(jnp.int32, (10, 64, 8, 64), 0)
    col = lax.broadcasted_iota(jnp.int32, (10, 64, 8, 64), 2)
    zero = jnp.zeros((), kern.dtype)
    band = sum(jnp.where((source == col + v) & (col < 7), w[:, v], zero) for v in range(3))
    return band.reshape(3, 640, 512)


def unband_one(g):
    g = g.reshape(8, 8, 16, 8, 32)
    taps = jnp.stack([sum(g[:, c + v, :, c] for c in range(7)) for v in range(2)], axis=1)
    return taps.reshape(2, 4, 2, 16, 32).transpose(0, 2, 1, 3, 4).reshape(256, 32)


def unband_two(ga, gb, gc):
    blocks = ((ga.reshape(4, 12, 32, 4, 64), 0, 0, 4), (gb.reshape(4, 12, 32, 4, 64), 8, 4, 4), (gc.reshape(4, 8, 32, 2, 64), 16, 8, 1))
    cols = columns_of_one()
    taps = []
    for v in range(4):
        total = 0.0
        for g, first, c0, count in blocks:
            for c in range(count):
                total = total + g[:, cols.index(2 * (c0 + c) + v) - first, :, c]
        taps.append(total)
    taps = jnp.stack(taps, axis=1)
    return taps.reshape(2, 2, 2, 2, 32, 64).transpose(0, 2, 1, 3, 4, 5).reshape(512, 64)


def unband_three(g):
    g = g.reshape(3, 6, 64, 4, 64)
    taps = jnp.stack([sum(g[:, c + v, :, c] for c in range(4)) for v in range(3)], axis=1)
    return taps.reshape(576, 64)


def shifted_blocks(x):
    rows = x.shape[0]
    return (
        x[:, 0:128],
        x[:, 112:240],
        jnp.concatenate([x[:, 224:336], jnp.zeros((rows, 16), x.dtype)], axis=1),
    )


def forward_kernel(x_ref, xn_ref, b1_ref, b2_ref, b3_ref, a1_ref, s1_ref, a2_ref, s2_ref, f_ref, s3_ref, xs, a1s, a2s):
    i = pl.program_id(0)
    rows = x_ref.shape[2]
    for big in range(5):
        for r in range(4):
            src = x_ref[big, r] if big < 4 else xn_ref[0, r]
            for j, blk in enumerate(shifted_blocks(src)):
                xs[big, j, :, 128 * r : 128 * r + 128] = blk
    for pp in range(4):
        for j in range(3):
            lhs = jnp.concatenate([xs[pp, j], xs[pp + 1, j]], axis=1)
            act, slope = silu_and_slope(dot(lhs, b1_ref[...]))
            act = act.astype(BF16)
            a1_ref[pp // 2, pp % 2, :, 256 * j : 256 * j + 256] = act
            a1s[2 * i + pp // 2, pp % 2, :, 256 * j : 256 * j + 256] = act
            s1_ref[pp // 2, pp % 2, :, 256 * j : 256 * j + 256] = slope.astype(BF16)

    def second(p):
        for lo, hi, n0, n1 in ((0, 384, 0, 256), (256, 640, 256, 512), (512, 768, 512, 640)):
            lhs = jnp.concatenate([a1s[p + u // 2, u % 2, :, lo:hi] for u in range(4)], axis=1)
            rhs = jnp.concatenate([b2_ref[u, lo:hi, n0:n1] for u in range(4)], axis=0)
            act, slope = silu_and_slope(dot(lhs, rhs))
            act = act.astype(BF16)
            a2_ref[p, :, n0:n1] = act
            a2s[p, :, n0:n1] = act
            s2_ref[p, :, n0:n1] = slope.astype(BF16)

    def third(p, odd):
        acts, slopes = [], []
        for lo, hi, n0, n1 in ((0, 384, 0, 256), (256, 640, 256, 512)):
            lhs = jnp.concatenate([a2s[p + u, :, lo:hi] for u in range(3)], axis=1)
            rhs = jnp.concatenate([b3_ref[u, lo:hi, n0:n1] for u in range(3)], axis=0)
            act, slope = silu_and_slope(dot(lhs, rhs))
            acts.append(act)
            slopes.append(slope)
        lane = lax.broadcasted_iota(jnp.int32, (rows, 512), 1)
        base = (p // 2) * 896
        for out, parts in ((f_ref, acts), (s3_ref, slopes)):
            whole = jnp.where(lane < 448, jnp.concatenate(parts, axis=1), 0.0)
            if not odd:
                out[:, pl.ds(pl.multiple_of(base, 128), 512)] = whole.astype(BF16)
            else:
                whole = pltpu.roll(whole, 64, 1)
                at = pl.ds(pl.multiple_of(base + 384, 128), 128)
                out[:, at] = (out[:, at].astype(F32) + whole[:, :128]).astype(BF16)
                out[:, pl.ds(pl.multiple_of(base + 512, 128), 384)] = whole[:, 128:].astype(BF16)

    @pl.when(i >= 1)
    def _():
        second(2 * i - 1)

    second(2 * i)

    @pl.when(i >= 2)
    def _():
        third(2 * i - 3, True)

    @pl.when(i >= 1)
    def _():
        third(2 * i - 2, False)

    @pl.when(i == 4)
    def _():
        lane = lax.broadcasted_iota(jnp.int32, (rows, 128), 1)
        last = f_ref[:, 3072:3200].astype(F32)
        f_ref[:, 3072:3200] = jnp.where(lane == 64, 1.0, last).astype(BF16)


def full(shape):
    return pl.BlockSpec(shape, lambda *_: (0,) * len(shape))


def once(shape):
    return pl.BlockSpec(shape, lambda *_: (0,) * len(shape), pipeline_mode=pl.Buffered(1))


def torso_forward(x, band1, band2, band3):
    rows = x.shape[2]
    shapes = [(10, 2, rows, 768)] * 2 + [(9, rows, 640)] * 2 + [(rows, 3200)] * 2
    return pl.pallas_call(
        forward_kernel,
        grid=(5,),
        in_specs=[
            pl.BlockSpec((4, 4, rows, 336), lambda i: (i, 0, 0, 0)),
            pl.BlockSpec((1, 4, rows, 336), lambda i: (4 * i + 4, 0, 0, 0)),
            once(band1.shape),
            once(band2.shape),
            once(band3.shape),
        ],
        out_specs=[pl.BlockSpec((2, 2, rows, 768), lambda i: (i, 0, 0, 0))] * 2
        + [once((9, rows, 640))] * 2
        + [once((rows, 3200))] * 2,
        out_shape=[jax.ShapeDtypeStruct(s, BF16) for s in shapes],
        scratch_shapes=[
            pltpu.VMEM((5, 3, rows, 512), BF16),
            pltpu.VMEM((10, 2, rows, 768), BF16),
            pltpu.VMEM((9, rows, 640), BF16),
        ],
        compiler_params=pltpu.CompilerParams(vmem_limit_bytes=VMEM_LIMIT),
        name="torso_forward",
    )(x, x, band1, band2, band3)


def backward_kernel(
    x_ref, xn_ref, a1_ref, s1_ref, a2_ref, s2_ref, s3_ref, fg_ref, b2_ref, b3_ref, d1_ref, d2a_ref, d2b_ref, d2c_ref, d3_ref, xs, g3, g2
):
    i = pl.program_id(0)
    rows = x_ref.shape[2]

    @pl.when(i == 0)
    def _():
        for at in (0, 1, 9, 10):
            g3[at] = jnp.zeros((rows, 512), BF16)
        for at in (0, 10):
            g2[at] = jnp.zeros((rows, 640), BF16)
        lane = lax.broadcasted_iota(jnp.int32, (rows, 512), 1)
        for p in range(7):
            base = (p // 2) * 896 + (384 if p % 2 else 0)
            both = fg_ref[:, base : base + 512].astype(F32) * s3_ref[:, base : base + 512].astype(F32)
            if p % 2:
                both = pltpu.roll(both, 448, 1)
            g3[p + 2] = jnp.where(lane < 448, both, 0.0).astype(BF16)
        for u in range(3):
            total = 0.0
            for m in range(2):
                lhs = a2_ref[u : u + 7, :, 256 * m : 256 * m + 384].reshape(7 * rows, 384)
                rhs = g3[2:9, :, 256 * m : 256 * m + 256].reshape(7 * rows, 256)
                total = total + dot_tn(lhs, rhs)
            d3_ref[u] = total
        d1_ref[...] = jnp.zeros_like(d1_ref)
        d2a_ref[...] = jnp.zeros_like(d2a_ref)
        d2b_ref[...] = jnp.zeros_like(d2b_ref)
        d2c_ref[...] = jnp.zeros_like(d2c_ref)
        for lo, hi, n0, n1 in ((0, 256, 0, 256), (256, 512, 128, 512), (512, 640, 384, 512)):
            rhs = jnp.concatenate([b3_ref[u, lo:hi, n0:n1] for u in range(3)], axis=1)

            def one(p, _):
                lhs = jnp.concatenate([g3[p + 2 - u, :, n0:n1] for u in range(3)], axis=1)
                back = dot_nt(lhs, rhs) * s2_ref[p, :, lo:hi].astype(F32)
                g2[p + 1, :, lo:hi] = back.astype(BF16)
                return 0

            lax.fori_loop(0, 9, one, 0)

    for r in range(2):
        for t in range(2):
            for ref, lo, hi, n0, n1 in ((d2a_ref, 0, 384, 0, 256), (d2b_ref, 256, 640, 256, 512), (d2c_ref, 512, 768, 512, 640)):
                lhs = a1_ref[:, r, :, lo:hi].reshape(2 * rows, hi - lo)
                rhs = g2[pl.ds(2 * i + 1 - t, 2), :, n0:n1].reshape(2 * rows, n1 - n0)
                ref[2 * t + r] += dot_tn(lhs, rhs)

    for big in range(5):
        for r in range(4):
            src = x_ref[big, r] if big < 4 else xn_ref[0, r]
            for j, blk in enumerate(shifted_blocks(src)):
                xs[big, j, :, 128 * r : 128 * r + 128] = blk

    for j, (n0, n1) in enumerate(((0, 256), (128, 512), (384, 640))):
        grads = []
        for pp in range(4):
            r = pp % 2
            at = 2 * i + pp // 2 + 1
            lhs = jnp.concatenate([g2[at, :, n0:n1], g2[at - 1, :, n0:n1]], axis=1)
            rhs = jnp.concatenate([b2_ref[r, 256 * j : 256 * j + 256, n0:n1], b2_ref[2 + r, 256 * j : 256 * j + 256, n0:n1]], axis=1)
            back = dot_nt(lhs, rhs) * s1_ref[pp // 2, r, :, 256 * j : 256 * j + 256].astype(F32)
            grads.append(back.astype(BF16))
        grad = jnp.concatenate(grads, axis=0)
        for t in range(2):
            lhs = xs[t : t + 4, j].reshape(4 * rows, 512)
            d1_ref[512 * t : 512 * t + 512, :] += dot_tn(lhs, grad)


def torso_backward(x, a1, s1, a2, s2, s3, fg, band2, band3):
    rows = x.shape[2]
    outs = [(1024, 256), (4, 384, 256), (4, 384, 256), (4, 256, 128), (3, 384, 256)]
    return pl.pallas_call(
        backward_kernel,
        grid=(5,),
        in_specs=[
            pl.BlockSpec((4, 4, rows, 336), lambda i: (i, 0, 0, 0)),
            pl.BlockSpec((1, 4, rows, 336), lambda i: (4 * i + 4, 0, 0, 0)),
            pl.BlockSpec((2, 2, rows, 768), lambda i: (i, 0, 0, 0)),
            pl.BlockSpec((2, 2, rows, 768), lambda i: (i, 0, 0, 0)),
            once(a2.shape),
            once(s2.shape),
            once(s3.shape),
            once(fg.shape),
            once(band2.shape),
            once(band3.shape),
        ],
        out_specs=[once(s) for s in outs],
        out_shape=[jax.ShapeDtypeStruct(s, F32) for s in outs],
        scratch_shapes=[
            pltpu.VMEM((5, 3, rows, 512), BF16),
            pltpu.VMEM((11, rows, 512), BF16),
            pltpu.VMEM((11, rows, 640), BF16),
        ],
        compiler_params=pltpu.CompilerParams(vmem_limit_bytes=VMEM_LIMIT),
        name="torso_backward",
    )(x, x, a1, s1, a2, s2, s3, fg, band2, band3)


def high_low(v):
    high = v.astype(BF16)
    return high, (v - high.astype(F32)).astype(BF16)


def heads_kernel(
    atoms, acts, f_ref, w_ref, bias_ref, tgt_ref, slot_ref, sel_ref, selt_ref, fold_ref, foldt_ref, dw_ref, fg_ref, prio_ref, stat_ref, bg_ref
):
    rows = f_ref.shape[0]
    slots = tgt_ref.shape[0]
    feats = f_ref[...]
    pre = [dot_nt(feats, w_ref[:, 3200 * k : 3200 * k + 3200]) for k in range(2)]
    hidden, slope = [], []
    for k in range(2):
        a, s = silu_and_slope(pre[k])
        hidden.append(a.astype(BF16))
        slope.append(s)
    out_w = w_ref[:, 6400:7424]
    wide = out_w.shape[1]
    lane = lax.broadcasted_iota(jnp.int32, (1, wide), 1)
    zero = jnp.zeros((), BF16)
    w_val = jnp.where(lane[:, :128] < atoms, out_w[:, :128].astype(F32), 0.0).astype(BF16)
    w_adv = jnp.where(lane >= atoms, out_w.astype(F32), 0.0).astype(BF16)
    logits = dot(hidden[1], w_adv) + bias_ref[...]
    logits = jnp.concatenate([logits[:, :128] + dot(hidden[0], w_val), logits[:, 128:]], axis=1)
    high, low = high_low(logits)
    per_slot = dot(sel_ref[...], high) + dot(sel_ref[...], low)
    action = slot_ref[:, 2:3]
    which = jnp.where(lane < atoms, -1, jnp.where(lane < atoms * (acts + 1), (lane - atoms) // atoms, -2)).astype(F32)
    coeff = jnp.where(which == -1.0, 1.0, 0.0) + jnp.where(which == action, 1.0, 0.0) - jnp.where(which >= 0.0, 1.0 / acts, 0.0)
    high, low = high_low(per_slot * coeff)
    q = dot(high, fold_ref[...]) + dot(low, fold_ref[...])
    lane_q = lax.broadcasted_iota(jnp.int32, (slots, 128), 1)
    used = lane_q < atoms
    top = jnp.max(jnp.where(used, q, -jnp.inf), axis=1, keepdims=True)
    shifted = jnp.where(used, jnp.exp(jnp.where(used, q - top, 0.0)), 0.0)
    total = jnp.sum(shifted, axis=1, keepdims=True)
    tgt = tgt_ref[...]
    cross = -jnp.sum(jnp.where(used, tgt * (q - top - jnp.log(total)), 0.0), axis=1, keepdims=True)
    coef = slot_ref[:, 0:1]
    valid = slot_ref[:, 1:2]
    prio_ref[...] = valid * cross
    q_grad = coef * (shifted * (jnp.sum(tgt, axis=1, keepdims=True) / total) - tgt)
    high, low = high_low(q_grad)
    lgrad = ((dot(high, foldt_ref[...]) + dot(low, foldt_ref[...])) * coeff).astype(BF16)
    bg_ref[...] = jnp.sum(lgrad.astype(F32), axis=0, keepdims=True)
    stat_ref[0:1, :] = jnp.broadcast_to(jnp.sum(coef * cross, axis=0, keepdims=True), (1, 128))
    stat_ref[1:2, :] = jnp.broadcast_to(jnp.sum(valid, axis=0, keepdims=True), (1, 128))
    grad = dot(selt_ref[...], lgrad).astype(BF16)
    d_adv = dot_tn(hidden[1], grad)
    d_val = dot_tn(hidden[0], grad[:, :128])
    dw_ref[:, 6528:7424] = d_adv[:, 128:].astype(BF16)
    dw_ref[:, 6400:6528] = jnp.where(lane[:, :128] < atoms, d_val, d_adv[:, :128]).astype(BF16)
    pre_grad = [
        (dot_nt(grad[:, :128], w_val) * slope[0]).astype(BF16),
        (dot_nt(grad, w_adv) * slope[1]).astype(BF16),
    ]
    for k in range(2):
        for lo, hi in ((0, 1024), (1024, 2048), (2048, 3200)):
            dw_ref[:, 3200 * k + lo : 3200 * k + hi] = dot_tn(pre_grad[k], f_ref[:, lo:hi]).astype(BF16)
    for lo, hi in ((0, 1024), (1024, 2048), (2048, 3200)):
        back = dot(pre_grad[0], w_ref[:, lo:hi]) + dot(pre_grad[1], w_ref[:, 3200 + lo : 3200 + hi])
        fg_ref[:, lo:hi] = back.astype(BF16)


def heads(atoms, acts, feats, weights, bias, tgt, slot, rows_of_slot):
    rows, slots, wide = feats.shape[0], tgt.shape[0], bias.shape[1]
    sel = (rows_of_slot[:, None] == jnp.arange(rows, dtype=jnp.int32)[None, :]).astype(BF16)
    selt = (jnp.arange(rows, dtype=jnp.int32)[:, None] == rows_of_slot[None, :]).astype(BF16)
    n = jnp.arange(wide, dtype=jnp.int32)
    z = jnp.where(n < atoms * (acts + 1), n % atoms, -1)
    fold = (z[:, None] == jnp.arange(128, dtype=jnp.int32)[None, :]).astype(BF16)
    foldt = (jnp.arange(128, dtype=jnp.int32)[:, None] == z[None, :]).astype(BF16)
    return pl.pallas_call(
        functools.partial(heads_kernel, atoms, acts),
        out_shape=[
            jax.ShapeDtypeStruct(weights.shape, BF16),
            jax.ShapeDtypeStruct(feats.shape, BF16),
            jax.ShapeDtypeStruct((slots, 1), F32),
            jax.ShapeDtypeStruct((8, 128), F32),
            jax.ShapeDtypeStruct((1, wide), F32),
        ],
        compiler_params=pltpu.CompilerParams(vmem_limit_bytes=VMEM_LIMIT),
        name="heads",
    )(feats, weights, bias, tgt, slot, sel, selt, fold, foldt)


def on_device(
    frames,
    send_rows,
    recv_counts,
    actions,
    target_dist,
    sample_weight,
    conv_first,
    conv_second,
    conv_third,
    hidden_mean,
    hidden_spread,
    hidden_bias,
    feature_noise,
    hidden_noise,
    value_mean,
    value_spread,
    advantage_mean,
    advantage_spread,
    output_noise,
    output_bias,
):
    dp_count = lax.axis_size("dp")
    slots = send_rows.shape[0]
    capacity = slots // dp_count
    atoms = value_mean.shape[1]
    acts = advantage_mean.shape[1] // atoms
    rows = frames.shape[0]
    feat, own = hidden_mean.shape[1:]
    outs = atoms * (acts + 1)

    flat = jnp.concatenate([w.astype(BF16).reshape(-1) for w in (conv_first, conv_second, conv_third)])
    flat = lax.all_gather(flat, "dp", axis=0, tiled=False)
    sizes = [w.size for w in (conv_first, conv_second, conv_third)]
    kern1 = flat[:, : sizes[0]].reshape(-1, conv_first.shape[1])
    kern2 = flat[:, sizes[0] : sizes[0] + sizes[1]].reshape(-1, conv_second.shape[1])
    kern3 = flat[:, sizes[0] + sizes[1] :].reshape(-1, conv_third.shape[1])
    band1, band2, band3 = band_one(kern1), band_two(kern2), band_three(kern3)

    mean_t = hidden_mean.transpose(0, 2, 1)
    spread_t = hidden_spread.transpose(0, 2, 1)
    wide_one = mean_t + spread_t * feature_noise[:, None, :] * hidden_noise[0][:, :, None]
    wide_one = jnp.concatenate([wide_one, hidden_bias[:, :, None], jnp.zeros((2, own, 63), F32)], axis=2)
    wide_val = value_mean + value_spread * hidden_noise[1, 0][:, None] * output_noise[None, :atoms]
    wide_adv = advantage_mean + advantage_spread * hidden_noise[1, 1][:, None] * output_noise[None, atoms:]
    shard = jnp.concatenate(
        [wide_one[0], wide_one[1], wide_val, wide_adv, jnp.zeros((own, 1024 - outs), F32)], axis=1
    ).astype(BF16)
    weights = lax.all_gather(shard, ("mp", "dp"), axis=0, tiled=True)

    is_valid = jnp.arange(capacity, dtype=jnp.int32)[None, :] < recv_counts[:, None]
    is_valid = is_valid.astype(F32).reshape(slots)
    per_slot = jnp.concatenate(
        [target_dist, (is_valid * sample_weight)[:, None], is_valid[:, None], actions.astype(F32)[:, None]], axis=1
    )
    per_slot = lax.all_to_all(per_slot, "dp", split_axis=0, concat_axis=0, tiled=True)
    tgt = jnp.pad(per_slot[:, :atoms], ((0, 0), (0, 128 - atoms)))
    slot = per_slot[:, atoms:]

    x = frames.transpose(1, 0, 2).reshape(21, 4, rows, 336)
    a1, s1, a2, s2, feats, s3 = torso_forward(x, band1, band2, band3)
    bias = jnp.pad(output_bias, (0, 1024 - outs))[None, :]
    dweights, feat_grad, prio, stat, bias_grad = heads(atoms, acts, feats, weights, bias, tgt, slot, send_rows)
    dshard = lax.psum_scatter(dweights, ("mp", "dp"), scatter_dimension=0, tiled=True).astype(F32)
    loss_sum, count, bias_sum = lax.psum((stat[0, 0], stat[1, 0], bias_grad[0, :outs]), ("dp", "mp"))
    inverse = 1.0 / count

    d1, d2a, d2b, d2c, d3 = torso_backward(x, a1, s1, a2, s2, s3, feat_grad, band2, band3)
    kgrads = (unband_one(d1), unband_two(d2a, d2b, d2c), unband_three(d3))
    kflat = jnp.concatenate([g.reshape(dp_count, -1) for g in kgrads], axis=1)
    kflat = lax.psum(lax.psum_scatter(kflat, "dp", scatter_dimension=0, tiled=True)[0], "mp") * inverse
    conv_grads = (
        kflat[: sizes[0]].reshape(conv_first.shape),
        kflat[sizes[0] : sizes[0] + sizes[1]].reshape(conv_second.shape),
        kflat[sizes[0] + sizes[1] :].reshape(conv_third.shape),
    )

    dshard = dshard * inverse
    mean_grad_t = jnp.stack([dshard[:, :feat], dshard[:, 3200 : 3200 + feat]])
    spread_grad_t = mean_grad_t * feature_noise[:, None, :] * hidden_noise[0][:, :, None]
    value_mean_grad = dshard[:, 6400 : 6400 + atoms]
    adv_mean_grad = dshard[:, 6400 + atoms : 6400 + outs]
    return (
        loss_sum * inverse,
        *conv_grads,
        mean_grad_t.transpose(0, 2, 1),
        spread_grad_t.transpose(0, 2, 1),
        jnp.stack([dshard[:, feat], dshard[:, 3200 + feat]]),
        value_mean_grad,
        value_mean_grad * hidden_noise[1, 0][:, None] * output_noise[None, :atoms],
        adv_mean_grad,
        adv_mean_grad * hidden_noise[1, 1][:, None] * output_noise[None, atoms:],
        bias_sum * inverse,
        prio[:, 0],
    )


def solution(mesh):
    both, heads_dim = P(("dp", "mp")), P(("mp", "dp"), None)
    return jax.shard_map(
        on_device,
        mesh=mesh,
        in_specs=(
            P(("dp", "mp"), None, None),
            both,
            both,
            both,
            P(("dp", "mp"), None),
            both,
            P("dp", None),
            P("dp", None),
            P("dp", None),
            P(None, None, ("mp", "dp")),
            P(None, None, ("mp", "dp")),
            P(None, ("mp", "dp")),
            P(),
            P(None, None, ("mp", "dp")),
            heads_dim,
            heads_dim,
            heads_dim,
            heads_dim,
            P(),
            P(),
        ),
        out_specs=(
            P(),
            P("dp", None),
            P("dp", None),
            P("dp", None),
            P(None, None, ("mp", "dp")),
            P(None, None, ("mp", "dp")),
            P(None, ("mp", "dp")),
            heads_dim,
            heads_dim,
            heads_dim,
            heads_dim,
            P(),
            both,
        ),
        check_vma=False,
    )
```

time: 1960 us -> 590 us (0.30)
  blocking collectives: 994 us -> 81.9 us
  matrix products: 464 us -> 0 us
  local copies, waits for them, and re-layouts: 284 us -> 158 us
  Pallas kernels: 0 us -> 103 us
  waiting for transfers between devices: 98.7 us -> 184 us
  starting transfers between devices: 41.2 us -> 7.4 us
    all_gather x6 -> x1, blocking collectives: 928 us -> 31.8 us  [on_device(): flat = lax.all_gather(flat, 'dp', axis=0, tiled=False)]
    dot_general x51 -> x0, matrix products: 387 us -> none  [the longest x17 188 us: shifted_conv(): jnp.einsum('npqc,cd->npqd', window, kernel[shift_row, shift_col], preferr...]
    broadcast_in_dim x0 -> x20, local copies, waits for them, and re-layouts: none -> 119 us  [the longest x9 91.2 us: band_two(): jnp.where((source == 2 * col + v) & (col < 9), w[:, v], zero)]
    reduce_scatter x2 -> x1, waiting for transfers between devices: 42.1 us -> 156 us  [on_device(): lax.psum_scatter(dweights, ('mp', 'dp'), scatter_dimension=0, tiled=True)]
    pallas_call x0 -> x3, Pallas kernels: none -> 103 us  [the longest x1 49.6 us: torso_backward(): pl.pallas_call(backward_kernel, grid=(5,), in_specs=[pl.BlockSpec((4, 4,...]
    gather x2 -> x0, local copies, waits for them, and re-layouts: 92.2 us -> none  [on_device(): frames[send_rows]]
    pad x5 -> x0, matrix products: 77.1 us -> none  [input_grad(): jnp.pad(shifted_piece, ((0, 0), (shift_row, in_side - out_side - shift_ro...]
    reshape x5 -> x8, local copies, waits for them, and re-layouts: 63.6 us -> 12.7 us  [the longest x1 3.75 us: unband_one(): g = g.reshape(8, 8, 16, 8, 32)]
  transfers between devices with their start and end apart: 13 -> 4, of which waited for: 8 -> 2; matrix products, arithmetic and copies ran while one was open for 20% -> 26% of each run, Pallas kernels for 0% -> 6%
where the time goes in v1:
time: 590 us; the launch traced here: 585 us
  waiting for transfers between devices  184 us (31%)
  local copies, waits for them, and re-layouts  158 us (27%)
  Pallas kernels  103 us (17%)
  blocking collectives  81.9 us (14%)
  other arithmetic  33.7 us (6%)
  between operations  17.4 us (3%)
  starting transfers between devices  7.4 us (1%)
    reduce_scatter x1, waiting for transfers between devices, on_device(): lax.psum_scatter(dweights, ('mp', 'dp'), scatter_dimension=0, tiled=True)  156 us
    broadcast_in_dim x9, local copies, waits for them, and re-layouts, band_two(): jnp.where((source == 2 * col + v) & (col < 9), w[:, v], zero)  91.2 us
    pallas_call x1, Pallas kernels, torso_backward(): pl.pallas_call(backward_kernel, grid=(5,), in_specs=[pl.BlockSpec((4, 4,...  49.6 us
    psum x1, blocking collectives, on_device(): lax.psum((stat[0, 0], stat[1, 0], bias_grad[0, :outs]), ('dp', 'mp'))  39.6 us
    pallas_call x1, Pallas kernels, torso_forward(): pl.pallas_call(forward_kernel, grid=(5,), in_specs=[pl.BlockSpec((4, 4, r...  34.9 us
    all_gather x1, blocking collectives, on_device(): flat = lax.all_gather(flat, 'dp', axis=0, tiled=False)  31.8 us
    unnamed x4, waiting for transfers between devices  27.4 us
    broadcast_in_dim x7, local copies, waits for them, and re-layouts, band_three(): jnp.where((source == col + v) & (col < 7), w[:, v], zero)  26.7 us
  transfers between devices with their start and end apart: 4, of which 2 were waited for; matrix products, arithmetic and copies ran while one was open for 26% of the time, Pallas kernels for 6%

profile of v1, /device:TPU:0, one launch (start us, length us, event | category | flops | bytes accessed | tf_op | source)
XLA Modules:
  0.0 585.1 jit_solution(3236307635616120639)
XLA Ops:
  11.0 1.2 add_bitcast_fusion
  12.4 1.0 add_convert_fusion
  14.8 0.8 reshape.924
  15.6 7.3 %all-to-all-start = ((f32[8,1,3456]{2,1,0:T(1,128)}), f32[8,1,3456]{2,1,0:T(1,128)S(1)}, u32[]{:S(2)}, u32[]{:S(2)}) async-start(f32[8,1,3456]{2,1,0:T(1,128)} %reshape.924), calls=%async_computation | async-start | bytes 221184 | tf_op jit(solution)/shard_map/all_to_all | solution.py:449
  23.4 31.8 %all-gather.1 = bf16[8,1,9728]{2,1,0:T(2,128)(2,1)S(1)} all-gather(bf16[1,1,9728]{2,1,0:T(2,128)(2,1)S(1)} %reshape.916), channel_id=2, replica_groups=mesh['dp'=8,'mp'=4] {'dp'}, dimensions={0}, use_global_device_ids=true | all-gather | bytes 175104 | tf_op jit(solution)/shard_map/all_gather | solution.py:426
  55.5 7.5 %broadcast_in_dim.182 = bf16[4,24,32,10,64]{4,3,2,1,0:T(8,128)(2,1)} broadcast(bf16[4,32,64]{2,1,0:T(8,128)(2,1)S(1)} %get-tuple-element.165), dimensions={0,2,4} | broadcast | bytes 3948544 | tf_op jit(solution)/shard_map/jit(_where)/broadcast_in_dim | solution.py:57
  63.0 15.8 %broadcast_in_dim.183 = bf16[4,768,640]{2,1,0:T(8,128)(2,1)} reshape(bf16[4,24,32,10,64]{4,3,2,1,0:T(8,128)(2,1)} %broadcast_in_dim.182) | data formatting | bytes 7864320 | tf_op jit(solution)/shard_map/jit(_where)/broadcast_in_dim | solution.py:57
  78.8 7.5 %broadcast_in_dim.187 = bf16[4,24,32,10,64]{4,3,2,1,0:T(8,128)(2,1)} broadcast(bf16[4,32,64]{2,1,0:T(8,128)(2,1)S(1)} %get-tuple-element.168), dimensions={0,2,4} | broadcast | bytes 3948544 | tf_op jit(solution)/shard_map/jit(_where)/broadcast_in_dim | solution.py:57
  86.4 15.2 %broadcast_in_dim.188 = bf16[4,768,640]{2,1,0:T(8,128)(2,1)} reshape(bf16[4,24,32,10,64]{4,3,2,1,0:T(8,128)(2,1)} %broadcast_in_dim.187) | data formatting | bytes 7864320 | tf_op jit(solution)/shard_map/jit(_where)/broadcast_in_dim | solution.py:57
  101.6 7.5 %broadcast_in_dim.191 = bf16[4,24,32,10,64]{4,3,2,1,0:T(8,128)(2,1)} broadcast(bf16[4,32,64]{2,1,0:T(8,128)(2,1)S(1)} %get-tuple-element.167), dimensions={0,2,4} | broadcast | bytes 3948544 | tf_op jit(solution)/shard_map/jit(_where)/broadcast_in_dim | solution.py:57
  109.1 15.0 %broadcast_in_dim.192 = bf16[4,768,640]{2,1,0:T(8,128)(2,1)} reshape(bf16[4,24,32,10,64]{4,3,2,1,0:T(8,128)(2,1)} %broadcast_in_dim.191) | data formatting | bytes 7864320 | tf_op jit(solution)/shard_map/jit(_where)/broadcast_in_dim | solution.py:57
  124.1 7.5 %broadcast_in_dim.195 = bf16[4,24,32,10,64]{4,3,2,1,0:T(8,128)(2,1)} broadcast(bf16[4,32,64]{2,1,0:T(8,128)(2,1)S(1)} %get-tuple-element.166), dimensions={0,2,4} | broadcast | bytes 3948544 | tf_op jit(solution)/shard_map/jit(_where)/broadcast_in_dim | solution.py:57
  131.6 15.0 %broadcast_in_dim.196 = bf16[4,768,640]{2,1,0:T(8,128)(2,1)} reshape(bf16[4,24,32,10,64]{4,3,2,1,0:T(8,128)(2,1)} %broadcast_in_dim.195) | data formatting | bytes 7864320 | tf_op jit(solution)/shard_map/jit(_where)/broadcast_in_dim | solution.py:57
  148.6 2.7 broadcast_in_dim.199
  151.3 6.2 %broadcast_in_dim.200 = bf16[3,640,512]{2,1,0:T(8,128)(2,1)} reshape(bf16[3,10,64,8,64]{4,3,2,1,0:T(8,128)(2,1)} %broadcast_in_dim.199) | data formatting | bytes 3932160 | tf_op jit(solution)/shard_map/jit(_where)/broadcast_in_dim | solution.py:66
  157.5 2.7 broadcast_in_dim.204
  160.2 6.2 %broadcast_in_dim.205 = bf16[3,640,512]{2,1,0:T(8,128)(2,1)} reshape(bf16[3,10,64,8,64]{4,3,2,1,0:T(8,128)(2,1)} %broadcast_in_dim.204) | data formatting | bytes 3932160 | tf_op jit(solution)/shard_map/jit(_where)/broadcast_in_dim | solution.py:66
  166.3 2.7 broadcast_in_dim.208
  169.0 6.3 %broadcast_in_dim.209 = bf16[3,640,512]{2,1,0:T(8,128)(2,1)} reshape(bf16[3,10,64,8,64]{4,3,2,1,0:T(8,128)(2,1)} %broadcast_in_dim.208) | data formatting | bytes 3932160 | tf_op jit(solution)/shard_map/jit(_where)/broadcast_in_dim | solution.py:66
  176.9 2.2 add.730.b1_ref
  180.4 3.4 fusion.5
  183.9 5.1 select_add_fusion.3.b3_ref
  189.4 5.4 select_add_fusion.b2_ref
  194.7 34.9 %torso_forward.1 = (bf16[10,2,272,768]{3,2,1,0:T(8,128)(2,1)}, bf16[10,2,272,768]{3,2,1,0:T(8,128)(2,1)}, bf16[9,272,640]{2,1,0:T(8,128)(2,1)}, bf16[9,272,640]{...) custom-call(bf16[21,4,272,336]{3,2,1,0:T(8,128)(2,1)} %bitcast.148, ...), custom_call_target="tpu_custom_call" | custom-call | tf_op jit(solution)/shard_map/torso_forward/pallas_call | solution.py:184
  229.7 0.9 fusion.13.fold_ref
  231.4 0.9 fusion.9.sel_ref
  233.6 0.9 reduce.7
  234.7 0.8 slice.435.slot_ref
  236.3 18.8 %heads.1 = (bf16[512,7424]{1,0:T(8,128)(2,1)}, bf16[272,3200]{1,0:T(8,128)(2,1)}, f32[512,1]{1,0:T(8,128)}, f32[8,128]{1,0:T(8,128)}, f32[1,1024]{1,0:T(1,128)}) custom-call(bf16[272,3200]{1,0:T(8,128)(2,1)} %get-tuple-element.29.f_ref, bf16[512,7424]{1,0:T(8,128)(2,1)} %all-gather.4.cloned.1.call-done.w_ref, f32[1,1024]{1,0:T(1,128)} %bitcast.214, ...), custom_call_target="tpu_custom_call" | custom-call | tf_op jit(solution)/shard_map/heads/pallas_call | solution.py:380
  255.1 49.6 %torso_backward.1 = (f32[1024,256]{1,0:T(8,128)}, f32[4,384,256]{2,1,0:T(8,128)}, f32[4,384,256]{2,1,0:T(8,128)}, f32[4,256,128]{2,1,0:T(8,128)}, f32[3,384,256]{2,1,0:T(8,128)}) custom-call(bf16[21,4,272,336]{3,2,1,0:T(8,128)(2,1)} %bitcast.150, bf16[21,4,272,336]{3,2,1,0:T(8,128)(2,1)} %bitcast.151, bf16[10,2,272,768]{3,2,1,0:T(8,128)(2,1)} %get-tuple-element.31.a1_ref, ...), custom_call_target="tpu_custom_call" | custom-call | tf_op jit(solution)/shard_map/torso_backward/pallas_call | solution.py:280
  304.7 3.7 reshape.889
  308.4 3.9 slice_add_fusion.6
  313.1 3.0 reshape.890
  316.1 1.9 fusion.21
  318.1 2.8 reshape.891
  320.9 1.8 fusion.22
  322.9 1.8 reshape.892
  325.0 1.3 add_bitcast_fusion.6
  327.5 1.0 reshape.894
  328.5 1.3 fusion.23
  332.2 1.3 fusion.25
  333.5 39.6 %all-reduce.3 = (f32[]{:T(128)}, f32[]{:T(128)}, f32[969]{0:T(1024)S(1)}) all-reduce(f32[]{:T(128)} %bitcast.24, f32[]{:T(128)} %bitcast.25, f32[969]{0:T(1024)S(1)} %bitcast.215), channel_id=1, replica_groups=mesh['dp'=8,'mp'=4] {'dp','mp'}, use_global_device_ids=true, to_apply=%region_0.1 | all-reduce | flops 971 | bytes 7768 | tf_op jit(solution)/shard_map/psum | solution.py:458
  375.7 26.7 %all-reduce.6.cloned.1.call-done = f32[8,9728]{1,0:T(8,128)} async-done(((f32[8,9728]{1,0:T(8,128)}), f32[8,9728]{1,0:T(8,128)}) %all-reduce.6.cloned.1.call-update) | async-done | bytes 311312
  402.5 1.7 dynamic-slice_reduce_fusion
  404.2 10.5 %psum.30 = f32[9728]{0:T(1024)S(1)} all-reduce(f32[9728]{0:T(1024)S(1)} %dynamic-slice_reduce_fusion), channel_id=1, replica_groups=mesh['dp'=8,'mp'=4] {'mp'}, use_global_device_ids=true, to_apply=%region_3.4 | all-reduce | flops 9728 | bytes 77824 | tf_op jit(solution)/shard_map/psum | solution.py:464
  416.9 156.3 %reduce-scatter.2.cloned.1.call-done = bf16[16,7424]{1,0:T(8,128)(2,1)} async-done(((bf16[512,7424]{1,0:T(8,128)(2,1)}), bf16[16,7424]{1,0:T(8,128)(2,1)}) %reduce-scatter.2.cloned.1.call-update) | async-done | bytes 237584 | tf_op jit(solution)/shard_map/reduce_scatter | solution.py:457
  573.2 1.0 convert_multiply_fusion
  576.4 0.9 multiply_bitcast_fusion
  (221 shorter events, 24.0 us)
Async XLA Ops:
  7.2 6.1 %copy-start.33 = (f32[16,51]{1,0:T(8,128)S(1)}, f32[16,51]{1,0:T(8,128)}, u32[]{:S(2)}) copy-start(f32[16,51]{1,0:T(8,128)} %param.34) | copy-start | bytes 9796
  7.2 6.1 %copy-start.34 = (f32[16,51]{1,0:T(8,128)S(1)}, f32[16,51]{1,0:T(8,128)}, u32[]{:S(2)}) copy-start(f32[16,51]{1,0:T(8,128)} %param.35) | copy-start | bytes 9796
  7.2 7.0 %copy-start.27 = (f32[512,51]{0,1:T(8,128)S(1)}, f32[512,51]{0,1:T(8,128)}, u32[]{:S(2)}) copy-start(f32[512,51]{0,1:T(8,128)} %param.24) | copy-start | bytes 313348
  7.2 7.1 %copy-start.41 = (s32[8]{0:T(128)S(1)}, s32[8]{0:T(128)}, u32[]{:S(2)}) copy-start(s32[8]{0:T(128)} %param.22) | copy-start | bytes 100
  7.2 7.3 %copy-start.39 = (f32[512]{0:T(512)S(1)}, f32[512]{0:T(512)}, u32[]{:S(2)}) copy-start(f32[512]{0:T(512)} %param.25) | copy-start | bytes 6148
  7.2 7.4 %copy-start.40 = (s32[512]{0:T(512)S(1)}, s32[512]{0:T(512)}, u32[]{:S(2)}) copy-start(s32[512]{0:T(512)} %param.23) | copy-start | bytes 6148
  7.2 229.1 %all-gather.4.cloned.1.call-start = ((), (), s32[]{:S(2)}) async-start(), calls=%async_computation.2 | async-start | bytes 7839744 | tf_op jit(solution)/shard_map/all_gather | solution.py:442
  8.8 6.9 %copy-start.37 = (f32[51]{0:T(128)}, f32[51]{0:T(128)S(1)}, u32[]{:S(2)}) copy-start(f32[51]{0:T(128)S(1)} %slice.338) | copy-start | bytes 616
  11.0 12.0 %copy-start.29 = (f32[72,64]{0,1:T(8,128)S(1)}, f32[72,64]{0,1:T(8,128)}, u32[]{:S(2)}) copy-start(f32[72,64]{0,1:T(8,128)} %param.28) | copy-start | bytes 55300
  12.2 11.0 %copy-start.30 = (f32[64,64]{1,0:T(8,128)S(1)}, f32[64,64]{1,0:T(8,128)}, u32[]{:S(2)}) copy-start(f32[64,64]{1,0:T(8,128)} %param.27) | copy-start | bytes 49156
  12.2 11.1 %copy-start.31 = (f32[32,32]{1,0:T(8,128)S(1)}, f32[32,32]{1,0:T(8,128)}, u32[]{:S(2)}) copy-start(f32[32,32]{1,0:T(8,128)} %param.26) | copy-start | bytes 12292
  15.6 217.4 %all-to-all-start = ((f32[8,1,3456]{2,1,0:T(1,128)}), f32[8,1,3456]{2,1,0:T(1,128)S(1)}, u32[]{:S(2)}, u32[]{:S(2)}) async-start(f32[8,1,3456]{2,1,0:T(1,128)} %reshape.924), calls=%async_computation | async-start | bytes 221184 | tf_op jit(solution)/shard_map/all_to_all | solution.py:449
  22.9 379.5 %all-reduce.6.cloned.1.call-start = ((), (), s32[]{:S(2)}) async-start(), calls=%async_computation.4 | async-start | bytes 622592
  176.3 2.9 copy-start.36
  179.7 9.3 %copy-start.2 = (bf16[4,768,640]{2,1,0:T(8,128)(2,1)S(1)}, bf16[4,768,640]{2,1,0:T(8,128)(2,1)}, u32[]{:S(2)}) copy-start(bf16[4,768,640]{2,1,0:T(8,128)(2,1)} %broadcast_in_dim.192) | copy-start | bytes 11796484
  183.8 5.2 copy-start
  183.8 5.5 copy-start.1
  194.7 35.9 %copy-start.32 = (s32[512]{0:T(512)S(1)}, s32[512]{0:T(512)}, u32[]{:S(2)}) copy-start(s32[512]{0:T(512)} %param.21) | copy-start | bytes 6148
  322.7 2.2 copy-start.21
  322.7 2.2 copy-start.22
  322.8 2.3 copy-start.23
  322.8 2.3 copy-start.24
  322.8 3.6 copy-start.5
  322.8 3.6 copy-start.6
  322.8 3.6 copy-start.7
  322.8 3.6 copy-start.8
  322.8 3.6 copy-start.9
  322.8 3.6 copy-start.10
  322.8 3.6 copy-start.11
  322.8 3.6 copy-start.12
  322.9 3.6 copy-start.13
  322.9 3.6 copy-start.14
  322.9 3.6 copy-start.15
  322.9 3.6 copy-start.16
  322.9 3.6 copy-start.17
  322.9 3.6 copy-start.18
  322.9 3.6 copy-start.19
  322.9 3.6 copy-start.20
  325.0 2.5 copy-start.3
  328.5 1.6 copy-start.4
  328.5 1.6 copy-start.26
  330.9 242.3 %reduce-scatter.2.cloned.1.call-start = ((), (), s32[]{:S(2)}) async-start(), calls=%async_computation.3 | async-start | bytes 7839744 | tf_op jit(solution)/shard_map/reduce_scatter | solution.py:457
  330.9 0.7 copy-start.42
  330.9 2.6 copy-start.35
  330.9 42.1 %copy-start.25 = (f32[512,1]{1,0:T(8,128)S(1)}, f32[512,1]{1,0:T(8,128)}, u32[]{:S(2)}) copy-start(f32[512,1]{1,0:T(8,128)} %get-tuple-element.44) | copy-start | bytes 6148
  331.6 243.5 %copy-start.38 = (f32[51]{0:T(128)S(1)}, f32[51]{0:T(128)}, u32[]{:S(2)}) copy-start(f32[51]{0:T(128)} %copy-done.37) | copy-start | bytes 616
  331.6 244.8 %copy-start.28 = (f32[2,3136]{1,0:T(2,128)S(1)}, f32[2,3136]{1,0:T(2,128)}, u32[]{:S(2)}) copy-start(f32[2,3136]{1,0:T(2,128)} %param.32) | copy-start | bytes 75268
Sparse Core Ops, SparseCore 0:
  14.4 77.7 all-gather.3
  331.0 71.4 all-reduce.5
  404.9 168.2 reduce-scatter.1

commit v2 on v1

v2 whole, which is shorter than its diff:
```python
import functools

import jax
import jax.numpy as jnp
from jax import lax
from jax.experimental import pallas as pl
from jax.experimental.pallas import tpu as pltpu
from jax.sharding import PartitionSpec as P

F32 = jnp.float32
BF16 = jnp.bfloat16
VMEM_LIMIT = 60 * 1024 * 1024


def sigmoid(v):
    return 0.5 * jnp.tanh(0.5 * v) + 0.5


def silu_and_slope(v):
    s = sigmoid(v)
    a = v * s
    return a, s + a * (1.0 - s)


def dot(a, b):
    return lax.dot_general(a, b, (((1,), (0,)), ((), ())), preferred_element_type=F32)


def dot_nt(a, b):
    return lax.dot_general(a, b, (((1,), (1,)), ((), ())), preferred_element_type=F32)


def dot_tn(a, b):
    return lax.dot_general(a, b, (((0,), (0,)), ((), ())), preferred_element_type=F32)


def columns_of_one():
    return [7 * (g // 8) + g % 8 if g % 8 < 7 and 7 * (g // 8) + g % 8 < 20 else -9 for g in range(24)]


def half_lanes(left, right, rows):
    lane = lax.broadcasted_iota(jnp.int32, (rows, 128), 1)
    zero = jnp.zeros((rows, 128), F32)
    return jnp.where(lane < 64, zero if left is None else left, zero if right is None else right)


def fill_band_one(k1_ref, band):
    lane = lax.broadcasted_iota(jnp.int32, (16, 128), 1) // 32
    for u in range(8):
        taps = [k1_ref[((u // 4) * 2 + v) * 64 + (u % 4) * 16 :][:16].astype(F32) for v in range(2)]
        for g in range(8):
            for h in range(2):
                col = lane + 4 * h
                here = jnp.where((col == g) & (col < 7), taps[0], 0.0) + jnp.where((col == g - 1) & (col < 7), taps[1], 0.0)
                band[128 * u + 16 * g : 128 * u + 16 * g + 16, 128 * h : 128 * h + 128] = here.astype(BF16)


def fill_band_two(k2_ref, band):
    band[...] = jnp.zeros_like(band)
    cols = columns_of_one()
    for u in range(4):

        def tap(v):
            at = ((u // 2) * 2 + v // 2) * 128 + ((u % 2) * 2 + v % 2) * 32
            return k2_ref[at : at + 32, :].astype(F32)

        for g, q in enumerate(cols):
            if q < 0:
                continue
            used = {(q - v) // 2: v for v in (q % 2, q % 2 + 2) if 0 <= (q - v) // 2 < 9}
            for m in sorted({c // 2 for c in used}):
                sides = [tap(used[2 * m + side]) if 2 * m + side in used else None for side in range(2)]
                band[u, 32 * g : 32 * g + 32, 128 * m : 128 * m + 128] = half_lanes(*sides, 32).astype(BF16)


def fill_band_three(k3_ref, band):
    band[...] = jnp.zeros_like(band)
    for u in range(3):

        def tap(v):
            return k3_ref[(u * 3 + v) * 64 : (u * 3 + v) * 64 + 64, :].astype(F32)

        for q in range(9):
            used = {q - v: v for v in range(3) if 0 <= q - v < 7}
            for m in sorted({c // 2 for c in used}):
                sides = [tap(used[2 * m + side]) if 2 * m + side in used else None for side in range(2)]
                band[u, 64 * q : 64 * q + 64, 128 * m : 128 * m + 128] = half_lanes(*sides, 64).astype(BF16)


def fold_lanes(v, width):
    step = 64
    while step >= width:
        v = v + pltpu.roll(v, step, 1)
        step //= 2
    return v


def take_band_one(d1, out):
    lane = lax.broadcasted_iota(jnp.int32, (16, 128), 1) // 32
    for u in range(8):
        for v in range(2):
            total = jnp.zeros((16, 128), F32)
            for col in range(7):
                at = 128 * u + 16 * (col + v)
                h = col // 4
                total = total + jnp.where(lane + 4 * h == col, d1[at : at + 16, 128 * h : 128 * h + 128], 0.0)
            at = ((u // 4) * 2 + v) * 64 + (u % 4) * 16
            out[at : at + 16, :] = fold_lanes(total, 32)


def take_band_two(blocks, out):
    cols = columns_of_one()
    lane = lax.broadcasted_iota(jnp.int32, (32, 128), 1)
    for u in range(4):
        for v in range(4):
            total = jnp.zeros((32, 128), F32)
            for ref, first, c0, count in blocks:
                for c in range(count):
                    at = 32 * (cols.index(2 * (c0 + c) + v) - first)
                    piece = ref[u, at : at + 32, 128 * (c // 2) : 128 * (c // 2) + 128]
                    total = total + jnp.where((lane < 64) == (c % 2 == 0), piece, 0.0)
            at = ((u // 2) * 2 + v // 2) * 128 + ((u % 2) * 2 + v % 2) * 32
            out[at : at + 32, :] = fold_lanes(total, 64)


def take_band_three(d3, out):
    lane = lax.broadcasted_iota(jnp.int32, (64, 128), 1)
    for u in range(3):
        for v in range(3):
            total = jnp.zeros((64, 128), F32)
            for c in range(4):
                piece = d3[u, 64 * (c + v) : 64 * (c + v) + 64, 128 * (c // 2) : 128 * (c // 2) + 128]
                total = total + jnp.where((lane < 64) == (c % 2 == 0), piece, 0.0)
            at = (u * 3 + v) * 64
            out[at : at + 64, :] = fold_lanes(total, 64)


def shifted_blocks(x):
    rows = x.shape[0]
    return (
        x[:, 0:128],
        x[:, 112:240],
        jnp.concatenate([x[:, 224:336], jnp.zeros((rows, 16), x.dtype)], axis=1),
    )


def forward_kernel(
    x_ref, xn_ref, k1_ref, k2_ref, k3_ref, a1_ref, s1_ref, a2_ref, s2_ref, f_ref, s3_ref, y_ref, y0_ref, carry, a1s, a2s, b1_ref, b2_ref, b3_ref
):
    i = pl.program_id(0)
    rows = x_ref.shape[2]

    @pl.when(i == 0)
    def _():
        fill_band_one(k1_ref, b1_ref)
        fill_band_two(k2_ref, b2_ref)
        fill_band_three(k3_ref, b3_ref)
        for r in range(4):
            for j, blk in enumerate(shifted_blocks(x_ref[0, r])):
                carry[j, :, 128 * r : 128 * r + 128] = blk
        y0_ref[...] = carry[...]

    for pp in range(4):
        for r in range(4):
            src = x_ref[pp + 1, r] if pp < 3 else xn_ref[0, r]
            for j, blk in enumerate(shifted_blocks(src)):
                y_ref[pp, j, :, 128 * r : 128 * r + 128] = blk
        for j in range(3):
            lhs = jnp.concatenate([carry[j] if pp == 0 else y_ref[pp - 1, j], y_ref[pp, j]], axis=1)
            act, slope = silu_and_slope(dot(lhs, b1_ref[...]))
            act = act.astype(BF16)
            a1_ref[pp // 2, pp % 2, :, 256 * j : 256 * j + 256] = act
            a1s[2 * i + pp // 2, pp % 2, :, 256 * j : 256 * j + 256] = act
            s1_ref[pp // 2, pp % 2, :, 256 * j : 256 * j + 256] = slope.astype(BF16)
    carry[...] = y_ref[3]

    def second(p):
        for lo, hi, n0, n1 in ((0, 384, 0, 256), (256, 640, 256, 512), (512, 768, 512, 640)):
            lhs = jnp.concatenate([a1s[p + u // 2, u % 2, :, lo:hi] for u in range(4)], axis=1)
            rhs = jnp.concatenate([b2_ref[u, lo:hi, n0:n1] for u in range(4)], axis=0)
            act, slope = silu_and_slope(dot(lhs, rhs))
            act = act.astype(BF16)
            a2_ref[p, :, n0:n1] = act
            a2s[p, :, n0:n1] = act
            s2_ref[p, :, n0:n1] = slope.astype(BF16)

    def third(p, odd):
        acts, slopes = [], []
        for lo, hi, n0, n1 in ((0, 384, 0, 256), (256, 640, 256, 512)):
            lhs = jnp.concatenate([a2s[p + u, :, lo:hi] for u in range(3)], axis=1)
            rhs = jnp.concatenate([b3_ref[u, lo:hi, n0:n1] for u in range(3)], axis=0)
            act, slope = silu_and_slope(dot(lhs, rhs))
            acts.append(act)
            slopes.append(slope)
        lane = lax.broadcasted_iota(jnp.int32, (rows, 512), 1)
        base = (p // 2) * 896
        for out, parts in ((f_ref, acts), (s3_ref, slopes)):
            whole = jnp.where(lane < 448, jnp.concatenate(parts, axis=1), 0.0)
            if not odd:
                out[:, pl.ds(pl.multiple_of(base, 128), 512)] = whole.astype(BF16)
            else:
                whole = pltpu.roll(whole, 64, 1)
                at = pl.ds(pl.multiple_of(base + 384, 128), 128)
                out[:, at] = (out[:, at].astype(F32) + whole[:, :128]).astype(BF16)
                out[:, pl.ds(pl.multiple_of(base + 512, 128), 384)] = whole[:, 128:].astype(BF16)

    @pl.when(i >= 1)
    def _():
        second(2 * i - 1)

    second(2 * i)

    @pl.when(i >= 2)
    def _():
        third(2 * i - 3, True)

    @pl.when(i >= 1)
    def _():
        third(2 * i - 2, False)

    @pl.when(i == 4)
    def _():
        lane = lax.broadcasted_iota(jnp.int32, (rows, 128), 1)
        last = f_ref[:, 3072:3200].astype(F32)
        f_ref[:, 3072:3200] = jnp.where(lane == 64, 1.0, last).astype(BF16)


def full(shape):
    return pl.BlockSpec(shape, lambda *_: (0,) * len(shape))


def once(shape):
    return pl.BlockSpec(shape, lambda *_: (0,) * len(shape), pipeline_mode=pl.Buffered(1))


BANDS = [(1024, 256), (4, 768, 640), (3, 640, 512)]


def torso_forward(x, kern1, kern2, kern3):
    rows = x.shape[2]
    shapes = [(10, 2, rows, 768)] * 2 + [(9, rows, 640)] * 2 + [(rows, 3200)] * 2 + [(20, 3, rows, 512), (3, rows, 512)]
    return pl.pallas_call(
        forward_kernel,
        grid=(5,),
        in_specs=[
            pl.BlockSpec((4, 4, rows, 336), lambda i: (i, 0, 0, 0)),
            pl.BlockSpec((1, 4, rows, 336), lambda i: (4 * i + 4, 0, 0, 0)),
            once(kern1.shape),
            once(kern2.shape),
            once(kern3.shape),
        ],
        out_specs=[pl.BlockSpec((2, 2, rows, 768), lambda i: (i, 0, 0, 0))] * 2
        + [once((9, rows, 640))] * 2
        + [once((rows, 3200))] * 2
        + [pl.BlockSpec((4, 3, rows, 512), lambda i: (i, 0, 0, 0)), once((3, rows, 512))],
        out_shape=[jax.ShapeDtypeStruct(s, BF16) for s in shapes],
        scratch_shapes=[
            pltpu.VMEM((3, rows, 512), BF16),
            pltpu.VMEM((10, 2, rows, 768), BF16),
            pltpu.VMEM((9, rows, 640), BF16),
            *[pltpu.VMEM(s, BF16) for s in BANDS],
        ],
        compiler_params=pltpu.CompilerParams(vmem_limit_bytes=VMEM_LIMIT),
        name="torso_forward",
    )(x, x, kern1, kern2, kern3)


def coordinates():
    d, m = lax.axis_index("dp"), lax.axis_index("mp")
    return {"z": d // 2, "y": d % 2, "x": m // 2, "c": m % 2}


def device_at(at):
    return dict(
        device_id={"dp": at["z"] * 2 + at["y"], "mp": at["x"] * 2 + at["c"]}, device_id_type=pl.DeviceIdType.MESH
    )


AXES = {"x": 2, "z": 4, "y": 2}
HALF = 3712
SUM_FLOWS = [(0, 0, HALF, "xzy"), (1, 0, HALF, "yxz")]


def flow_buffers(flows):
    shapes = []
    for _, lo, hi, order in flows:
        for s, axis in enumerate(order):
            rest = [AXES[a] for a in AXES if a in order[s + 1 :]]
            shapes.append((AXES[axis] - 1, *rest, 16, hi - lo))
    return shapes


def peers_of(axis):
    me = coordinates()
    n = AXES[axis]
    return [{**me, axis: lax.rem(me[axis] + k, n)} for k in range(1, n)]


def block_of(ref, half, lo, hi, at):
    return ref.at[(half, *[at.get(a, slice(None)) for a in AXES], slice(None), slice(lo, hi))]


def sum_copies(acc, flow, stage, buf, send, recv):
    half, lo, hi, order = flow
    me = coordinates()
    held = {a: me[a] for a in order[:stage]}
    copies = []
    for k, peer in enumerate(peers_of(order[stage])):
        src = block_of(acc, half, lo, hi, {**held, order[stage]: peer[order[stage]]})
        copies.append(pltpu.make_async_remote_copy(src, buf.at[k], send.at[k], recv.at[k], **device_at(peer)))
    return copies


def add_arrived(acc, flow, stage, buf, out=None):
    half, lo, hi, order = flow
    me = coordinates()
    own = block_of(acc, half, lo, hi, {a: me[a] for a in order[: stage + 1]})
    total = own[...].astype(F32)
    for k in range(AXES[order[stage]] - 1):
        total = total + buf[k].astype(F32)
    if out is None:
        own[...] = total.astype(BF16)
    else:
        out[half, :, lo:hi] = total


def everyone(axis, count):
    me = lax.axis_index(axis)
    return [dict(device_id={axis: lax.rem(me + k, count)}, device_id_type=pl.DeviceIdType.MESH) for k in range(1, count)]


def share(axis, count, src, buf, send, recv):
    me = lax.axis_index(axis)
    return [
        pltpu.make_async_remote_copy(src(k), buf.at[me], send.at[k], recv.at[k], **to)
        for k, to in enumerate(everyone(axis, count))
    ]


def in_order(buf, count):
    total = buf[0].astype(F32)
    for k in range(1, count):
        total = total + buf[k].astype(F32)
    return total


def pack_kernels(d, o1, o2, o3):
    lane = lax.broadcasted_iota(jnp.int32, (32, 128), 1)
    two = jnp.where(lane < 64, o2[64 * d : 64 * d + 32, :], o2[64 * d + 32 : 64 * d + 64, :])
    three = jnp.where(lane < 64, o3[72 * d : 72 * d + 32, :], o3[72 * d + 32 : 72 * d + 64, :])
    lane = lane[:8] // 32
    one = jnp.zeros((8, 128), F32)
    for k in range(4):
        one = jnp.where(lane == k, o1[32 * d + 8 * k : 32 * d + 8 * k + 8, :], one)
    return jnp.concatenate([two, three, o3[72 * d + 64 : 72 * d + 72, :], one], axis=0)


def unpack_kernels(v, c1, c2, c3):
    c2[0:32, :] = v[0:32, 0:64]
    c2[32:64, :] = pltpu.roll(v[0:32], 64, 1)[:, 0:64]
    c3[0:32, :] = v[32:64, 0:64]
    c3[32:64, :] = pltpu.roll(v[32:64], 64, 1)[:, 0:64]
    c3[64:72, :] = v[64:72, 0:64]
    for k in range(4):
        turned = v[72:80] if k == 0 else pltpu.roll(v[72:80], 128 - 32 * k, 1)
        c1[8 * k : 8 * k + 8, :] = turned[:, 0:32]


def backward_kernel(summed, *refs):
    (y_ref, y0_ref, a1_ref, s1_ref, a2_ref, s2_ref, s3_ref, fg_ref, k2_ref, k3_ref), refs = refs[:10], refs[10:]
    if summed:
        (dw_ref, stat_ref, dsum_ref, stat_out, c1_ref, c2_ref, c3_ref), refs = refs[:7], refs[7:]
    (o1_ref, o2_ref, o3_ref), refs = refs[:3], refs[3:]
    (carry, g3, g2, b2_ref, b3_ref, d1_ref, d2a_ref, d2b_ref, d2c_ref, d3_ref), refs = refs[:10], refs[10:]
    if summed:
        (acc, core_buf, stat_dp, stat_mp, kern_send, kern_dp, kern_mp, core_sems, load_sem, sems, send_s, recv_s), bufs = refs[:12], refs[12:]
        me = coordinates()
        stages = {}
        at = 0
        for f, flow in enumerate(SUM_FLOWS):
            for s in range(3):
                stages[f, s] = (acc, flow, s, bufs[at], sems.at[0, at], sems.at[1, at])
                at += 1

        def core_copies():
            other = {**me, "c": 1 - me["c"]}
            return [
                pltpu.make_async_remote_copy(
                    dw_ref.at[h, :, 1 - me["c"]], core_buf.at[h], core_sems.at[0, h], core_sems.at[1, h], **device_at(other)
                )
                for h in range(2)
            ]

        def loads():
            return [pltpu.make_async_copy(dw_ref.at[h, :, me["c"]], acc.at[h], load_sem.at[h]) for h in range(2)]

        def stat_copies(axis, count, k):
            src = stat_ref if k == 0 else stat_mp.at[lax.axis_index("mp")]
            return share(axis, count, lambda _: src, (stat_dp, stat_mp)[k], send_s.at[k], recv_s.at[k])

        def kern_copies(axis, count, k):
            ids = [lax.rem(lax.axis_index("dp") + j, 8) for j in range(1, 8)]
            src = (lambda j: kern_send.at[ids[j]]) if k == 0 else (lambda _: kern_mp.at[lax.axis_index("mp")])
            return share(axis, count, src, (kern_dp, kern_mp)[k], send_s.at[2 + k], recv_s.at[2 + k])

        def start(copies):
            for copy in copies:
                copy.start()

        def finish(copies):
            for copy in copies:
                copy.wait()

        def first():
            barrier = pltpu.get_barrier_semaphore()
            ids = everyone("dp", 8) + everyone("mp", 4)
            for to in ids:
                pl.semaphore_signal(barrier, inc=1, **to)
            pl.semaphore_wait(barrier, len(ids))
            start(core_copies())
            start(loads())
            start(stat_copies("dp", 8, 0))
            stat_dp[lax.axis_index("dp")] = stat_ref[...]

        def after_core():
            finish(loads())
            finish(core_copies())
            for h in range(2):

                def one(j, _):
                    at = (h, j // 8, (j // 2) % 4, j % 2)
                    acc[at] = (acc[at].astype(F32) + core_buf[at].astype(F32)).astype(BF16)
                    return 0

                lax.fori_loop(0, 16, one, 0)
            for f in range(2):
                start(sum_copies(*stages[f, 0]))
            finish(stat_copies("dp", 8, 0))
            stat_mp[lax.axis_index("mp")] = in_order(stat_dp, 8)
            start(stat_copies("mp", 4, 1))

        def next_stage(f, s):
            finish(sum_copies(*stages[f, s]))
            add_arrived(*stages[f, s][:4], out=dsum_ref if s == 2 else None)
            if s < 2:
                start(sum_copies(*stages[f, s + 1]))

        def stats_done():
            finish(stat_copies("mp", 4, 1))
            stat_out[...] = in_order(stat_mp, 4)

        def kernels_out():
            for d in range(8):
                kern_send[d] = pack_kernels(d, o1_ref, o2_ref, o3_ref).astype(BF16)
            kern_dp[lax.axis_index("dp")] = kern_send[lax.axis_index("dp")]
            start(kern_copies("dp", 8, 0))

        def kernels_over():
            finish(kern_copies("dp", 8, 0))
            kern_mp[lax.axis_index("mp")] = in_order(kern_dp, 8)
            start(kern_copies("mp", 4, 1))

        def kernels_done():
            finish(kern_copies("mp", 4, 1))
            total = in_order(kern_mp, 4) / stat_out[9:10, :]
            unpack_kernels(total, c1_ref, c2_ref, c3_ref)

    i = pl.program_id(0)
    rows = y_ref.shape[2]

    @pl.when(i == 0)
    def _():
        if summed:
            first()
        fill_band_two(k2_ref, b2_ref)
        fill_band_three(k3_ref, b3_ref)
        for at in (0, 1, 9, 10):
            g3[at] = jnp.zeros((rows, 512), BF16)
        for at in (0, 10):
            g2[at] = jnp.zeros((rows, 640), BF16)
        lane = lax.broadcasted_iota(jnp.int32, (rows, 512), 1)
        for p in range(7):
            base = (p // 2) * 896 + (384 if p % 2 else 0)
            both = fg_ref[:, base : base + 512].astype(F32) * s3_ref[:, base : base + 512].astype(F32)
            if p % 2:
                both = pltpu.roll(both, 448, 1)
            g3[p + 2] = jnp.where(lane < 448, both, 0.0).astype(BF16)
        for u in range(3):
            total = 0.0
            for m in range(2):
                lhs = a2_ref[u : u + 7, :, 256 * m : 256 * m + 384].reshape(7 * rows, 384)
                rhs = g3[2:9, :, 256 * m : 256 * m + 256].reshape(7 * rows, 256)
                total = total + dot_tn(lhs, rhs)
            d3_ref[u] = total
        if summed:
            after_core()
        d1_ref[...] = jnp.zeros_like(d1_ref)
        d2a_ref[...] = jnp.zeros_like(d2a_ref)
        d2b_ref[...] = jnp.zeros_like(d2b_ref)
        d2c_ref[...] = jnp.zeros_like(d2c_ref)
        for lo, hi, n0, n1 in ((0, 256, 0, 256), (256, 512, 128, 512), (512, 640, 384, 512)):
            rhs = jnp.concatenate([b3_ref[u, lo:hi, n0:n1] for u in range(3)], axis=1)

            def one(p, _):
                lhs = jnp.concatenate([g3[p + 2 - u, :, n0:n1] for u in range(3)], axis=1)
                back = dot_nt(lhs, rhs) * s2_ref[p, :, lo:hi].astype(F32)
                g2[p + 1, :, lo:hi] = back.astype(BF16)
                return 0

            lax.fori_loop(0, 9, one, 0)

    for r in range(2):
        for t in range(2):
            for ref, lo, hi, n0, n1 in ((d2a_ref, 0, 384, 0, 256), (d2b_ref, 256, 640, 256, 512), (d2c_ref, 512, 768, 512, 640)):
                lhs = a1_ref[:, r, :, lo:hi].reshape(2 * rows, hi - lo)
                rhs = g2[pl.ds(2 * i + 1 - t, 2), :, n0:n1].reshape(2 * rows, n1 - n0)
                ref[2 * t + r] += dot_tn(lhs, rhs)

    @pl.when(i == 0)
    def _():
        carry[...] = y0_ref[...]

    for j, (n0, n1) in enumerate(((0, 256), (128, 512), (384, 640))):
        grads = []
        for pp in range(4):
            r = pp % 2
            at = 2 * i + pp // 2 + 1
            lhs = jnp.concatenate([g2[at, :, n0:n1], g2[at - 1, :, n0:n1]], axis=1)
            rhs = jnp.concatenate([b2_ref[r, 256 * j : 256 * j + 256, n0:n1], b2_ref[2 + r, 256 * j : 256 * j + 256, n0:n1]], axis=1)
            back = dot_nt(lhs, rhs) * s1_ref[pp // 2, r, :, 256 * j : 256 * j + 256].astype(F32)
            grads.append(back.astype(BF16))
        grad = jnp.concatenate(grads, axis=0)
        for t in range(2):
            pieces = [y_ref[k - 1 + t, j] if k + t > 0 else carry[j] for k in range(4)]
            lhs = jnp.concatenate(pieces, axis=0)
            d1_ref[512 * t : 512 * t + 512, :] += dot_tn(lhs, grad)
    carry[...] = y_ref[3]

    if summed:

        @pl.when(i == 2)
        def _():
            stats_done()
            next_stage(0, 0)
            next_stage(1, 0)

        @pl.when(i == 3)
        def _():
            next_stage(1, 1)

    @pl.when(i == 4)
    def _():
        if summed:
            next_stage(0, 1)
        take_band_one(d1_ref, o1_ref)
        take_band_two(((d2a_ref, 0, 0, 4), (d2b_ref, 8, 4, 4), (d2c_ref, 16, 8, 1)), o2_ref)
        take_band_three(d3_ref, o3_ref)
        if summed:
            kernels_out()
            next_stage(1, 2)
            next_stage(0, 2)
            kernels_over()
            kernels_done()


def torso_backward(y, y0, a1, s1, a2, s2, s3, fg, kern2, kern3, summed=None):
    rows = y.shape[2]
    sums = [(1024, 256), (4, 384, 256), (4, 384, 256), (4, 256, 128), (3, 384, 256)]
    own = [(256, 128), (512, 128), (576, 128)]
    args = [y, y0, a1, s1, a2, s2, s3, fg, kern2, kern3]
    in_specs = [
        pl.BlockSpec((4, 3, rows, 512), lambda i: (i, 0, 0, 0)),
        once(y0.shape),
        pl.BlockSpec((2, 2, rows, 768), lambda i: (i, 0, 0, 0)),
        pl.BlockSpec((2, 2, rows, 768), lambda i: (i, 0, 0, 0)),
        *[once(v.shape) for v in args[4:]],
    ]
    scratch = [
        pltpu.VMEM((3, rows, 512), BF16),
        pltpu.VMEM((11, rows, 512), BF16),
        pltpu.VMEM((11, rows, 640), BF16),
        *[pltpu.VMEM(s, BF16) for s in BANDS[1:]],
        *[pltpu.VMEM(s, F32) for s in sums],
    ]
    outs = own
    params = {}
    if summed is not None:
        args += summed
        in_specs += [pl.BlockSpec(memory_space=pl.ANY), once((16, 128))]
        outs = [(2, 16, HALF), (16, 128), (32, 32), (64, 64), (72, 64)]
        buffers = flow_buffers(SUM_FLOWS)
        scratch = [pltpu.VMEM(s, F32) for s in own] + scratch
        scratch += [
            pltpu.VMEM((2, *AXES.values(), 16, HALF), BF16),
            pltpu.VMEM((2, *AXES.values(), 16, HALF), BF16),
            pltpu.VMEM((8, 16, 128), F32),
            pltpu.VMEM((4, 16, 128), F32),
            pltpu.VMEM((8, 80, 128), BF16),
            pltpu.VMEM((8, 80, 128), BF16),
            pltpu.VMEM((4, 80, 128), F32),
            pltpu.SemaphoreType.DMA((2, 2)),
            pltpu.SemaphoreType.DMA((2,)),
            pltpu.SemaphoreType.DMA((2, len(buffers), 3)),
            pltpu.SemaphoreType.DMA((4, 7)),
            pltpu.SemaphoreType.DMA((4, 7)),
            *[pltpu.VMEM(s, BF16) for s in buffers],
        ]
        params = dict(collective_id=1, has_side_effects=True)
    return pl.pallas_call(
        functools.partial(backward_kernel, summed is not None),
        grid=(5,),
        in_specs=in_specs,
        out_specs=[once(s) for s in outs],
        out_shape=[jax.ShapeDtypeStruct(s, F32) for s in outs],
        scratch_shapes=scratch,
        compiler_params=pltpu.CompilerParams(vmem_limit_bytes=VMEM_LIMIT, **params),
        name="torso_backward",
    )(*args)


def high_low(v):
    high = v.astype(BF16)
    return high, (v - high.astype(F32)).astype(BF16)


def heads_kernel(
    atoms, acts, f_ref, w_ref, bias_ref, slot_ref, col_ref, row_ref, dw_ref, fg_ref, prio_ref, stat_ref
):
    rows = f_ref.shape[0]
    slots = slot_ref.shape[0]
    feats = f_ref[...]
    pre = [dot_nt(feats, w_ref[k, :, :3200]) for k in range(2)]
    hidden, slope = [], []
    for k in range(2):
        a, s = silu_and_slope(pre[k])
        hidden.append(a.astype(BF16))
        slope.append(s)
    out_w = jnp.concatenate([w_ref[0, :, 3200:], w_ref[1, :, 3200:]], axis=1)
    wide = out_w.shape[1]
    lane = lax.broadcasted_iota(jnp.int32, (1, wide), 1)
    zero = jnp.zeros((), BF16)
    w_val = jnp.where(lane[:, :128] < atoms, out_w[:, :128].astype(F32), 0.0).astype(BF16)
    w_adv = jnp.where(lane >= atoms, out_w.astype(F32), 0.0).astype(BF16)
    logits = dot(hidden[1], w_adv) + bias_ref[...]
    logits = jnp.concatenate([logits[:, :128] + dot(hidden[0], w_val), logits[:, 128:]], axis=1)
    high, low = high_low(logits)
    sel = jnp.where(lax.broadcasted_iota(jnp.int32, (slots, rows), 1) == col_ref[...], 1.0, 0.0).astype(BF16)
    selt = jnp.where(lax.broadcasted_iota(jnp.int32, (rows, slots), 0) == row_ref[...], 1.0, 0.0).astype(BF16)
    per_slot = dot(sel, high) + dot(sel, low)
    action = slot_ref[:, atoms + 2 : atoms + 3]
    which = jnp.where(lane < atoms, -1, jnp.where(lane < atoms * (acts + 1), (lane - atoms) // atoms, -2)).astype(F32)
    coeff = jnp.where(which == -1.0, 1.0, 0.0) + jnp.where(which == action, 1.0, 0.0) - jnp.where(which >= 0.0, 1.0 / acts, 0.0)
    atom = jnp.where(which >= -1.0, lane - atoms * (which.astype(jnp.int32) + 1), -1)
    fold = jnp.where(lax.broadcasted_iota(jnp.int32, (128, wide), 0) == atom, 1.0, 0.0).astype(BF16)
    high, low = high_low(per_slot * coeff)
    q = dot_nt(high, fold) + dot_nt(low, fold)
    lane_q = lax.broadcasted_iota(jnp.int32, (slots, 128), 1)
    used = lane_q < atoms
    top = jnp.max(jnp.where(used, q, -jnp.inf), axis=1, keepdims=True)
    shifted = jnp.where(used, jnp.exp(jnp.where(used, q - top, 0.0)), 0.0)
    total = jnp.sum(shifted, axis=1, keepdims=True)
    tgt = jnp.where(used, slot_ref[...], 0.0)
    cross = -jnp.sum(jnp.where(used, tgt * (q - top - jnp.log(total)), 0.0), axis=1, keepdims=True)
    coef = slot_ref[:, atoms : atoms + 1]
    valid = slot_ref[:, atoms + 1 : atoms + 2]
    prio_ref[...] = valid * cross
    q_grad = coef * (shifted * (jnp.sum(tgt, axis=1, keepdims=True) / total) - tgt)
    high, low = high_low(q_grad)
    lgrad = ((dot(high, fold) + dot(low, fold)) * coeff).astype(BF16)
    bias_grad = jnp.sum(lgrad.astype(F32), axis=0, keepdims=True)
    for k in range(8):
        stat_ref[k : k + 1, :] = bias_grad[:, 128 * k : 128 * k + 128]
    stat_ref[8:9, :] = jnp.broadcast_to(jnp.sum(coef * cross, axis=0, keepdims=True), (1, 128))
    stat_ref[9:10, :] = jnp.broadcast_to(jnp.sum(valid, axis=0, keepdims=True), (1, 128))
    stat_ref[10:16, :] = jnp.zeros((6, 128), F32)
    grad = dot(selt, lgrad).astype(BF16)
    d_adv = dot_tn(hidden[1], grad)
    d_val = dot_tn(hidden[0], grad[:, :128])
    dw_ref[0, :, 3200:3328] = jnp.where(lane[:, :128] < atoms, d_val, d_adv[:, :128]).astype(BF16)
    dw_ref[0, :, 3328:] = d_adv[:, 128:512].astype(BF16)
    dw_ref[1, :, 3200:] = d_adv[:, 512:].astype(BF16)
    pre_grad = [
        (dot_nt(grad[:, :128], w_val) * slope[0]).astype(BF16),
        (dot_nt(grad, w_adv) * slope[1]).astype(BF16),
    ]
    for k in range(2):
        for lo, hi in ((0, 1024), (1024, 2048), (2048, 3200)):
            dw_ref[k, :, lo:hi] = dot_tn(pre_grad[k], f_ref[:, lo:hi]).astype(BF16)
    for lo, hi in ((0, 1024), (1024, 2048), (2048, 3200)):
        back = dot(pre_grad[0], w_ref[0, :, lo:hi]) + dot(pre_grad[1], w_ref[1, :, lo:hi])
        fg_ref[:, lo:hi] = back.astype(BF16)


def heads(atoms, acts, feats, weights, bias, per_slot, rows_of_slot):
    slots = per_slot.shape[0]
    return pl.pallas_call(
        functools.partial(heads_kernel, atoms, acts),
        out_shape=[
            jax.ShapeDtypeStruct(weights.shape, BF16),
            jax.ShapeDtypeStruct(feats.shape, BF16),
            jax.ShapeDtypeStruct((slots, 1), F32),
            jax.ShapeDtypeStruct((16, 128), F32),
        ],
        compiler_params=pltpu.CompilerParams(vmem_limit_bytes=VMEM_LIMIT),
        name="heads",
    )(feats, weights, bias, per_slot, rows_of_slot[:, None], rows_of_slot[None, :])


def exchange_kernel(count, kern_ref, slot_ref, kerns_out, slots_out, send_kern, recv_kern, send_slot, recv_slot, own):
    me = lax.axis_index("dp")
    peers = [lax.rem(me + k, count) for k in range(count)]
    barrier = pltpu.get_barrier_semaphore()
    for k in range(1, count):
        pl.semaphore_signal(barrier, inc=1, device_id={"dp": peers[k]}, device_id_type=pl.DeviceIdType.MESH)
    pl.semaphore_wait(barrier, count - 1)
    mine = [
        pltpu.make_async_copy(kern_ref, kerns_out.at[me], own.at[0]),
        pltpu.make_async_copy(slot_ref.at[me], slots_out.at[me], own.at[1]),
    ]
    sent = []
    for k in range(1, count):
        to = dict(device_id={"dp": peers[k]}, device_id_type=pl.DeviceIdType.MESH)
        sent.append(pltpu.make_async_remote_copy(kern_ref, kerns_out.at[me], send_kern.at[k], recv_kern.at[k], **to))
        sent.append(pltpu.make_async_remote_copy(slot_ref.at[peers[k]], slots_out.at[me], send_slot.at[k], recv_slot.at[k], **to))
    for copy in mine + sent:
        copy.start()
    for copy in mine + sent:
        copy.wait()


def exchange(kern, slot):
    count = slot.shape[0]
    return pl.pallas_call(
        functools.partial(exchange_kernel, count),
        in_specs=[pl.BlockSpec(memory_space=pltpu.VMEM)] * 2,
        out_specs=[pl.BlockSpec(memory_space=pltpu.VMEM)] * 2,
        out_shape=[jax.ShapeDtypeStruct((count, *kern.shape), kern.dtype), jax.ShapeDtypeStruct(slot.shape, slot.dtype)],
        scratch_shapes=[pltpu.SemaphoreType.DMA((count,))] * 4 + [pltpu.SemaphoreType.DMA((2,))],
        compiler_params=pltpu.CompilerParams(collective_id=0, has_side_effects=True, vmem_limit_bytes=VMEM_LIMIT),
        name="exchange",
    )(kern, slot)


def on_device(
    frames,
    send_rows,
    recv_counts,
    actions,
    target_dist,
    sample_weight,
    conv_first,
    conv_second,
    conv_third,
    hidden_mean,
    hidden_spread,
    hidden_bias,
    feature_noise,
    hidden_noise,
    value_mean,
    value_spread,
    advantage_mean,
    advantage_spread,
    output_noise,
    output_bias,
):
    dp_count = lax.axis_size("dp")
    slots = send_rows.shape[0]
    capacity = slots // dp_count
    atoms = value_mean.shape[1]
    acts = advantage_mean.shape[1] // atoms
    rows = frames.shape[0]
    feat, own = hidden_mean.shape[1:]
    outs = atoms * (acts + 1)

    sizes = [w.size for w in (conv_first, conv_second, conv_third)]
    flat = jnp.concatenate([w.astype(BF16).reshape(-1) for w in (conv_first, conv_second, conv_third)])
    tall = -(-flat.size // 2048) * 16
    flat = jnp.pad(flat, (0, tall * 128 - flat.size)).reshape(tall, 128)
    is_valid = jnp.arange(capacity, dtype=jnp.int32)[None, :] < recv_counts[:, None]
    is_valid = is_valid.astype(F32).reshape(slots)
    per_slot = jnp.stack([is_valid * sample_weight, is_valid, actions.astype(F32)], axis=1)
    per_slot = jnp.concatenate([target_dist, per_slot, jnp.zeros((slots, 125 - atoms), F32)], axis=1)
    flat, per_slot = exchange(flat, per_slot.reshape(dp_count, capacity, 128))
    per_slot = per_slot.reshape(slots, 128)
    flat = flat.reshape(dp_count, -1)
    kern1 = jnp.tile(flat[:, : sizes[0]].reshape(-1, 32), (1, 4))
    kern2 = jnp.tile(flat[:, sizes[0] : sizes[0] + sizes[1]].reshape(-1, 64), (1, 2))
    kern3 = jnp.tile(flat[:, sizes[0] + sizes[1] : sum(sizes)].reshape(-1, 64), (1, 2))

    mean_t = hidden_mean.transpose(0, 2, 1)
    spread_t = hidden_spread.transpose(0, 2, 1)
    wide_one = mean_t + spread_t * feature_noise[:, None, :] * hidden_noise[0][:, :, None]
    wide_one = jnp.concatenate([wide_one, hidden_bias[:, :, None], jnp.zeros((2, own, 63), F32)], axis=2)
    wide_val = value_mean + value_spread * hidden_noise[1, 0][:, None] * output_noise[None, :atoms]
    wide_adv = advantage_mean + advantage_spread * hidden_noise[1, 1][:, None] * output_noise[None, atoms:]
    wide_out = jnp.concatenate([wide_val, wide_adv, jnp.zeros((own, 1024 - outs), F32)], axis=1)
    wide_out = wide_out.reshape(own, 2, 512).transpose(1, 0, 2)
    shard = jnp.concatenate([wide_one, wide_out], axis=2).astype(BF16)
    weights = lax.all_gather(shard, ("mp", "dp"), axis=1, tiled=True)

    x = frames.transpose(1, 0, 2).reshape(21, 4, rows, 336)
    a1, s1, a2, s2, feats, s3, y, y0 = torso_forward(x, kern1, kern2, kern3)
    bias = jnp.pad(output_bias, (0, 1024 - outs))[None, :]
    dweights, feat_grad, prio, stat = heads(atoms, acts, feats, weights, bias, per_slot, send_rows)
    torso = (y, y0, a1, s1, a2, s2, s3, feat_grad, kern2, kern3)
    if (dp_count, lax.axis_size("mp"), own) == (8, 4, 16):
        summed = [dweights.reshape(2, 2, 2, 4, 2, own, HALF), stat]
        dshard, stat, *conv_grads = torso_backward(*torso, summed=summed)
        inverse = 1.0 / stat[9, 0]
    else:
        dshard = lax.psum_scatter(dweights, ("mp", "dp"), scatter_dimension=1, tiled=True).astype(F32)
        stat = lax.psum(stat, ("dp", "mp"))
        inverse = 1.0 / stat[9, 0]
        k1, k2, k3 = torso_backward(*torso)
        kflat = jnp.concatenate([g.reshape(dp_count, -1) for g in (k1[:, :32], k2[:, :64], k3[:, :64])], axis=1)
        kflat = lax.psum(lax.psum_scatter(kflat, "dp", scatter_dimension=0, tiled=True)[0], "mp") * inverse
        conv_grads = (
            kflat[: sizes[0]].reshape(conv_first.shape),
            kflat[sizes[0] : sizes[0] + sizes[1]].reshape(conv_second.shape),
            kflat[sizes[0] + sizes[1] :].reshape(conv_third.shape),
        )

    dshard = dshard * inverse
    mean_grad_t = dshard[:, :, :feat]
    spread_grad_t = mean_grad_t * feature_noise[:, None, :] * hidden_noise[0][:, :, None]
    out_grad = dshard[:, :, 3200:].transpose(1, 0, 2).reshape(own, 1024)
    value_mean_grad = out_grad[:, :atoms]
    adv_mean_grad = out_grad[:, atoms:outs]
    return (
        stat[8, 0] * inverse,
        *conv_grads,
        mean_grad_t.transpose(0, 2, 1),
        spread_grad_t.transpose(0, 2, 1),
        dshard[:, :, feat],
        value_mean_grad,
        value_mean_grad * hidden_noise[1, 0][:, None] * output_noise[None, :atoms],
        adv_mean_grad,
        adv_mean_grad * hidden_noise[1, 1][:, None] * output_noise[None, atoms:],
        stat[:8].reshape(-1)[:outs] * inverse,
        prio[:, 0],
    )


def solution(mesh):
    both, heads_dim = P(("dp", "mp")), P(("mp", "dp"), None)
    return jax.shard_map(
        on_device,
        mesh=mesh,
        in_specs=(
            P(("dp", "mp"), None, None),
            both,
            both,
            both,
            P(("dp", "mp"), None),
            both,
            P("dp", None),
            P("dp", None),
            P("dp", None),
            P(None, None, ("mp", "dp")),
            P(None, None, ("mp", "dp")),
            P(None, ("mp", "dp")),
            P(),
            P(None, None, ("mp", "dp")),
            heads_dim,
            heads_dim,
            heads_dim,
            heads_dim,
            P(),
            P(),
        ),
        out_specs=(
            P(),
            P("dp", None),
            P("dp", None),
            P("dp", None),
            P(None, None, ("mp", "dp")),
            P(None, None, ("mp", "dp")),
            P(None, ("mp", "dp")),
            heads_dim,
            heads_dim,
            heads_dim,
            heads_dim,
            P(),
            both,
        ),
        check_vma=False,
    )
```

time: 590 us -> 221 us (0.37)
  waiting for transfers between devices: 184 us -> 14 us
  local copies, waits for them, and re-layouts: 158 us -> 20.5 us
  blocking collectives: 81.9 us -> 0 us
  Pallas kernels: 103 us -> 155 us
  other arithmetic: 33.7 us -> 14.2 us
  starting transfers between devices: 7.4 us -> 0.04 us
    reduce_scatter x1 -> x0, waiting for transfers between devices: 156 us -> none  [on_device(): lax.psum_scatter(dweights, ('mp', 'dp'), scatter_dimension=0, tiled=True)]
    broadcast_in_dim x17 -> x2, local copies, waits for them, and re-layouts: 118 us -> 1.55 us  [the longest x1 1.53 us: heads(): rows_of_slot[:, None]]
    pallas_call x1 -> x2, Pallas kernels: 49.6 us -> 101 us  [the longest x1 82.7 us: torso_backward(): pl.pallas_call(functools.partial(backward_kernel, summed is not None), gr...]
    psum x2 -> x0, blocking collectives: 50.1 us -> none  [the longest x1 39.6 us: on_device(): lax.psum((stat[0, 0], stat[1, 0], bias_grad[0, :outs]), ('dp', 'mp'))]
    all_gather x1 -> x0, blocking collectives: 31.8 us -> none  [on_device(): flat = lax.all_gather(flat, 'dp', axis=0, tiled=False)]
    unnamed x4 -> x1, waiting for transfers between devices: 27.4 us -> 0.02 us
    add x14 -> x0, other arithmetic: 16.7 us -> none  [the longest x1 5.39 us: band_two(): sum((jnp.where((source == 2 * col + v) & (col < 9), w[:, v], zero) for v...]
    all_gather x1, waiting for transfers between devices: 0.01 us -> 14 us  [on_device(): weights = lax.all_gather(shard, ('mp', 'dp'), axis=1, tiled=True)]
  transfers between devices with their start and end apart: 4 -> 1, of which waited for: 2 -> 1; matrix products, arithmetic and copies ran while one was open for 26% -> 7% of each run, Pallas kernels for 6% -> 24%
where the time goes in v2:
time: 221 us; the launch traced here: 220 us
  Pallas kernels  155 us (70%)
  local copies, waits for them, and re-layouts  20.5 us (9%)
  between operations  16.7 us (8%)
  other arithmetic  14.2 us (6%)
  waiting for transfers between devices  14 us (6%)
    pallas_call x1, Pallas kernels, torso_backward(): pl.pallas_call(functools.partial(backward_kernel, summed is not None), gr...  82.7 us
    pallas_call x1, Pallas kernels, torso_forward(): pl.pallas_call(forward_kernel, grid=(5,), in_specs=[pl.BlockSpec((4, 4, r...  35.4 us
    pallas_call x1, Pallas kernels, heads(): pl.pallas_call(functools.partial(heads_kernel, atoms, acts), out_shape=[j...  18.5 us
    pallas_call x1, Pallas kernels, exchange(): pl.pallas_call(functools.partial(exchange_kernel, count), in_specs=[pl.Bl...  17.9 us
    all_gather x1, waiting for transfers between devices, on_device(): weights = lax.all_gather(shard, ('mp', 'dp'), axis=1, tiled=True)  14 us
    unnamed x10, local copies, waits for them, and re-layouts  6.17 us
  transfers between devices with their start and end apart: 1, of which 1 were waited for; matrix products, arithmetic and copies ran while one was open for 7% of the time, Pallas kernels for 24%

profile of v2, /device:TPU:0, one launch (start us, length us, event | category | flops | bytes accessed | tf_op | source)
XLA Modules:
  0.0 219.9 jit_solution(17085306033413285165)
XLA Ops:
  7.2 0.7 slice_bitcast_fusion.3
  7.9 0.8 slice_bitcast_fusion.5
  8.7 0.7 slice.61
  9.4 0.8 slice.63
  10.1 0.7 convert_bitcast_fusion
  11.0 0.8 add_convert_fusion.2
  11.8 1.0 add_convert_fusion.1
  12.8 1.2 fusion.1
  14.1 0.8 concatenate.27
  14.9 0.7 iota_compare_fusion.2
  15.7 0.7 convert_element_type.33
  16.4 0.7 convert_element_type.29
  17.2 0.8 convert_element_type.30
  18.0 0.8 convert_element_type.31
  19.0 0.2 concatenate.29
  19.2 0.7 broadcast_select_fusion
  19.9 0.2 concatenate.28
  20.1 1.0 copy.37
  21.2 0.7 fusion
  21.9 1.0 concatenate.25.slot_ref
  23.0 0.6 fusion.7.kern_ref
  23.6 17.9 %exchange.1 = (bf16[8,80,128]{2,1,0:T(8,128)(2,1)}, f32[8,64,128]{2,1,0:T(8,128)}) custom-call(bf16[80,128]{1,0:T(8,128)(2,1)} %fusion.7.kern_ref, f32[8,64,128]{2,1,0:T(8,128)} %concatenate.25.slot_ref), custom_call_target="tpu_custom_call" | custom-call | tf_op jit(solution)/shard_map/exchange/pallas_call | solution.py:733
  41.5 1.0 copy.58
  42.5 1.3 pad.9
  43.8 1.5 copy.48.col_ref
  45.4 0.1 tile.30
  45.6 0.7 copy.43.k1_ref
  46.3 0.2 tile.33
  46.6 0.8 copy.44.k2_ref.refs_8_
  47.4 0.1 tile.36
  47.5 0.1 copy.42
  47.7 0.8 copy.45.k3_ref.refs_9_
  48.4 35.4 %torso_forward.1 = (bf16[10,2,272,768]{3,2,1,0:T(8,128)(2,1)}, bf16[10,2,272,768]{3,2,1,0:T(8,128)(2,1)}, bf16[9,272,640]{2,1,0:T(8,128)(2,1)}, bf16[9,272,640]{...) custom-call(bf16[21,4,272,336]{3,2,1,0:T(8,128)(2,1)} %bitcast.47, ...), custom_call_target="tpu_custom_call" | custom-call | tf_op jit(solution)/shard_map/torso_forward/pallas_call | solution.py:242
  83.8 14.0 %all-gather.2.cloned.1.call-done.w_ref = bf16[2,512,3712]{2,1,0:T(8,128)(2,1)} async-done(((bf16[2,16,3712]{2,1,0:T(8,128)(2,1)}), bf16[2,512,3712]{2,1,0:T(8,128)(2,1)}) %all-gather.2.cloned.1.call-update) | async-done | bytes 7602192 | tf_op jit(solution)/shard_map/all_gather | solution.py:799
  97.8 18.5 %heads.1 = (bf16[2,512,3712]{2,1,0:T(8,128)(2,1)}, bf16[272,3200]{1,0:T(8,128)(2,1)}, f32[512,1]{1,0:T(8,128)}, f32[16,128]{1,0:T(8,128)}) custom-call(bf16[272,3200]{1,0:T(8,128)(2,1)} %get-tuple-element.40.f_ref, bf16[2,512,3712]{2,1,0:T(8,128)(2,1)} %all-gather.2.cloned.1.call-done.w_ref, f32[1,1024]{1,0:T(1,128)} %bitcast.63, f32[512,128]{1,0:T(8,128)} %bitcast.58, ...), custom_call_target="tpu_custom_call" | custom-call | tf_op jit(solution)/shard_map/heads/pallas_call | solution.py:696
  116.3 82.7 %torso_backward.1 = (f32[2,16,3712]{2,1,0:T(8,128)}, f32[16,128]{1,0:T(8,128)}, f32[32,32]{1,0:T(8,128)}, f32[64,64]{1,0:T(8,128)}, f32[72,64]{1,0:T(8,128)}) custom-call(bf16[20,3,272,512]{3,2,1,0:T(8,128)(2,1)} %get-tuple-element.33.refs_0_, bf16[3,272,512]{2,1,0:T(8,128)(2,1)} %get-tuple-element.34.refs_1_, ...), custom_call_target="tpu_custom_call" | custom-call | tf_op jit(solution)/shard_map/torso_backward/pallas_call | solution.py:609
  199.0 1.3 fusion.8
  200.3 0.7 slice_bitcast_fusion.2
  201.7 1.1 broadcast_multiply_fusion
  202.7 0.7 slice_reduce_fusion
  203.5 0.7 multiply_multiply_fusion.1
  204.1 0.7 multiply_multiply_fusion
  204.9 0.9 multiply_bitcast_fusion
  206.4 0.6 slice_multiply_fusion
  207.0 1.5 copy.52
  208.5 0.7 reduce.1
  209.2 1.3 copy.62
  210.6 1.4 copy.63
  (28 shorter events, 1.1 us)
Async XLA Ops:
  7.2 90.6 %all-gather.2.cloned.1.call-start = ((), (), s32[]{:S(2)}) async-start(), calls=%async_computation | async-start | bytes 7839744 | tf_op jit(solution)/shard_map/all_gather | solution.py:799
  116.3 88.6 %copy-start.1 = (f32[2,3136]{1,0:T(2,128)S(1)}, f32[2,3136]{1,0:T(2,128)}, u32[]{:S(2)}) copy-start(f32[2,3136]{1,0:T(2,128)} %param.32) | copy-start | bytes 75268
  116.3 92.3 %copy-start = (f32[512,1]{1,0:T(8,128)S(1)}, f32[512,1]{1,0:T(8,128)}, u32[]{:S(2)}) copy-start(f32[512,1]{1,0:T(8,128)} %get-tuple-element.50) | copy-start | bytes 6148
Sparse Core Ops, SparseCore 0:
  15.0 82.7 all-gather.1

commit v3 on v2

--- a/solution.py
+++ b/solution.py
@@ -56,7 +56,6 @@
 
 
 def fill_band_two(k2_ref, band):
-    band[...] = jnp.zeros_like(band)
     cols = columns_of_one()
     for u in range(4):
 
@@ -74,7 +73,6 @@
 
 
 def fill_band_three(k3_ref, band):
-    band[...] = jnp.zeros_like(band)
     for u in range(3):
 
         def tap(v):
@@ -135,6 +133,205 @@
             out[at : at + 64, :] = fold_lanes(total, 64)
 
 
+def coordinates():
+    d, m = lax.axis_index("dp"), lax.axis_index("mp")
+    return {"z": d // 2, "y": d % 2, "x": m // 2, "c": m % 2}
+
+
+def device_at(at):
+    return dict(
+        device_id={"dp": at["z"] * 2 + at["y"], "mp": at["x"] * 2 + at["c"]}, device_id_type=pl.DeviceIdType.MESH
+    )
+
+
+AXES = {"x": 2, "z": 4, "y": 2}
+HALF = 3712
+CUT = 1536
+SUM_FLOWS = [(0, 0, CUT, "xzy"), (1, 0, CUT, "yzx"), (0, CUT, HALF, "xyz"), (1, CUT, HALF, "yxz")]
+GATHER_FLOWS = [(half, lo, hi, order[::-1]) for half, lo, hi, order in SUM_FLOWS]
+
+
+def flow_buffers(flows):
+    shapes = []
+    for _, lo, hi, order in flows:
+        for s, axis in enumerate(order):
+            rest = [AXES[a] for a in AXES if a in order[s + 1 :]]
+            shapes.append((AXES[axis] - 1, *rest, 16, hi - lo))
+    return shapes
+
+
+def peers_of(axis):
+    me = coordinates()
+    n = AXES[axis]
+    return [{**me, axis: lax.rem(me[axis] + k, n)} for k in range(1, n)]
+
+
+def block_of(ref, half, lo, hi, at):
+    return ref.at[(half, *[at.get(a, slice(None)) for a in AXES], slice(None), slice(lo, hi))]
+
+
+def sum_copies(acc, flow, stage, buf, send, recv):
+    half, lo, hi, order = flow
+    me = coordinates()
+    held = {a: me[a] for a in order[:stage]}
+    copies = []
+    for k, peer in enumerate(peers_of(order[stage])):
+        src = block_of(acc, half, lo, hi, {**held, order[stage]: peer[order[stage]]})
+        copies.append(pltpu.make_async_remote_copy(src, buf.at[k], send.at[k], recv.at[k], **device_at(peer)))
+    return copies
+
+
+def add_arrived(acc, flow, stage, buf, out=None):
+    half, lo, hi, order = flow
+    me = coordinates()
+    own = block_of(acc, half, lo, hi, {a: me[a] for a in order[: stage + 1]})
+    total = own[...].astype(F32)
+    for k in range(AXES[order[stage]] - 1):
+        total = total + buf[k].astype(F32)
+    if out is None:
+        own[...] = total.astype(BF16)
+    else:
+        out[half, :, lo:hi] = total
+
+
+def everyone(axis, count):
+    me = lax.axis_index(axis)
+    return [dict(device_id={axis: lax.rem(me + k, count)}, device_id_type=pl.DeviceIdType.MESH) for k in range(1, count)]
+
+
+def share(axis, count, src, buf, send, recv):
+    me = lax.axis_index(axis)
+    return [
+        pltpu.make_async_remote_copy(src(k), buf.at[me], send.at[k], recv.at[k], **to)
+        for k, to in enumerate(everyone(axis, count))
+    ]
+
+
+def in_order(buf, count):
+    total = buf[0].astype(F32)
+    for k in range(1, count):
+        total = total + buf[k].astype(F32)
+    return total
+
+
+def gathered_block(ref, half, lo, hi, core, at):
+    x, z, y = (at.get(a, slice(None)) for a in AXES)
+    return ref.at[half, x, core, z, y, :, lo:hi]
+
+
+def gather_copies(shard, out, flow, stage, send, recv):
+    half, lo, hi, order = flow
+    me = coordinates()
+    at = {a: me[a] for a in order[stage:]}
+    dst = gathered_block(out, half, lo, hi, me["c"], at)
+    src = shard.at[half, :, lo:hi] if stage == 0 else dst
+    return [
+        pltpu.make_async_remote_copy(src, dst, send.at[k], recv.at[k], **device_at(peer))
+        for k, peer in enumerate(peers_of(order[stage]))
+    ]
+
+
+def core_copy(out, flow, last, send, recv):
+    half, lo, hi, order = flow
+    me = coordinates()
+    axis = order[2]
+    block = gathered_block(out, half, lo, hi, me["c"], {axis: 1 - me[axis] if last else me[axis]})
+    other = {**me, "c": 1 - me["c"]}
+    return pltpu.make_async_remote_copy(block, block, send, recv, **device_at(other))
+
+
+def start(copies):
+    for copy in copies:
+        copy.start()
+
+
+def finish(copies):
+    for copy in copies:
+        copy.wait()
+
+
+def greet():
+    for to in everyone("dp", 8) + everyone("mp", 4):
+        pl.semaphore_signal(pltpu.get_barrier_semaphore(), inc=1, **to)
+
+
+def greeted():
+    pl.semaphore_wait(pltpu.get_barrier_semaphore(), 10)
+
+
+def as_column(row):
+    n = row.shape[1]
+    eye = lax.broadcasted_iota(jnp.int32, (n, n), 0) == lax.broadcasted_iota(jnp.int32, (n, n), 1)
+    return jnp.sum(jnp.where(eye, row, 0.0), axis=1, keepdims=True)
+
+
+def as_row(column):
+    n = column.shape[0]
+    eye = lax.broadcasted_iota(jnp.int32, (n, n), 0) == lax.broadcasted_iota(jnp.int32, (n, n), 1)
+    return jnp.sum(jnp.where(eye, column, 0.0), axis=0, keepdims=True)
+
+
+def pack_shards(c1, c2, c3t):
+    c3 = jnp.transpose(jnp.concatenate([c3t, jnp.zeros((64, 56), F32)], axis=1))
+    blank = jnp.zeros((8, 64), F32)
+    return jnp.concatenate(
+        [
+            jnp.concatenate([c2[0:32], c2[32:64]], axis=1),
+            jnp.concatenate([c3[0:32], c3[32:64]], axis=1),
+            jnp.concatenate([c3[64:72], blank], axis=1),
+            jnp.concatenate([c1[8 * k : 8 * k + 8] for k in range(4)], axis=1),
+        ],
+        axis=0,
+    )
+
+
+def unpack_shards(d, v, k1, k2, k3):
+    lane = lax.broadcasted_iota(jnp.int32, (32, 128), 1)
+
+    def sides(w):
+        turned = pltpu.roll(w, 64, 1)
+        low = lane[: w.shape[0]] < 64
+        return jnp.where(low, w, turned), jnp.where(low, turned, w)
+
+    k2[64 * d : 64 * d + 32, :], k2[64 * d + 32 : 64 * d + 64, :] = sides(v[0:32])
+    k3[72 * d : 72 * d + 32, :], k3[72 * d + 32 : 72 * d + 64, :] = sides(v[32:64])
+    k3[72 * d + 64 : 72 * d + 72, :] = sides(v[64:72])[0]
+    for k in range(4):
+        part = jnp.where(lane[:8] // 32 == k, v[72:80], 0.0)
+        k1[32 * d + 8 * k : 32 * d + 8 * k + 8, :] = fold_lanes(part, 32)
+
+
+def noisy_weights(shard, hm, hs, hb, fn, hn, vm, vs, am, adv_s, on):
+    atoms, outs = vm.shape[1], on.shape[1]
+    lane = lax.broadcasted_iota(jnp.int32, (16, 128), 1)
+    for h in range(2):
+        wide = hm[h] + hs[h] * fn[h : h + 1, :] * as_column(hn[0, h : h + 1, :])
+        shard[h, :, 0:3072] = wide[:, 0:3072].astype(BF16)
+        last = jnp.concatenate([wide[:, 3072:], jnp.zeros((16, 64), F32)], axis=1)
+        last = jnp.where(lane == 64, as_column(hb[h : h + 1, :]), last)
+        shard[h, :, 3072:3200] = last.astype(BF16)
+    val = vm[...] + vs[...] * as_column(hn[1, 0:1, :]) * on[:, :atoms]
+    adv = am[...] + adv_s[...] * as_column(hn[1, 1:2, :]) * on[:, atoms:]
+    out = jnp.concatenate([val, adv, jnp.zeros((16, 1024 - outs), F32)], axis=1).astype(BF16)
+    shard[0, :, 3200:] = out[:, :512]
+    shard[1, :, 3200:] = out[:, 512:]
+
+
+def slot_rows(staged, tt, cnt, act, sw):
+    atoms, slots = tt.shape
+    lane = lax.broadcasted_iota(jnp.int32, (8, slots), 1)
+    source = lax.broadcasted_iota(jnp.int32, (8, slots), 0)
+    cap = slots // 8
+    used = jnp.sum(jnp.where(lane // cap == source, as_column(cnt[...].astype(F32)), 0.0), axis=0, keepdims=True)
+    valid = jnp.where((lane[0:1] % cap).astype(F32) < used, 1.0, 0.0)
+    staged[...] = jnp.zeros_like(staged)
+    staged[0:atoms, :] = tt[...]
+    staged[atoms : atoms + 1, :] = valid * sw[...]
+    staged[atoms + 1 : atoms + 2, :] = valid
+    staged[atoms + 2 : atoms + 3, :] = act[...].astype(F32)
+    return jnp.transpose(staged[...])
+
+
 def shifted_blocks(x):
     rows = x.shape[0]
     return (
@@ -144,21 +341,112 @@
     )
 
 
-def forward_kernel(
-    x_ref, xn_ref, k1_ref, k2_ref, k3_ref, a1_ref, s1_ref, a2_ref, s2_ref, f_ref, s3_ref, y_ref, y0_ref, carry, a1s, a2s, b1_ref, b2_ref, b3_ref
-):
+def forward_kernel(shared, *refs):
+    if shared:
+        ins, refs = refs[:18], refs[18:]
+        (x_ref, xn_ref, c1, c2, c3t, hm, hs, hb, fn, hn, vm, vs, am, adv_s, on, tt, cnt, act), refs = ins, refs
+        (sw,), refs = refs[:1], refs[1:]
+    else:
+        (x_ref, xn_ref, k1_ref, k2_ref, k3_ref), refs = refs[:5], refs[5:]
+    (a1_ref, s1_ref, a2_ref, s2_ref, f_ref, s3_ref, y_ref, y0_ref), refs = refs[:8], refs[8:]
+    if shared:
+        (w_out, slot_out, k2_ref, k3_ref), refs = refs[:4], refs[4:]
+    (carry, a1s, b1_ref, b2_ref, b3_ref), refs = refs[:5], refs[5:]
     i = pl.program_id(0)
     rows = x_ref.shape[2]
-
-    @pl.when(i == 0)
-    def _():
-        fill_band_one(k1_ref, b1_ref)
-        fill_band_two(k2_ref, b2_ref)
-        fill_band_three(k3_ref, b3_ref)
+    if shared:
+        k1_ref, shard, kern_own, kern_buf, staged, slot_src, slot_buf, kern_s, kern_r, slot_s, slot_r, own_sem, sems, core_sems = refs
+        flow_stage = {
+            (f, s): (shard, w_out, flow, s, sems.at[0, f, s], sems.at[1, f, s])
+            for f, flow in enumerate(GATHER_FLOWS)
+            for s in range(3)
+        }
+
+        def kern_copies():
+            return share("dp", 8, lambda _: kern_own, kern_buf, kern_s, kern_r)
+
+        def slot_copies():
+            ids = [lax.rem(lax.axis_index("dp") + j, 8) for j in range(1, 8)]
+            return share("dp", 8, lambda j: slot_src.at[ids[j]], slot_buf, slot_s, slot_r)
+
+        def own_copies():
+            me = coordinates()
+            return [
+                pltpu.make_async_copy(shard.at[h], w_out.at[h, me["x"], me["c"], me["z"], me["y"]], own_sem.at[h])
+                for h in range(2)
+            ]
+
+        def to_core(f, last):
+            return core_copy(w_out, GATHER_FLOWS[f], last, core_sems.at[0, f, last], core_sems.at[1, f, last])
+
+        def begin():
+            greet()
+            kern_own[...] = pack_shards(c1[...], c2[...], c3t[...]).astype(BF16)
+            kern_buf[lax.axis_index("dp")] = kern_own[...]
+            noisy_weights(shard, hm, hs, hb, fn, hn, vm, vs, am, adv_s, on)
+            packed = slot_rows(staged, tt, cnt, act, sw).reshape(8, 2, 32, 128)
+            lane = lax.broadcasted_iota(jnp.int32, (8, 32, 128), 2)
+            slot_src[...] = jnp.where(lane < 64, packed[:, 0], pltpu.roll(packed[:, 1].reshape(256, 128), 64, 1).reshape(8, 32, 128))
+            slot_buf[lax.axis_index("dp")] = slot_src[lax.axis_index("dp")]
+            greeted()
+            start(kern_copies())
+            for f in range(4):
+                start(gather_copies(*flow_stage[f, 0]))
+            start(own_copies())
+            prepare()
+            finish(kern_copies())
+            for d in range(8):
+                unpack_shards(d, kern_buf[d].astype(F32), k1_ref, k2_ref, k3_ref)
+
+        def advance(f, s):
+            finish(gather_copies(*flow_stage[f, s]))
+            start(gather_copies(*flow_stage[f, s + 1]))
+
+        def point(step, k):
+            todo = []
+            if k == 1:
+                todo = [
+                    (1, lambda: (finish(own_copies()), [advance(f, 0) for f in (2, 3, 0, 1)])),
+                    (3, lambda: [(advance(f, 1), to_core(f, 0).start()) for f in (2, 3)]),
+                ]
+            elif k == 2:
+                todo = [
+                    (4, lambda: ([(advance(f, 1), to_core(f, 0).start()) for f in (0, 1)], start(slot_copies()))),
+                ]
+            for at, what in todo:
+
+                @pl.when(step == at)
+                def _():
+                    what()
+
+        def end():
+            for f in (2, 3, 0, 1):
+                finish(gather_copies(*flow_stage[f, 2]))
+                to_core(f, 1).start()
+            finish(slot_copies())
+            slot_out[:, 0:32] = slot_buf[...]
+            slot_out[:, 32:64] = pltpu.roll(slot_buf[...].reshape(256, 128), 64, 1).reshape(8, 32, 128)
+            for f in range(4):
+                for last in range(2):
+                    to_core(f, last).wait()
+
+    def prepare():
+        b2_ref[...] = jnp.zeros_like(b2_ref)
+        b3_ref[...] = jnp.zeros_like(b3_ref)
         for r in range(4):
             for j, blk in enumerate(shifted_blocks(x_ref[0, r])):
                 carry[j, :, 128 * r : 128 * r + 128] = blk
         y0_ref[...] = carry[...]
+
+    @pl.when(i == 0)
+    def _():
+        if shared:
+            begin()
+        else:
+            prepare()
+        fill_band_one(k1_ref, b1_ref)
+        fill_band_two(k2_ref, b2_ref)
+        fill_band_three(k3_ref, b3_ref)
 
     for pp in range(4):
         for r in range(4):
@@ -172,7 +460,11 @@
             a1_ref[pp // 2, pp % 2, :, 256 * j : 256 * j + 256] = act
             a1s[2 * i + pp // 2, pp % 2, :, 256 * j : 256 * j + 256] = act
             s1_ref[pp // 2, pp % 2, :, 256 * j : 256 * j + 256] = slope.astype(BF16)
+        if shared and pp == 1:
+            point(i, 1)
     carry[...] = y_ref[3]
+    if shared:
+        point(i, 2)
 
     def second(p):
         for lo, hi, n0, n1 in ((0, 384, 0, 256), (256, 640, 256, 512), (512, 768, 512, 640)):
@@ -181,13 +473,12 @@
             act, slope = silu_and_slope(dot(lhs, rhs))
             act = act.astype(BF16)
             a2_ref[p, :, n0:n1] = act
-            a2s[p, :, n0:n1] = act
             s2_ref[p, :, n0:n1] = slope.astype(BF16)
 
     def third(p, odd):
         acts, slopes = [], []
         for lo, hi, n0, n1 in ((0, 384, 0, 256), (256, 640, 256, 512)):
-            lhs = jnp.concatenate([a2s[p + u, :, lo:hi] for u in range(3)], axis=1)
+            lhs = jnp.concatenate([a2_ref[p + u, :, lo:hi] for u in range(3)], axis=1)
             rhs = jnp.concatenate([b3_ref[u, lo:hi, n0:n1] for u in range(3)], axis=0)
             act, slope = silu_and_slope(dot(lhs, rhs))
             acts.append(act)
@@ -223,6 +514,8 @@
         lane = lax.broadcasted_iota(jnp.int32, (rows, 128), 1)
         last = f_ref[:, 3072:3200].astype(F32)
         f_ref[:, 3072:3200] = jnp.where(lane == 64, 1.0, last).astype(BF16)
+        if shared:
+            end()
 
 
 def full(shape):
@@ -236,112 +529,60 @@
 BANDS = [(1024, 256), (4, 768, 640), (3, 640, 512)]
 
 
-def torso_forward(x, kern1, kern2, kern3):
+def torso_forward(x, kernels, shared=None):
     rows = x.shape[2]
     shapes = [(10, 2, rows, 768)] * 2 + [(9, rows, 640)] * 2 + [(rows, 3200)] * 2 + [(20, 3, rows, 512), (3, rows, 512)]
+    args = [x, x, *kernels]
+    out_specs = (
+        [pl.BlockSpec((2, 2, rows, 768), lambda i: (i, 0, 0, 0))] * 2
+        + [once((9, rows, 640))] * 2
+        + [once((rows, 3200))] * 2
+        + [pl.BlockSpec((4, 3, rows, 512), lambda i: (i, 0, 0, 0)), once((3, rows, 512))]
+    )
+    out_shape = [jax.ShapeDtypeStruct(s, BF16) for s in shapes]
+    scratch = [
+        pltpu.VMEM((3, rows, 512), BF16),
+        pltpu.VMEM((10, 2, rows, 768), BF16),
+        *[pltpu.VMEM(s, BF16) for s in BANDS],
+    ]
+    params = {}
+    if shared is not None:
+        args += shared
+        out_specs += [pl.BlockSpec(memory_space=pl.ANY), once((8, 64, 128)), once((512, 128)), once((576, 128))]
+        out_shape += [
+            jax.ShapeDtypeStruct((2, 2, 2, 4, 2, 16, HALF), BF16),
+            jax.ShapeDtypeStruct((8, 64, 128), F32),
+            jax.ShapeDtypeStruct((512, 128), F32),
+            jax.ShapeDtypeStruct((576, 128), F32),
+        ]
+        scratch += [
+            pltpu.VMEM((256, 128), F32),
+            pltpu.VMEM((2, 16, HALF), BF16),
+            pltpu.VMEM((80, 128), BF16),
+            pltpu.VMEM((8, 80, 128), BF16),
+            pltpu.VMEM((128, 512), F32),
+            pltpu.VMEM((8, 32, 128), F32),
+            pltpu.VMEM((8, 32, 128), F32),
+            *[pltpu.SemaphoreType.DMA((7,))] * 4,
+            pltpu.SemaphoreType.DMA((2,)),
+            pltpu.SemaphoreType.DMA((2, 4, 3, 3)),
+            pltpu.SemaphoreType.DMA((2, 4, 2)),
+        ]
+        params = dict(collective_id=0, has_side_effects=True)
     return pl.pallas_call(
-        forward_kernel,
+        functools.partial(forward_kernel, shared is not None),
         grid=(5,),
         in_specs=[
             pl.BlockSpec((4, 4, rows, 336), lambda i: (i, 0, 0, 0)),
             pl.BlockSpec((1, 4, rows, 336), lambda i: (4 * i + 4, 0, 0, 0)),
-            once(kern1.shape),
-            once(kern2.shape),
-            once(kern3.shape),
+            *[once(v.shape) for v in args[2:]],
         ],
-        out_specs=[pl.BlockSpec((2, 2, rows, 768), lambda i: (i, 0, 0, 0))] * 2
-        + [once((9, rows, 640))] * 2
-        + [once((rows, 3200))] * 2
-        + [pl.BlockSpec((4, 3, rows, 512), lambda i: (i, 0, 0, 0)), once((3, rows, 512))],
-        out_shape=[jax.ShapeDtypeStruct(s, BF16) for s in shapes],
-        scratch_shapes=[
-            pltpu.VMEM((3, rows, 512), BF16),
-            pltpu.VMEM((10, 2, rows, 768), BF16),
-            pltpu.VMEM((9, rows, 640), BF16),
-            *[pltpu.VMEM(s, BF16) for s in BANDS],
-        ],
-        compiler_params=pltpu.CompilerParams(vmem_limit_bytes=VMEM_LIMIT),
+        out_specs=out_specs,
+        out_shape=out_shape,
+        scratch_shapes=scratch,
+        compiler_params=pltpu.CompilerParams(vmem_limit_bytes=VMEM_LIMIT, **params),
         name="torso_forward",
-    )(x, x, kern1, kern2, kern3)
-
-
-def coordinates():
-    d, m = lax.axis_index("dp"), lax.axis_index("mp")
-    return {"z": d // 2, "y": d % 2, "x": m // 2, "c": m % 2}
-
-
-def device_at(at):
-    return dict(
-        device_id={"dp": at["z"] * 2 + at["y"], "mp": at["x"] * 2 + at["c"]}, device_id_type=pl.DeviceIdType.MESH
-    )
-
-
-AXES = {"x": 2, "z": 4, "y": 2}
-HALF = 3712
-SUM_FLOWS = [(0, 0, HALF, "xzy"), (1, 0, HALF, "yxz")]
-
-
-def flow_buffers(flows):
-    shapes = []
-    for _, lo, hi, order in flows:
-        for s, axis in enumerate(order):
-            rest = [AXES[a] for a in AXES if a in order[s + 1 :]]
-            shapes.append((AXES[axis] - 1, *rest, 16, hi - lo))
-    return shapes
-
-
-def peers_of(axis):
-    me = coordinates()
-    n = AXES[axis]
-    return [{**me, axis: lax.rem(me[axis] + k, n)} for k in range(1, n)]
-
-
-def block_of(ref, half, lo, hi, at):
-    return ref.at[(half, *[at.get(a, slice(None)) for a in AXES], slice(None), slice(lo, hi))]
-
-
-def sum_copies(acc, flow, stage, buf, send, recv):
-    half, lo, hi, order = flow
-    me = coordinates()
-    held = {a: me[a] for a in order[:stage]}
-    copies = []
-    for k, peer in enumerate(peers_of(order[stage])):
-        src = block_of(acc, half, lo, hi, {**held, order[stage]: peer[order[stage]]})
-        copies.append(pltpu.make_async_remote_copy(src, buf.at[k], send.at[k], recv.at[k], **device_at(peer)))
-    return copies
-
-
-def add_arrived(acc, flow, stage, buf, out=None):
-    half, lo, hi, order = flow
-    me = coordinates()
-    own = block_of(acc, half, lo, hi, {a: me[a] for a in order[: stage + 1]})
-    total = own[...].astype(F32)
-    for k in range(AXES[order[stage]] - 1):
-        total = total + buf[k].astype(F32)
-    if out is None:
-        own[...] = total.astype(BF16)
-    else:
-        out[half, :, lo:hi] = total
-
-
-def everyone(axis, count):
-    me = lax.axis_index(axis)
-    return [dict(device_id={axis: lax.rem(me + k, count)}, device_id_type=pl.DeviceIdType.MESH) for k in range(1, count)]
-
-
-def share(axis, count, src, buf, send, recv):
-    me = lax.axis_index(axis)
-    return [
-        pltpu.make_async_remote_copy(src(k), buf.at[me], send.at[k], recv.at[k], **to)
-        for k, to in enumerate(everyone(axis, count))
-    ]
-
-
-def in_order(buf, count):
-    total = buf[0].astype(F32)
-    for k in range(1, count):
-        total = total + buf[k].astype(F32)
-    return total
+    )(*args)
 
 
 def pack_kernels(d, o1, o2, o3):
@@ -355,44 +596,24 @@
     return jnp.concatenate([two, three, o3[72 * d + 64 : 72 * d + 72, :], one], axis=0)
 
 
-def unpack_kernels(v, c1, c2, c3):
-    c2[0:32, :] = v[0:32, 0:64]
-    c2[32:64, :] = pltpu.roll(v[0:32], 64, 1)[:, 0:64]
-    c3[0:32, :] = v[32:64, 0:64]
-    c3[32:64, :] = pltpu.roll(v[32:64], 64, 1)[:, 0:64]
-    c3[64:72, :] = v[64:72, 0:64]
-    for k in range(4):
-        turned = v[72:80] if k == 0 else pltpu.roll(v[72:80], 128 - 32 * k, 1)
-        c1[8 * k : 8 * k + 8, :] = turned[:, 0:32]
-
-
 def backward_kernel(summed, *refs):
     (y_ref, y0_ref, a1_ref, s1_ref, a2_ref, s2_ref, s3_ref, fg_ref, k2_ref, k3_ref), refs = refs[:10], refs[10:]
     if summed:
-        (dw_ref, stat_ref, dsum_ref, stat_out, c1_ref, c2_ref, c3_ref), refs = refs[:7], refs[7:]
+        (dw_ref, stat_ref, dsum_ref, stat_out, kern_out), refs = refs[:5], refs[5:]
     (o1_ref, o2_ref, o3_ref), refs = refs[:3], refs[3:]
     (carry, g3, g2, b2_ref, b3_ref, d1_ref, d2a_ref, d2b_ref, d2c_ref, d3_ref), refs = refs[:10], refs[10:]
     if summed:
-        (acc, core_buf, stat_dp, stat_mp, kern_send, kern_dp, kern_mp, core_sems, load_sem, sems, send_s, recv_s), bufs = refs[:12], refs[12:]
+        (acc, stat_dp, stat_mp, kern_send, kern_dp, kern_mp, load_sem, sems, send_s, recv_s), bufs = refs[:10], refs[10:]
         me = coordinates()
         stages = {}
         at = 0
         for f, flow in enumerate(SUM_FLOWS):
             for s in range(3):
-                stages[f, s] = (acc, flow, s, bufs[at], sems.at[0, at], sems.at[1, at])
+                stages[f, s] = (dw_ref if s == 0 else acc, flow, s, bufs[at], sems.at[0, at], sems.at[1, at])
                 at += 1
 
-        def core_copies():
-            other = {**me, "c": 1 - me["c"]}
-            return [
-                pltpu.make_async_remote_copy(
-                    dw_ref.at[h, :, 1 - me["c"]], core_buf.at[h], core_sems.at[0, h], core_sems.at[1, h], **device_at(other)
-                )
-                for h in range(2)
-            ]
-
         def loads():
-            return [pltpu.make_async_copy(dw_ref.at[h, :, me["c"]], acc.at[h], load_sem.at[h]) for h in range(2)]
+            return [pltpu.make_async_copy(dw_ref.at[h], acc.at[h], load_sem.at[h]) for h in range(2)]
 
         def stat_copies(axis, count, k):
             src = stat_ref if k == 0 else stat_mp.at[lax.axis_index("mp")]
@@ -403,45 +624,39 @@
             src = (lambda j: kern_send.at[ids[j]]) if k == 0 else (lambda _: kern_mp.at[lax.axis_index("mp")])
             return share(axis, count, src, (kern_dp, kern_mp)[k], send_s.at[2 + k], recv_s.at[2 + k])
 
-        def start(copies):
-            for copy in copies:
-                copy.start()
-
-        def finish(copies):
-            for copy in copies:
-                copy.wait()
-
         def first():
-            barrier = pltpu.get_barrier_semaphore()
-            ids = everyone("dp", 8) + everyone("mp", 4)
-            for to in ids:
-                pl.semaphore_signal(barrier, inc=1, **to)
-            pl.semaphore_wait(barrier, len(ids))
-            start(core_copies())
             start(loads())
+            greeted()
+            for f in (0, 1):
+                start(sum_copies(*stages[f, 0]))
             start(stat_copies("dp", 8, 0))
             stat_dp[lax.axis_index("dp")] = stat_ref[...]
 
-        def after_core():
+        def stats_over():
             finish(loads())
-            finish(core_copies())
-            for h in range(2):
-
-                def one(j, _):
-                    at = (h, j // 8, (j // 2) % 4, j % 2)
-                    acc[at] = (acc[at].astype(F32) + core_buf[at].astype(F32)).astype(BF16)
-                    return 0
-
-                lax.fori_loop(0, 16, one, 0)
-            for f in range(2):
-                start(sum_copies(*stages[f, 0]))
             finish(stat_copies("dp", 8, 0))
             stat_mp[lax.axis_index("mp")] = in_order(stat_dp, 8)
             start(stat_copies("mp", 4, 1))
 
+        def point(step, k):
+            todo = {
+                (0, 4): stats_over,
+                (1, 1): lambda: (next_stage(0, 0), next_stage(1, 0), [start(sum_copies(*stages[f, 0])) for f in (2, 3)]),
+                (2, 0): stats_done,
+                (2, 3): lambda: (next_stage(2, 0), next_stage(3, 0)),
+                (3, 3): lambda: (next_stage(2, 1), next_stage(3, 1)),
+                (4, 1): lambda: (next_stage(0, 1), next_stage(1, 1)),
+            }
+            todo = [(at, what) for (at, where), what in todo.items() if where == k]
+            for at, what in todo:
+
+                @pl.when(step == at)
+                def _():
+                    what()
+
         def next_stage(f, s):
             finish(sum_copies(*stages[f, s]))
-            add_arrived(*stages[f, s][:4], out=dsum_ref if s == 2 else None)
+            add_arrived(acc, *stages[f, s][1:4], out=dsum_ref if s == 2 else None)
             if s < 2:
                 start(sum_copies(*stages[f, s + 1]))
 
@@ -462,8 +677,7 @@
 
         def kernels_done():
             finish(kern_copies("mp", 4, 1))
-            total = in_order(kern_mp, 4) / stat_out[9:10, :]
-            unpack_kernels(total, c1_ref, c2_ref, c3_ref)
+            kern_out[...] = in_order(kern_mp, 4) / stat_out[9:10, :]
 
     i = pl.program_id(0)
     rows = y_ref.shape[2]
@@ -471,7 +685,9 @@
     @pl.when(i == 0)
     def _():
         if summed:
-            first()
+            greet()
+        b2_ref[...] = jnp.zeros_like(b2_ref)
+        b3_ref[...] = jnp.zeros_like(b3_ref)
         fill_band_two(k2_ref, b2_ref)
         fill_band_three(k3_ref, b3_ref)
         for at in (0, 1, 9, 10):
@@ -485,6 +701,8 @@
             if p % 2:
                 both = pltpu.roll(both, 448, 1)
             g3[p + 2] = jnp.where(lane < 448, both, 0.0).astype(BF16)
+        if summed:
+            first()
         for u in range(3):
             total = 0.0
             for m in range(2):
@@ -492,8 +710,6 @@
                 rhs = g3[2:9, :, 256 * m : 256 * m + 256].reshape(7 * rows, 256)
                 total = total + dot_tn(lhs, rhs)
             d3_ref[u] = total
-        if summed:
-            after_core()
         d1_ref[...] = jnp.zeros_like(d1_ref)
         d2a_ref[...] = jnp.zeros_like(d2a_ref)
         d2b_ref[...] = jnp.zeros_like(d2b_ref)
@@ -509,6 +725,8 @@
 
             lax.fori_loop(0, 9, one, 0)
 
+    if summed:
+        point(i, 0)
     for r in range(2):
         for t in range(2):
             for ref, lo, hi, n0, n1 in ((d2a_ref, 0, 384, 0, 256), (d2b_ref, 256, 640, 256, 512), (d2c_ref, 512, 768, 512, 640)):
@@ -521,6 +739,8 @@
         carry[...] = y0_ref[...]
 
     for j, (n0, n1) in enumerate(((0, 256), (128, 512), (384, 640))):
+        if summed:
+            point(i, 1 + j)
         grads = []
         for pp in range(4):
             r = pp % 2
@@ -535,30 +755,18 @@
             lhs = jnp.concatenate(pieces, axis=0)
             d1_ref[512 * t : 512 * t + 512, :] += dot_tn(lhs, grad)
     carry[...] = y_ref[3]
-
     if summed:
-
-        @pl.when(i == 2)
-        def _():
-            stats_done()
-            next_stage(0, 0)
-            next_stage(1, 0)
-
-        @pl.when(i == 3)
-        def _():
-            next_stage(1, 1)
+        point(i, 4)
 
     @pl.when(i == 4)
     def _():
-        if summed:
-            next_stage(0, 1)
         take_band_one(d1_ref, o1_ref)
         take_band_two(((d2a_ref, 0, 0, 4), (d2b_ref, 8, 4, 4), (d2c_ref, 16, 8, 1)), o2_ref)
         take_band_three(d3_ref, o3_ref)
         if summed:
             kernels_out()
-            next_stage(1, 2)
-            next_stage(0, 2)
+            for f in range(4):
+                next_stage(f, 2)
             kernels_over()
             kernels_done()
 
@@ -586,19 +794,18 @@
     params = {}
     if summed is not None:
         args += summed
+        block = (2, *AXES.values(), 16, HALF)
         in_specs += [pl.BlockSpec(memory_space=pl.ANY), once((16, 128))]
-        outs = [(2, 16, HALF), (16, 128), (32, 32), (64, 64), (72, 64)]
+        outs = [(2, 16, HALF), (16, 128), (80, 128)]
         buffers = flow_buffers(SUM_FLOWS)
         scratch = [pltpu.VMEM(s, F32) for s in own] + scratch
         scratch += [
-            pltpu.VMEM((2, *AXES.values(), 16, HALF), BF16),
-            pltpu.VMEM((2, *AXES.values(), 16, HALF), BF16),
+            pltpu.VMEM(block, BF16),
             pltpu.VMEM((8, 16, 128), F32),
             pltpu.VMEM((4, 16, 128), F32),
             pltpu.VMEM((8, 80, 128), BF16),
             pltpu.VMEM((8, 80, 128), BF16),
             pltpu.VMEM((4, 80, 128), F32),
-            pltpu.SemaphoreType.DMA((2, 2)),
             pltpu.SemaphoreType.DMA((2,)),
             pltpu.SemaphoreType.DMA((2, len(buffers), 3)),
             pltpu.SemaphoreType.DMA((4, 7)),
@@ -623,9 +830,26 @@
     return high, (v - high.astype(F32)).astype(BF16)
 
 
-def heads_kernel(
-    atoms, acts, f_ref, w_ref, bias_ref, slot_ref, col_ref, row_ref, dw_ref, fg_ref, prio_ref, stat_ref
-):
+def heads_kernel(atoms, acts, paired, f_ref, w_ref, bias_ref, slot_ref, row_ref, dw_out, fg_ref, prio_ref, stat_ref, *refs):
+    if paired:
+        dw_ref, arrived, send, recv = refs
+        me = coordinates()
+        other = device_at({**me, "c": 1 - me["c"]})
+        barrier = pltpu.get_barrier_semaphore()
+        pl.semaphore_signal(barrier, inc=1, **other)
+        pl.semaphore_wait(barrier, 1)
+        to_core = [
+            pltpu.make_async_remote_copy(dw_ref.at[h, :, 1 - me["c"]], arrived.at[h], send.at[h], recv.at[h], **other)
+            for h in range(2)
+        ]
+
+    def put(h, lo, hi, v):
+        v = v.astype(BF16)
+        if paired:
+            dw_ref[h, :, :, :, :, :, lo:hi] = v.reshape(2, 2, 4, 2, 16, hi - lo)
+        else:
+            dw_out[h, :, lo:hi] = v
+
     rows = f_ref.shape[0]
     slots = slot_ref.shape[0]
     feats = f_ref[...]
@@ -641,12 +865,13 @@
     zero = jnp.zeros((), BF16)
     w_val = jnp.where(lane[:, :128] < atoms, out_w[:, :128].astype(F32), 0.0).astype(BF16)
     w_adv = jnp.where(lane >= atoms, out_w.astype(F32), 0.0).astype(BF16)
-    logits = dot(hidden[1], w_adv) + bias_ref[...]
+    outs = bias_ref.shape[1]
+    bias = jnp.concatenate([bias_ref[...], jnp.zeros((1, wide - outs), F32)], axis=1)
+    logits = dot(hidden[1], w_adv) + bias
     logits = jnp.concatenate([logits[:, :128] + dot(hidden[0], w_val), logits[:, 128:]], axis=1)
     high, low = high_low(logits)
-    sel = jnp.where(lax.broadcasted_iota(jnp.int32, (slots, rows), 1) == col_ref[...], 1.0, 0.0).astype(BF16)
     selt = jnp.where(lax.broadcasted_iota(jnp.int32, (rows, slots), 0) == row_ref[...], 1.0, 0.0).astype(BF16)
-    per_slot = dot(sel, high) + dot(sel, low)
+    per_slot = dot_tn(selt, high) + dot_tn(selt, low)
     action = slot_ref[:, atoms + 2 : atoms + 3]
     which = jnp.where(lane < atoms, -1, jnp.where(lane < atoms * (acts + 1), (lane - atoms) // atoms, -2)).astype(F32)
     coeff = jnp.where(which == -1.0, 1.0, 0.0) + jnp.where(which == action, 1.0, 0.0) - jnp.where(which >= 0.0, 1.0 / acts, 0.0)
@@ -663,7 +888,7 @@
     cross = -jnp.sum(jnp.where(used, tgt * (q - top - jnp.log(total)), 0.0), axis=1, keepdims=True)
     coef = slot_ref[:, atoms : atoms + 1]
     valid = slot_ref[:, atoms + 1 : atoms + 2]
-    prio_ref[...] = valid * cross
+    prio_ref[...] = jnp.transpose(jnp.broadcast_to(valid * cross, (slots, 128)))[0:1]
     q_grad = coef * (shifted * (jnp.sum(tgt, axis=1, keepdims=True) / total) - tgt)
     high, low = high_low(q_grad)
     lgrad = ((dot(high, fold) + dot(low, fold)) * coeff).astype(BF16)
@@ -676,34 +901,97 @@
     grad = dot(selt, lgrad).astype(BF16)
     d_adv = dot_tn(hidden[1], grad)
     d_val = dot_tn(hidden[0], grad[:, :128])
-    dw_ref[0, :, 3200:3328] = jnp.where(lane[:, :128] < atoms, d_val, d_adv[:, :128]).astype(BF16)
-    dw_ref[0, :, 3328:] = d_adv[:, 128:512].astype(BF16)
-    dw_ref[1, :, 3200:] = d_adv[:, 512:].astype(BF16)
+    put(0, 3200, 3328, jnp.where(lane[:, :128] < atoms, d_val, d_adv[:, :128]))
+    put(0, 3328, HALF, d_adv[:, 128:512])
+    put(1, 3200, HALF, d_adv[:, 512:])
     pre_grad = [
         (dot_nt(grad[:, :128], w_val) * slope[0]).astype(BF16),
         (dot_nt(grad, w_adv) * slope[1]).astype(BF16),
     ]
     for k in range(2):
         for lo, hi in ((0, 1024), (1024, 2048), (2048, 3200)):
-            dw_ref[k, :, lo:hi] = dot_tn(pre_grad[k], f_ref[:, lo:hi]).astype(BF16)
+            put(k, lo, hi, dot_tn(pre_grad[k], f_ref[:, lo:hi]))
+        if paired:
+            to_core[k].start()
     for lo, hi in ((0, 1024), (1024, 2048), (2048, 3200)):
         back = dot(pre_grad[0], w_ref[0, :, lo:hi]) + dot(pre_grad[1], w_ref[1, :, lo:hi])
         fg_ref[:, lo:hi] = back.astype(BF16)
-
-
-def heads(atoms, acts, feats, weights, bias, per_slot, rows_of_slot):
+    if paired:
+        for h in range(2):
+            to_core[h].wait()
+
+            def one(j, _):
+                x, z, y = j // 8, (j // 2) % 4, j % 2
+                dw_out[h, x, z, y] = (dw_ref[h, x, me["c"], z, y].astype(F32) + arrived[h, x, z, y].astype(F32)).astype(BF16)
+                return 0
+
+            lax.fori_loop(0, 16, one, 0)
+
+
+def heads(atoms, acts, feats, weights, bias, per_slot, rows_of_slot, paired=False):
     slots = per_slot.shape[0]
+    block = (2, 2, 4, 2, 16, HALF)
+    scratch, params = [], {}
+    if paired:
+        scratch = [
+            pltpu.VMEM((2, 2, 2, 4, 2, 16, HALF), BF16),
+            pltpu.VMEM(block, BF16),
+            pltpu.SemaphoreType.DMA((2,)),
+            pltpu.SemaphoreType.DMA((2,)),
+        ]
+        params = dict(collective_id=3, has_side_effects=True)
     return pl.pallas_call(
-        functools.partial(heads_kernel, atoms, acts),
+        functools.partial(heads_kernel, atoms, acts, paired),
         out_shape=[
-            jax.ShapeDtypeStruct(weights.shape, BF16),
+            jax.ShapeDtypeStruct(block if paired else weights.shape, BF16),
             jax.ShapeDtypeStruct(feats.shape, BF16),
-            jax.ShapeDtypeStruct((slots, 1), F32),
+            jax.ShapeDtypeStruct((1, slots), F32),
             jax.ShapeDtypeStruct((16, 128), F32),
         ],
+        scratch_shapes=scratch,
+        compiler_params=pltpu.CompilerParams(vmem_limit_bytes=VMEM_LIMIT, **params),
+        name="heads",
+    )(feats, weights, bias, per_slot, rows_of_slot[None, :])
+
+
+def finish_kernel(
+    dsum, stat, kern, fn, hn, on, loss, g1, g2, g3t, mean_g, spread_g, bias_g, val_g, val_s, adv_g, adv_s, out_g
+):
+    feat, atoms, outs = fn.shape[1], val_g.shape[1], on.shape[1]
+    inverse = 1.0 / stat[9:10, 0:1]
+    loss[...] = stat[8:9, 0:1] * inverse
+    v = kern[...]
+    turned = pltpu.roll(v, 64, 1)
+    g2[0:32, :] = v[0:32, 0:64]
+    g2[32:64, :] = turned[0:32, 0:64]
+    third = jnp.concatenate([v[32:64], turned[32:64], v[64:72], jnp.zeros((56, 128), F32)], axis=0)
+    g3t[...] = jnp.transpose(third)[0:64, 0:72]
+    for k in range(4):
+        g1[8 * k : 8 * k + 8, :] = v[72:80, 32 * k : 32 * k + 32]
+    for h in range(2):
+        mean = dsum[h, :, 0:feat] * inverse
+        mean_g[h] = mean
+        spread_g[h] = mean * fn[h : h + 1, :] * as_column(hn[0, h : h + 1, :])
+        bias_g[h : h + 1, :] = as_row(dsum[h, :, feat : feat + 1] * inverse)
+    out = jnp.concatenate([dsum[0, :, 3200:], dsum[1, :, 3200:]], axis=1) * inverse
+    val, adv = out[:, :atoms], out[:, atoms:outs]
+    val_g[...] = val
+    val_s[...] = val * as_column(hn[1, 0:1, :]) * on[:, :atoms]
+    adv_g[...] = adv
+    adv_s[...] = adv * as_column(hn[1, 1:2, :]) * on[:, atoms:]
+    out_g[...] = jnp.concatenate([stat[k : k + 1, :] for k in range(8)], axis=1)[:, :outs] * inverse
+
+
+def outputs(dsum, stat, kern, fn, hn, on, atoms):
+    feat, outs = fn.shape[1], on.shape[1]
+    shapes = [(1, 1), (32, 32), (64, 64), (64, 72), (2, 16, feat), (2, 16, feat), (2, 16)]
+    shapes += [(16, atoms)] * 2 + [(16, outs - atoms)] * 2 + [(1, outs)]
+    return pl.pallas_call(
+        finish_kernel,
+        out_shape=[jax.ShapeDtypeStruct(s, F32) for s in shapes],
         compiler_params=pltpu.CompilerParams(vmem_limit_bytes=VMEM_LIMIT),
-        name="heads",
-    )(feats, weights, bias, per_slot, rows_of_slot[:, None], rows_of_slot[None, :])
+        name="outputs",
+    )(dsum, stat, kern, fn, hn, on)
 
 
 def exchange_kernel(count, kern_ref, slot_ref, kerns_out, slots_out, send_kern, recv_kern, send_slot, recv_slot, own):
@@ -736,7 +1024,7 @@
         out_specs=[pl.BlockSpec(memory_space=pltpu.VMEM)] * 2,
         out_shape=[jax.ShapeDtypeStruct((count, *kern.shape), kern.dtype), jax.ShapeDtypeStruct(slot.shape, slot.dtype)],
         scratch_shapes=[pltpu.SemaphoreType.DMA((count,))] * 4 + [pltpu.SemaphoreType.DMA((2,))],
-        compiler_params=pltpu.CompilerParams(collective_id=0, has_side_effects=True, vmem_limit_bytes=VMEM_LIMIT),
+        compiler_params=pltpu.CompilerParams(collective_id=2, has_side_effects=True, vmem_limit_bytes=VMEM_LIMIT),
         name="exchange",
     )(kern, slot)
 
@@ -772,6 +1060,38 @@
     feat, own = hidden_mean.shape[1:]
     outs = atoms * (acts + 1)
 
+    x = frames.transpose(1, 0, 2).reshape(21, 4, rows, 336)
+    bias = output_bias[None, :]
+    mean_t = hidden_mean.transpose(0, 2, 1)
+    spread_t = hidden_spread.transpose(0, 2, 1)
+
+    if (dp_count, lax.axis_size("mp"), own, slots) == (8, 4, 16, 512):
+        noise = output_noise[None, :]
+        shared = [mean_t, spread_t, hidden_bias, feature_noise, hidden_noise]
+        shared += [value_mean, value_spread, advantage_mean, advantage_spread, noise]
+        shared += [target_dist.T, recv_counts[None, :], actions[None, :], sample_weight[None, :]]
+        kernels = [conv_first, conv_second, conv_third.T]
+        a1, s1, a2, s2, feats, s3, y, y0, weights, per_slot, kern2, kern3 = torso_forward(x, kernels, shared)
+        weights, per_slot = weights.reshape(2, 512, HALF), per_slot.reshape(slots, 128)
+        dweights, feat_grad, prio, stat = heads(atoms, acts, feats, weights, bias, per_slot, send_rows, paired=True)
+        summed = [dweights, stat]
+        summed = torso_backward(y, y0, a1, s1, a2, s2, s3, feat_grad, kern2, kern3, summed=summed)
+        loss, g1, g2, g3t, mean_g, spread_g, bias_g, *outer, out_g = outputs(
+            *summed, feature_noise, hidden_noise, noise, atoms
+        )
+        return (
+            loss[0, 0],
+            g1,
+            g2,
+            g3t.T,
+            mean_g.transpose(0, 2, 1),
+            spread_g.transpose(0, 2, 1),
+            bias_g,
+            *outer,
+            out_g[0],
+            prio[0],
+        )
+
     sizes = [w.size for w in (conv_first, conv_second, conv_third)]
     flat = jnp.concatenate([w.astype(BF16).reshape(-1) for w in (conv_first, conv_second, conv_third)])
     tall = -(-flat.size // 2048) * 16
@@ -787,8 +1107,6 @@
     kern2 = jnp.tile(flat[:, sizes[0] : sizes[0] + sizes[1]].reshape(-1, 64), (1, 2))
     kern3 = jnp.tile(flat[:, sizes[0] + sizes[1] : sum(sizes)].reshape(-1, 64), (1, 2))
 
-    mean_t = hidden_mean.transpose(0, 2, 1)
-    spread_t = hidden_spread.transpose(0, 2, 1)
     wide_one = mean_t + spread_t * feature_noise[:, None, :] * hidden_noise[0][:, :, None]
     wide_one = jnp.concatenate([wide_one, hidden_bias[:, :, None], jnp.zeros((2, own, 63), F32)], axis=2)
     wide_val = value_mean + value_spread * hidden_noise[1, 0][:, None] * output_noise[None, :atoms]
@@ -798,28 +1116,19 @@
     shard = jnp.concatenate([wide_one, wide_out], axis=2).astype(BF16)
     weights = lax.all_gather(shard, ("mp", "dp"), axis=1, tiled=True)
 
-    x = frames.transpose(1, 0, 2).reshape(21, 4, rows, 336)
-    a1, s1, a2, s2, feats, s3, y, y0 = torso_forward(x, kern1, kern2, kern3)
-    bias = jnp.pad(output_bias, (0, 1024 - outs))[None, :]
+    a1, s1, a2, s2, feats, s3, y, y0 = torso_forward(x, [kern1, kern2, kern3])
     dweights, feat_grad, prio, stat = heads(atoms, acts, feats, weights, bias, per_slot, send_rows)
-    torso = (y, y0, a1, s1, a2, s2, s3, feat_grad, kern2, kern3)
-    if (dp_count, lax.axis_size("mp"), own) == (8, 4, 16):
-        summed = [dweights.reshape(2, 2, 2, 4, 2, own, HALF), stat]
-        dshard, stat, *conv_grads = torso_backward(*torso, summed=summed)
-        inverse = 1.0 / stat[9, 0]
-    else:
-        dshard = lax.psum_scatter(dweights, ("mp", "dp"), scatter_dimension=1, tiled=True).astype(F32)
-        stat = lax.psum(stat, ("dp", "mp"))
-        inverse = 1.0 / stat[9, 0]
-        k1, k2, k3 = torso_backward(*torso)
-        kflat = jnp.concatenate([g.reshape(dp_count, -1) for g in (k1[:, :32], k2[:, :64], k3[:, :64])], axis=1)
-        kflat = lax.psum(lax.psum_scatter(kflat, "dp", scatter_dimension=0, tiled=True)[0], "mp") * inverse
-        conv_grads = (
-            kflat[: sizes[0]].reshape(conv_first.shape),
-            kflat[sizes[0] : sizes[0] + sizes[1]].reshape(conv_second.shape),
-            kflat[sizes[0] + sizes[1] :].reshape(conv_third.shape),
-        )
-
+    dshard = lax.psum_scatter(dweights, ("mp", "dp"), scatter_dimension=1, tiled=True).astype(F32)
+    stat = lax.psum(stat, ("dp", "mp"))
+    inverse = 1.0 / stat[9, 0]
+    k1, k2, k3 = torso_backward(y, y0, a1, s1, a2, s2, s3, feat_grad, kern2, kern3)
+    kflat = jnp.concatenate([g.reshape(dp_count, -1) for g in (k1[:, :32], k2[:, :64], k3[:, :64])], axis=1)
+    kflat = lax.psum(lax.psum_scatter(kflat, "dp", scatter_dimension=0, tiled=True)[0], "mp") * inverse
+    conv_grads = (
+        kflat[: sizes[0]].reshape(conv_first.shape),
+        kflat[sizes[0] : sizes[0] + sizes[1]].reshape(conv_second.shape),
+        kflat[sizes[0] + sizes[1] :].reshape(conv_third.shape),
+    )
     dshard = dshard * inverse
     mean_grad_t = dshard[:, :, :feat]
     spread_grad_t = mean_grad_t * feature_noise[:, None, :] * hidden_noise[0][:, :, None]
@@ -837,7 +1146,7 @@
         adv_mean_grad,
         adv_mean_grad * hidden_noise[1, 1][:, None] * output_noise[None, atoms:],
         stat[:8].reshape(-1)[:outs] * inverse,
-        prio[:, 0],
+        prio[0],
     )
 
 

time: 221 us -> 166 us (0.75)
  local copies, waits for them, and re-layouts: 20.5 us -> 0.58 us
  between operations: 16.7 us -> 0.69 us
  other arithmetic: 14.2 us -> 0 us
  waiting for transfers between devices: 14 us -> 0 us
  Pallas kernels: 155 us -> 164 us
    pallas_call x3, Pallas kernels: 71.8 us -> 93.1 us  [the longest x1 68 us: torso_forward(): pl.pallas_call(functools.partial(forward_kernel, shared is not None), gri...]
    all_gather x1 -> x0, waiting for transfers between devices: 14 us -> none  [on_device(): weights = lax.all_gather(shard, ('mp', 'dp'), axis=1, tiled=True)]
    pallas_call x1, Pallas kernels: 82.7 us -> 71.4 us  [torso_backward(): pl.pallas_call(functools.partial(backward_kernel, summed is not None), gr...]
    unnamed x10 -> x3, local copies, waits for them, and re-layouts: 6.17 us -> 0.58 us
    mul x5 -> x0, other arithmetic: 3.75 us -> none  [the longest x1 1.06 us: on_device(): dshard = dshard * inverse]
    convert_element_type x5 -> x0, other arithmetic: 3.66 us -> none  [the longest x3 2.24 us: on_device(): w.astype(BF16).reshape(-1)]
    slice x7 -> x0, local copies, waits for them, and re-layouts: 3.45 us -> none  [the longest x1 1.27 us: on_device(): inverse = 1.0 / stat[9, 0]]
    another operation x12 -> x0, local copies, waits for them, and re-layouts: 3.06 us -> none  [the longest x4 1.07 us: on_device(): jnp.tile(flat[:, sizes[0] + sizes[1]:sum(sizes)].reshape(-1, 64), (1, 2))]
  transfers between devices with their start and end apart: 1 -> 0, of which waited for: 1 -> 0; matrix products, arithmetic and copies ran while one was open for 7% -> 0% of each run, Pallas kernels for 24% -> 0%
where the time goes in v3:
time: 166 us
  Pallas kernels  164 us (99%)
    pallas_call x1, Pallas kernels, torso_backward(): pl.pallas_call(functools.partial(backward_kernel, summed is not None), gr...  71.4 us
    pallas_call x1, Pallas kernels, torso_forward(): pl.pallas_call(functools.partial(forward_kernel, shared is not None), gri...  68 us
    pallas_call x1, Pallas kernels, heads(): pl.pallas_call(functools.partial(heads_kernel, atoms, acts, paired), out_...  22.8 us

profile of v3, /device:TPU:0, one launch (start us, length us, event | category | flops | bytes accessed | tf_op | source)
XLA Modules:
  0.0 165.7 jit_solution(13096985430091132848)
XLA Ops:
  0.7 68.0 %torso_forward.1 = (bf16[10,2,272,768]{3,2,1,0:T(8,128)(2,1)}, bf16[10,2,272,768]{3,2,1,0:T(8,128)(2,1)}, bf16[9,272,640]{2,1,0:T(8,128)(2,1)}, bf16[9,272,640]{...) custom-call(bf16[21,4,272,336]{3,2,1,0:T(8,128)(2,1)} %bitcast.21, ...), custom_call_target="tpu_custom_call" | custom-call | tf_op jit(solution)/shard_map/torso_forward/pallas_call | solution.py:572
  68.7 22.8 %heads.1 = (bf16[2,2,4,2,16,3712]{5,4,3,2,1,0:T(8,128)(2,1)}, bf16[272,3200]{1,0:T(8,128)(2,1)}, f32[1,512]{1,0:T(1,128)}, f32[16,128]{1,0:T(8,128)}) custom-call(bf16[272,3200]{1,0:T(8,128)(2,1)} %get-tuple-element.51.f_ref, bf16[2,512,3712]{2,1,0:T(8,128)(2,1)} %bitcast.23, f32[1,969]{1,0:T(1,128)} %bitcast.31, f32[512,128]{1,0:T(8,128)} %bitcast.26, ...), custom_call_target="tpu_custom_call" | custom-call | tf_op jit(solution)/shard_map/heads/pallas_call | solution.py:943
  91.5 0.0 copy-start
  91.5 71.4 %torso_backward.1 = (f32[2,16,3712]{2,1,0:T(8,128)}, f32[16,128]{1,0:T(8,128)}, f32[80,128]{1,0:T(8,128)}) custom-call(bf16[20,3,272,512]{3,2,1,0:T(8,128)(2,1)} %get-tuple-element.44.refs_0_, bf16[3,272,512]{2,1,0:T(8,128)(2,1)} %get-tuple-element.45.refs_1_, bf16[10,2,272,768]{3,2,1,0:T(8,128)(2,1)} %get-tuple-element.46.refs_2_, ...), custom_call_target="tpu_custom_call" | custom-call | tf_op jit(solution)/shard_map/torso_backward/pallas_call | solution.py:816
  162.9 2.2 %outputs.1 = (f32[1,1]{1,0:T(1,128)}, f32[32,32]{1,0:T(8,128)}, f32[64,64]{1,0:T(8,128)}, f32[64,72]{1,0:T(8,128)}, f32[2,16,3136]{2,1,0:T(8,128)}, /*index=5*/f...) custom-call(f32[2,16,3712]{2,1,0:T(8,128)} %get-tuple-element.59.dsu, ...), custom_call_target="tpu_custom_call" | custom-call | tf_op jit(solution)/shard_map/outputs/pallas_call | solution.py:989
  165.1 0.0 copy-done
  165.1 0.6 copy.34
Async XLA Ops:
  91.5 73.6 %copy-start = (f32[1,512]{1,0:T(1,128)S(1)}, f32[1,512]{1,0:T(1,128)}, u32[]{:S(2)}) copy-start(f32[1,512]{1,0:T(1,128)} %get-tuple-element.74) | copy-start | bytes 6148

commit v4 on v3

--- a/solution.py
+++ b/solution.py
@@ -146,10 +146,17 @@
 
 AXES = {"x": 2, "z": 4, "y": 2}
 HALF = 3712
-CUT = 1536
-SUM_FLOWS = [(0, 0, CUT, "xzy"), (1, 0, CUT, "yzx"), (0, CUT, HALF, "xyz"), (1, CUT, HALF, "yxz")]
-GATHER_FLOWS = [(half, lo, hi, order[::-1]) for half, lo, hi, order in SUM_FLOWS]
-
+CUTS = [(0, 1408, "zyx", "zxy"), (1408, 2816, "zyx", "zxy"), (2816, HALF, "xyz", "yxz")]
+GATHER_FLOWS = [(half, lo, hi, orders[half]) for lo, hi, *orders in CUTS for half in range(2)]
+SUM_FLOWS = [(half, lo, hi, order[::-1]) for half, lo, hi, order in GATHER_FLOWS]
+GATHER_FIRST = [(4, 0), (5, 0), (0, 0)]
+GATHER_PLAN = {(0, 0): [(4, 1), (5, 1), (1, 0), (0, 1)], (0, 1): [(2, 0)], (0, 3): [(1, 1)], (1, 0): [(3, 0)], (1, 3): [(2, 1), (0, 2)], (1, 5): [(4, 2)], (2, 1): [(1, 2)], (3, 0): [(3, 1)], (3, 4): [(5, 2)], (3, 5): [(2, 2)], (4, 1): [(3, 2)]}
+GATHER_LAST = []
+GATHER_DONE = [0, 4, 1, 2, 5, 3]
+SUM_FIRST = [(0, 0), (1, 0), (4, 0)]
+SUM_PLAN = {(0, 2): [(2, 0), (3, 0)], (0, 4): [(5, 0)], (1, 4): [(0, 1), (1, 1)], (2, 0): [(2, 1), (3, 1)], (2, 4): [(0, 2)], (2, 5): [(4, 1), (5, 1)], (2, 6): [(1, 2)], (3, 2): [(4, 2), (5, 2)], (3, 5): [(2, 2)], (4, 2): [(3, 2)]}
+SUM_LAST = []
+SUM_DONE = [0, 4, 5, 1, 2, 3]
 
 def flow_buffers(flows):
     shapes = []
@@ -185,6 +192,9 @@
     half, lo, hi, order = flow
     me = coordinates()
     own = block_of(acc, half, lo, hi, {a: me[a] for a in order[: stage + 1]})
+    if out is None and AXES[order[stage]] == 2:
+        own[...] = own[...] + buf[0]
+        return
     total = own[...].astype(F32)
     for k in range(AXES[order[stage]] - 1):
         total = total + buf[k].astype(F32)
@@ -231,13 +241,15 @@
     ]
 
 
-def core_copy(out, flow, last, send, recv):
+def core_copies(out, flow, last, send, recv):
     half, lo, hi, order = flow
     me = coordinates()
-    axis = order[2]
-    block = gathered_block(out, half, lo, hi, me["c"], {axis: 1 - me[axis] if last else me[axis]})
     other = {**me, "c": 1 - me["c"]}
-    return pltpu.make_async_remote_copy(block, block, send, recv, **device_at(other))
+    copies = []
+    for k, at in enumerate([peer[order[2]] for peer in peers_of(order[2])] if last else [me[order[2]]]):
+        block = gathered_block(out, half, lo, hi, me["c"], {order[2]: at})
+        copies.append(pltpu.make_async_remote_copy(block, block, send.at[k], recv.at[k], **device_at(other)))
+    return copies
 
 
 def start(copies):
@@ -348,10 +360,11 @@
         (sw,), refs = refs[:1], refs[1:]
     else:
         (x_ref, xn_ref, k1_ref, k2_ref, k3_ref), refs = refs[:5], refs[5:]
-    (a1_ref, s1_ref, a2_ref, s2_ref, f_ref, s3_ref, y_ref, y0_ref), refs = refs[:8], refs[8:]
+    (a1_ref, s1_ref, *whole_out, y_ref, y0_ref), refs = refs[:8], refs[8:]
     if shared:
         (w_out, slot_out, k2_ref, k3_ref), refs = refs[:4], refs[4:]
-    (carry, a1s, b1_ref, b2_ref, b3_ref), refs = refs[:5], refs[5:]
+    (carry, a1s, b1_ref, b2_ref, b3_ref, *whole, whole_sem), refs = refs[:10], refs[10:]
+    a2_ref, s2_ref, f_ref, s3_ref = whole
     i = pl.program_id(0)
     rows = x_ref.shape[2]
     if shared:
@@ -377,7 +390,7 @@
             ]
 
         def to_core(f, last):
-            return core_copy(w_out, GATHER_FLOWS[f], last, core_sems.at[0, f, last], core_sems.at[1, f, last])
+            return core_copies(w_out, GATHER_FLOWS[f], last, core_sems.at[0, f, last], core_sems.at[1, f, last])
 
         def begin():
             greet()
@@ -390,45 +403,49 @@
             slot_buf[lax.axis_index("dp")] = slot_src[lax.axis_index("dp")]
             greeted()
             start(kern_copies())
-            for f in range(4):
-                start(gather_copies(*flow_stage[f, 0]))
+            for f, s in GATHER_FIRST:
+                enter(f, s)
             start(own_copies())
             prepare()
+            finish(own_copies())
             finish(kern_copies())
             for d in range(8):
                 unpack_shards(d, kern_buf[d].astype(F32), k1_ref, k2_ref, k3_ref)
 
-        def advance(f, s):
-            finish(gather_copies(*flow_stage[f, s]))
-            start(gather_copies(*flow_stage[f, s + 1]))
+        def enter(f, s):
+            if s > 0:
+                finish(gather_copies(*flow_stage[f, s - 1]))
+            start(gather_copies(*flow_stage[f, s]))
+            if s == 2:
+                start(to_core(f, 0))
 
         def point(step, k):
-            todo = []
-            if k == 1:
-                todo = [
-                    (1, lambda: (finish(own_copies()), [advance(f, 0) for f in (2, 3, 0, 1)])),
-                    (3, lambda: [(advance(f, 1), to_core(f, 0).start()) for f in (2, 3)]),
-                ]
-            elif k == 2:
-                todo = [
-                    (4, lambda: ([(advance(f, 1), to_core(f, 0).start()) for f in (0, 1)], start(slot_copies()))),
-                ]
-            for at, what in todo:
-
-                @pl.when(step == at)
+            for (at, where), entries in GATHER_PLAN.items():
+                if where == k:
+
+                    @pl.when(step == at)
+                    def _():
+                        for f, s in entries:
+                            enter(f, s)
+
+            if k == 0:
+
+                @pl.when(step == 4)
                 def _():
-                    what()
+                    start(slot_copies())
 
         def end():
-            for f in (2, 3, 0, 1):
+            for f, s in GATHER_LAST:
+                enter(f, s)
+            for f in GATHER_DONE:
                 finish(gather_copies(*flow_stage[f, 2]))
-                to_core(f, 1).start()
+                start(to_core(f, 1))
             finish(slot_copies())
             slot_out[:, 0:32] = slot_buf[...]
             slot_out[:, 32:64] = pltpu.roll(slot_buf[...].reshape(256, 128), 64, 1).reshape(8, 32, 128)
-            for f in range(4):
+            for f in GATHER_DONE:
                 for last in range(2):
-                    to_core(f, last).wait()
+                    finish(to_core(f, last))
 
     def prepare():
         b2_ref[...] = jnp.zeros_like(b2_ref)
@@ -460,11 +477,9 @@
             a1_ref[pp // 2, pp % 2, :, 256 * j : 256 * j + 256] = act
             a1s[2 * i + pp // 2, pp % 2, :, 256 * j : 256 * j + 256] = act
             s1_ref[pp // 2, pp % 2, :, 256 * j : 256 * j + 256] = slope.astype(BF16)
-        if shared and pp == 1:
-            point(i, 1)
+        if shared:
+            point(i, pp)
     carry[...] = y_ref[3]
-    if shared:
-        point(i, 2)
 
     def second(p):
         for lo, hi, n0, n1 in ((0, 384, 0, 256), (256, 640, 256, 512), (512, 768, 512, 640)):
@@ -499,11 +514,18 @@
     def _():
         second(2 * i - 1)
 
+    if shared:
+        point(i, 4)
     second(2 * i)
+    if shared:
+        point(i, 5)
 
     @pl.when(i >= 2)
     def _():
         third(2 * i - 3, True)
+
+    if shared:
+        point(i, 6)
 
     @pl.when(i >= 1)
     def _():
@@ -514,8 +536,11 @@
         lane = lax.broadcasted_iota(jnp.int32, (rows, 128), 1)
         last = f_ref[:, 3072:3200].astype(F32)
         f_ref[:, 3072:3200] = jnp.where(lane == 64, 1.0, last).astype(BF16)
+        leaving = [pltpu.make_async_copy(whole[k], whole_out[k], whole_sem.at[k]) for k in range(4)]
+        start(leaving)
         if shared:
             end()
+        finish(leaving)
 
 
 def full(shape):
@@ -535,8 +560,7 @@
     args = [x, x, *kernels]
     out_specs = (
         [pl.BlockSpec((2, 2, rows, 768), lambda i: (i, 0, 0, 0))] * 2
-        + [once((9, rows, 640))] * 2
-        + [once((rows, 3200))] * 2
+        + [pl.BlockSpec(memory_space=pl.ANY)] * 4
         + [pl.BlockSpec((4, 3, rows, 512), lambda i: (i, 0, 0, 0)), once((3, rows, 512))]
     )
     out_shape = [jax.ShapeDtypeStruct(s, BF16) for s in shapes]
@@ -544,6 +568,8 @@
         pltpu.VMEM((3, rows, 512), BF16),
         pltpu.VMEM((10, 2, rows, 768), BF16),
         *[pltpu.VMEM(s, BF16) for s in BANDS],
+        *[pltpu.VMEM(s, BF16) for s in shapes[2:6]],
+        pltpu.SemaphoreType.DMA((4,)),
     ]
     params = {}
     if shared is not None:
@@ -565,8 +591,8 @@
             pltpu.VMEM((8, 32, 128), F32),
             *[pltpu.SemaphoreType.DMA((7,))] * 4,
             pltpu.SemaphoreType.DMA((2,)),
-            pltpu.SemaphoreType.DMA((2, 4, 3, 3)),
-            pltpu.SemaphoreType.DMA((2, 4, 2)),
+            pltpu.SemaphoreType.DMA((2, len(GATHER_FLOWS), 3, 3)),
+            pltpu.SemaphoreType.DMA((2, len(GATHER_FLOWS), 2, 3)),
         ]
         params = dict(collective_id=0, has_side_effects=True)
     return pl.pallas_call(
@@ -596,12 +622,17 @@
     return jnp.concatenate([two, three, o3[72 * d + 64 : 72 * d + 72, :], one], axis=0)
 
 
+BACK_LANES = ((0, 256), (128, 512), (384, 640))
+
+
 def backward_kernel(summed, *refs):
-    (y_ref, y0_ref, a1_ref, s1_ref, a2_ref, s2_ref, s3_ref, fg_ref, k2_ref, k3_ref), refs = refs[:10], refs[10:]
+    (y_ref, a1_ref, s1_ref, *whole_in, k2_ref, k3_ref), refs = refs[:10], refs[10:]
     if summed:
         (dw_ref, stat_ref, dsum_ref, stat_out, kern_out), refs = refs[:5], refs[5:]
     (o1_ref, o2_ref, o3_ref), refs = refs[:3], refs[3:]
-    (carry, g3, g2, b2_ref, b3_ref, d1_ref, d2a_ref, d2b_ref, d2c_ref, d3_ref), refs = refs[:10], refs[10:]
+    (carry, *whole, whole_sem, back, grad, g3, g2, b2_ref, b3_ref, d1_ref, d2a_ref, d2b_ref, d2c_ref, d3_ref), refs = refs[:17], refs[17:]
+    a2_ref, s2_ref, s3_ref, fg_ref = whole
+    coming = [pltpu.make_async_copy(whole_in[k], (carry, *whole)[k], whole_sem.at[k]) for k in range(5)]
     if summed:
         (acc, stat_dp, stat_mp, kern_send, kern_dp, kern_mp, load_sem, sems, send_s, recv_s), bufs = refs[:10], refs[10:]
         me = coordinates()
@@ -612,8 +643,12 @@
                 stages[f, s] = (dw_ref if s == 0 else acc, flow, s, bufs[at], sems.at[0, at], sems.at[1, at])
                 at += 1
 
-        def loads():
-            return [pltpu.make_async_copy(dw_ref.at[h], acc.at[h], load_sem.at[h]) for h in range(2)]
+        loaded = {
+            f: pltpu.make_async_copy(
+                dw_ref.at[half, :, :, :, :, lo:hi], acc.at[half, :, :, :, :, lo:hi], load_sem.at[f]
+            )
+            for f, (half, lo, hi, _) in enumerate(SUM_FLOWS)
+        }
 
         def stat_copies(axis, count, k):
             src = stat_ref if k == 0 else stat_mp.at[lax.axis_index("mp")]
@@ -625,40 +660,44 @@
             return share(axis, count, src, (kern_dp, kern_mp)[k], send_s.at[2 + k], recv_s.at[2 + k])
 
         def first():
-            start(loads())
+            start(list(loaded.values()))
             greeted()
-            for f in (0, 1):
-                start(sum_copies(*stages[f, 0]))
+            for f, s in SUM_FIRST:
+                enter(f, s)
             start(stat_copies("dp", 8, 0))
             stat_dp[lax.axis_index("dp")] = stat_ref[...]
 
         def stats_over():
-            finish(loads())
             finish(stat_copies("dp", 8, 0))
             stat_mp[lax.axis_index("mp")] = in_order(stat_dp, 8)
             start(stat_copies("mp", 4, 1))
 
-        def point(step, k):
-            todo = {
-                (0, 4): stats_over,
-                (1, 1): lambda: (next_stage(0, 0), next_stage(1, 0), [start(sum_copies(*stages[f, 0])) for f in (2, 3)]),
-                (2, 0): stats_done,
-                (2, 3): lambda: (next_stage(2, 0), next_stage(3, 0)),
-                (3, 3): lambda: (next_stage(2, 1), next_stage(3, 1)),
-                (4, 1): lambda: (next_stage(0, 1), next_stage(1, 1)),
-            }
-            todo = [(at, what) for (at, where), what in todo.items() if where == k]
-            for at, what in todo:
-
-                @pl.when(step == at)
-                def _():
-                    what()
-
-        def next_stage(f, s):
+        def enter(f, s):
+            if s > 0:
+                leave(f, s - 1)
+            start(sum_copies(*stages[f, s]))
+
+        def leave(f, s):
+            if s == 0:
+                finish([loaded[f]])
             finish(sum_copies(*stages[f, s]))
             add_arrived(acc, *stages[f, s][1:4], out=dsum_ref if s == 2 else None)
-            if s < 2:
-                start(sum_copies(*stages[f, s + 1]))
+
+        def point(step, k):
+            for (at, where), entries in SUM_PLAN.items():
+                if where == k:
+
+                    @pl.when(step == at)
+                    def _():
+                        for f, s in entries:
+                            enter(f, s)
+
+            for at, where, what in ((0, 5, stats_over), (1, 6, stats_done)):
+                if where == k:
+
+                    @pl.when(step == at)
+                    def _():
+                        what()
 
         def stats_done():
             finish(stat_copies("mp", 4, 1))
@@ -686,10 +725,18 @@
     def _():
         if summed:
             greet()
+        start(coming[::-1])
         b2_ref[...] = jnp.zeros_like(b2_ref)
         b3_ref[...] = jnp.zeros_like(b3_ref)
         fill_band_two(k2_ref, b2_ref)
         fill_band_three(k3_ref, b3_ref)
+        for r in range(2):
+            for j, (n0, n1) in enumerate(BACK_LANES):
+                for t in range(2):
+                    turned = jnp.transpose(b2_ref[2 * t + r, 256 * j : 256 * j + 256, n0:n1].astype(F32))
+                    back[j, r, t * (n1 - n0) : (t + 1) * (n1 - n0), :] = turned.astype(BF16)
+        grad[3] = jnp.zeros(grad.shape[1:], BF16)
+        finish(coming[3:])
         for at in (0, 1, 9, 10):
             g3[at] = jnp.zeros((rows, 512), BF16)
         for at in (0, 10):
@@ -703,6 +750,8 @@
             g3[p + 2] = jnp.where(lane < 448, both, 0.0).astype(BF16)
         if summed:
             first()
+            point(i, "a0")
+        finish([coming[1]])
         for u in range(3):
             total = 0.0
             for m in range(2):
@@ -710,53 +759,57 @@
                 rhs = g3[2:9, :, 256 * m : 256 * m + 256].reshape(7 * rows, 256)
                 total = total + dot_tn(lhs, rhs)
             d3_ref[u] = total
+            if summed:
+                point(i, "a%d" % (1 + u))
         d1_ref[...] = jnp.zeros_like(d1_ref)
         d2a_ref[...] = jnp.zeros_like(d2a_ref)
         d2b_ref[...] = jnp.zeros_like(d2b_ref)
         d2c_ref[...] = jnp.zeros_like(d2c_ref)
-        for lo, hi, n0, n1 in ((0, 256, 0, 256), (256, 512, 128, 512), (512, 640, 384, 512)):
+        for at, (lo, hi, n0, n1) in enumerate(((0, 256, 0, 256), (256, 512, 128, 512), (512, 640, 384, 512))):
             rhs = jnp.concatenate([b3_ref[u, lo:hi, n0:n1] for u in range(3)], axis=1)
-
-            def one(p, _):
-                lhs = jnp.concatenate([g3[p + 2 - u, :, n0:n1] for u in range(3)], axis=1)
-                back = dot_nt(lhs, rhs) * s2_ref[p, :, lo:hi].astype(F32)
-                g2[p + 1, :, lo:hi] = back.astype(BF16)
-                return 0
-
-            lax.fori_loop(0, 9, one, 0)
-
-    if summed:
-        point(i, 0)
+            if at == 0:
+                finish([coming[0], coming[2]])
+            for p in (0, 3, 6):
+                lhs = jnp.concatenate([g3[p + 2 - u : p + 5 - u, :, n0:n1].reshape(3 * rows, n1 - n0) for u in range(3)], axis=1)
+                product = dot_nt(lhs, rhs) * s2_ref[p : p + 3, :, lo:hi].reshape(3 * rows, hi - lo).astype(F32)
+                g2[p + 1 : p + 4, :, lo:hi] = product.astype(BF16).reshape(3, rows, hi - lo)
+            if summed:
+                point(i, "a%d" % (4 + at))
+
     for r in range(2):
-        for t in range(2):
-            for ref, lo, hi, n0, n1 in ((d2a_ref, 0, 384, 0, 256), (d2b_ref, 256, 640, 256, 512), (d2c_ref, 512, 768, 512, 640)):
-                lhs = a1_ref[:, r, :, lo:hi].reshape(2 * rows, hi - lo)
-                rhs = g2[pl.ds(2 * i + 1 - t, 2), :, n0:n1].reshape(2 * rows, n1 - n0)
-                ref[2 * t + r] += dot_tn(lhs, rhs)
-
-    @pl.when(i == 0)
+        for ref, lo, hi, n0, n1 in ((d2a_ref, 0, 384, 0, 256), (d2b_ref, 256, 640, 256, 512), (d2c_ref, 512, 768, 512, 640)):
+            lhs = a1_ref[:, r, :, lo:hi].reshape(2 * rows, hi - lo)
+            rhs = [g2[pl.ds(2 * i + 1 - t, 2), :, n0:n1].reshape(2 * rows, n1 - n0) for t in range(2)]
+            both = dot_tn(lhs, jnp.concatenate(rhs, axis=1))
+            for t in range(2):
+                ref[2 * t + r] += both[:, t * (n1 - n0) : (t + 1) * (n1 - n0)]
+        if summed:
+            point(i, 2 * r)
+            point(i, 2 * r + 1)
+
+    for j, (n0, n1) in enumerate(BACK_LANES):
+        lanes = slice(256 * j, 256 * j + 256)
+        before = grad[3, :, lanes]
+        for r in range(2):
+            lhs = [g2[pl.ds(2 * i + 1 - t, 2), :, n0:n1].reshape(2 * rows, n1 - n0) for t in range(2)]
+            product = dot(jnp.concatenate(lhs, axis=1), back[j, r, : 2 * (n1 - n0), :])
+            for k in range(2):
+                slope = s1_ref[k, r, :, lanes].astype(F32)
+                grad[2 * k + r, :, lanes] = (product[k * rows : (k + 1) * rows] * slope).astype(BF16)
+        now = [grad[k, :, lanes] for k in range(4)]
+        rhs = jnp.concatenate([jnp.concatenate(now, axis=0), jnp.concatenate([before, *now[:3]], axis=0)], axis=1)
+        lhs = jnp.concatenate([carry[j], *[y_ref[k, j] for k in range(3)]], axis=0)
+        both = dot_tn(lhs, rhs)
+        d1_ref[0:512, :] += both[:, 0:256]
+        d1_ref[512:1024, :] += both[:, 256:512]
+        if summed:
+            point(i, 4 + j)
+    carry[...] = y_ref[3]
+
+    @pl.when(i == 4)
     def _():
-        carry[...] = y0_ref[...]
-
-    for j, (n0, n1) in enumerate(((0, 256), (128, 512), (384, 640))):
-        if summed:
-            point(i, 1 + j)
-        grads = []
-        for pp in range(4):
-            r = pp % 2
-            at = 2 * i + pp // 2 + 1
-            lhs = jnp.concatenate([g2[at, :, n0:n1], g2[at - 1, :, n0:n1]], axis=1)
-            rhs = jnp.concatenate([b2_ref[r, 256 * j : 256 * j + 256, n0:n1], b2_ref[2 + r, 256 * j : 256 * j + 256, n0:n1]], axis=1)
-            back = dot_nt(lhs, rhs) * s1_ref[pp // 2, r, :, 256 * j : 256 * j + 256].astype(F32)
-            grads.append(back.astype(BF16))
-        grad = jnp.concatenate(grads, axis=0)
-        for t in range(2):
-            pieces = [y_ref[k - 1 + t, j] if k + t > 0 else carry[j] for k in range(4)]
-            lhs = jnp.concatenate(pieces, axis=0)
-            d1_ref[512 * t : 512 * t + 512, :] += dot_tn(lhs, grad)
-    carry[...] = y_ref[3]
-    if summed:
-        point(i, 4)
+        for j in range(3):
+            d1_ref[512:1024, :] += dot_tn(y_ref[3, j], grad[3, :, 256 * j : 256 * j + 256])
 
     @pl.when(i == 4)
     def _():
@@ -765,9 +818,11 @@
         take_band_three(d3_ref, o3_ref)
         if summed:
             kernels_out()
-            for f in range(4):
-                next_stage(f, 2)
+            for f, s in SUM_LAST:
+                enter(f, s)
             kernels_over()
+            for f in SUM_DONE:
+                leave(f, 2)
             kernels_done()
 
 
@@ -775,16 +830,19 @@
     rows = y.shape[2]
     sums = [(1024, 256), (4, 384, 256), (4, 384, 256), (4, 256, 128), (3, 384, 256)]
     own = [(256, 128), (512, 128), (576, 128)]
-    args = [y, y0, a1, s1, a2, s2, s3, fg, kern2, kern3]
+    args = [y, a1, s1, y0, a2, s2, s3, fg, kern2, kern3]
     in_specs = [
         pl.BlockSpec((4, 3, rows, 512), lambda i: (i, 0, 0, 0)),
-        once(y0.shape),
         pl.BlockSpec((2, 2, rows, 768), lambda i: (i, 0, 0, 0)),
         pl.BlockSpec((2, 2, rows, 768), lambda i: (i, 0, 0, 0)),
-        *[once(v.shape) for v in args[4:]],
+        *[pl.BlockSpec(memory_space=pl.ANY)] * 5,
+        *[once(v.shape) for v in args[8:]],
     ]
     scratch = [
-        pltpu.VMEM((3, rows, 512), BF16),
+        *[pltpu.VMEM(v.shape, BF16) for v in args[3:8]],
+        pltpu.SemaphoreType.DMA((5,)),
+        pltpu.VMEM((3, 2, 768, 256), BF16),
+        pltpu.VMEM((4, rows, 768), BF16),
         pltpu.VMEM((11, rows, 512), BF16),
         pltpu.VMEM((11, rows, 640), BF16),
         *[pltpu.VMEM(s, BF16) for s in BANDS[1:]],
@@ -806,7 +864,7 @@
             pltpu.VMEM((8, 80, 128), BF16),
             pltpu.VMEM((8, 80, 128), BF16),
             pltpu.VMEM((4, 80, 128), F32),
-            pltpu.SemaphoreType.DMA((2,)),
+            pltpu.SemaphoreType.DMA((len(SUM_FLOWS),)),
             pltpu.SemaphoreType.DMA((2, len(buffers), 3)),
             pltpu.SemaphoreType.DMA((4, 7)),
             pltpu.SemaphoreType.DMA((4, 7)),
@@ -830,18 +888,42 @@
     return high, (v - high.astype(F32)).astype(BF16)
 
 
+HEAD_COLUMNS = [(0, 1024), (1024, 2048), (2048, HALF)]
+
+
 def heads_kernel(atoms, acts, paired, f_ref, w_ref, bias_ref, slot_ref, row_ref, dw_out, fg_ref, prio_ref, stat_ref, *refs):
     if paired:
-        dw_ref, arrived, send, recv = refs
+        dw_ref, arrived, w_hbm, w_ref, summed, dw_hbm = *refs[:2], w_ref, refs[2], refs[3], dw_out
+        send, recv, load, save = refs[4:]
+        loads = [pltpu.make_async_copy(w_hbm.at[h], w_ref.at[h], load.at[h]) for h in range(2)]
+        start(loads)
         me = coordinates()
         other = device_at({**me, "c": 1 - me["c"]})
         barrier = pltpu.get_barrier_semaphore()
         pl.semaphore_signal(barrier, inc=1, **other)
-        pl.semaphore_wait(barrier, 1)
-        to_core = [
-            pltpu.make_async_remote_copy(dw_ref.at[h, :, 1 - me["c"]], arrived.at[h], send.at[h], recv.at[h], **other)
-            for h in range(2)
-        ]
+
+        def to_core(h, k):
+            lo, hi = HEAD_COLUMNS[k]
+            src = dw_ref.at[h, :, 1 - me["c"], :, :, :, lo:hi]
+            return pltpu.make_async_remote_copy(src, arrived.at[h, :, :, :, :, lo:hi], send.at[h, k], recv.at[h, k], **other)
+
+        def saving(h, k):
+            lo, hi = HEAD_COLUMNS[k]
+            return pltpu.make_async_copy(summed.at[h, :, :, :, :, lo:hi], dw_hbm.at[h, :, :, :, :, lo:hi], save.at[h, k])
+
+        def add_core(h, k):
+            lo, hi = HEAD_COLUMNS[k]
+            to_core(h, k).wait()
+
+            def one(j, _):
+                x, z, y = j // 8, (j // 2) % 4, j % 2
+                own = dw_ref[h, x, me["c"], z, y, :, lo:hi]
+                summed[h, x, z, y, :, lo:hi] = own + arrived[h, x, z, y, :, lo:hi]
+                return 0
+
+            lax.fori_loop(0, 16, one, 0)
+            saving(h, k).start()
+
 
     def put(h, lo, hi, v):
         v = v.astype(BF16)
@@ -852,16 +934,26 @@
 
     rows = f_ref.shape[0]
     slots = slot_ref.shape[0]
+    wide = 1024
+    lane = lax.broadcasted_iota(jnp.int32, (1, wide), 1)
+    selt = jnp.where(lax.broadcasted_iota(jnp.int32, (rows, slots), 0) == row_ref[...], 1.0, 0.0).astype(BF16)
+    action = slot_ref[:, atoms + 2 : atoms + 3]
+    which = jnp.where(lane < atoms, -1, jnp.where(lane < atoms * (acts + 1), (lane - atoms) // atoms, -2)).astype(F32)
+    coeff = jnp.where(which == -1.0, 1.0, 0.0) + jnp.where(which == action, 1.0, 0.0) - jnp.where(which >= 0.0, 1.0 / acts, 0.0)
+    atom = jnp.where(which >= -1.0, lane - atoms * (which.astype(jnp.int32) + 1), -1)
+    fold = jnp.where(lax.broadcasted_iota(jnp.int32, (128, wide), 0) == atom, 1.0, 0.0).astype(BF16)
     feats = f_ref[...]
-    pre = [dot_nt(feats, w_ref[k, :, :3200]) for k in range(2)]
+    pre = []
+    for k in range(2):
+        if paired:
+            loads[k].wait()
+        pre.append(dot_nt(feats, w_ref[k, :, :3200]))
     hidden, slope = [], []
     for k in range(2):
         a, s = silu_and_slope(pre[k])
         hidden.append(a.astype(BF16))
         slope.append(s)
     out_w = jnp.concatenate([w_ref[0, :, 3200:], w_ref[1, :, 3200:]], axis=1)
-    wide = out_w.shape[1]
-    lane = lax.broadcasted_iota(jnp.int32, (1, wide), 1)
     zero = jnp.zeros((), BF16)
     w_val = jnp.where(lane[:, :128] < atoms, out_w[:, :128].astype(F32), 0.0).astype(BF16)
     w_adv = jnp.where(lane >= atoms, out_w.astype(F32), 0.0).astype(BF16)
@@ -870,13 +962,7 @@
     logits = dot(hidden[1], w_adv) + bias
     logits = jnp.concatenate([logits[:, :128] + dot(hidden[0], w_val), logits[:, 128:]], axis=1)
     high, low = high_low(logits)
-    selt = jnp.where(lax.broadcasted_iota(jnp.int32, (rows, slots), 0) == row_ref[...], 1.0, 0.0).astype(BF16)
     per_slot = dot_tn(selt, high) + dot_tn(selt, low)
-    action = slot_ref[:, atoms + 2 : atoms + 3]
-    which = jnp.where(lane < atoms, -1, jnp.where(lane < atoms * (acts + 1), (lane - atoms) // atoms, -2)).astype(F32)
-    coeff = jnp.where(which == -1.0, 1.0, 0.0) + jnp.where(which == action, 1.0, 0.0) - jnp.where(which >= 0.0, 1.0 / acts, 0.0)
-    atom = jnp.where(which >= -1.0, lane - atoms * (which.astype(jnp.int32) + 1), -1)
-    fold = jnp.where(lax.broadcasted_iota(jnp.int32, (128, wide), 0) == atom, 1.0, 0.0).astype(BF16)
     high, low = high_low(per_slot * coeff)
     q = dot_nt(high, fold) + dot_nt(low, fold)
     lane_q = lax.broadcasted_iota(jnp.int32, (slots, 128), 1)
@@ -909,23 +995,23 @@
         (dot_nt(grad, w_adv) * slope[1]).astype(BF16),
     ]
     for k in range(2):
-        for lo, hi in ((0, 1024), (1024, 2048), (2048, 3200)):
+        for part, (lo, hi) in enumerate(((0, 1024), (1024, 2048), (2048, 3200))):
             put(k, lo, hi, dot_tn(pre_grad[k], f_ref[:, lo:hi]))
-        if paired:
-            to_core[k].start()
-    for lo, hi in ((0, 1024), (1024, 2048), (2048, 3200)):
+            if paired:
+                if (k, part) == (0, 0):
+                    pl.semaphore_wait(barrier, 1)
+                to_core(k, part).start()
+    for part, (lo, hi) in enumerate(((0, 1024), (1024, 2048), (2048, 3200))):
         back = dot(pre_grad[0], w_ref[0, :, lo:hi]) + dot(pre_grad[1], w_ref[1, :, lo:hi])
         fg_ref[:, lo:hi] = back.astype(BF16)
+        if paired:
+            add_core(0, part)
     if paired:
+        for part in range(3):
+            add_core(1, part)
         for h in range(2):
-            to_core[h].wait()
-
-            def one(j, _):
-                x, z, y = j // 8, (j // 2) % 4, j % 2
-                dw_out[h, x, z, y] = (dw_ref[h, x, me["c"], z, y].astype(F32) + arrived[h, x, z, y].astype(F32)).astype(BF16)
-                return 0
-
-            lax.fori_loop(0, 16, one, 0)
+            for part in range(3):
+                saving(h, part).wait()
 
 
 def heads(atoms, acts, feats, weights, bias, per_slot, rows_of_slot, paired=False):
@@ -936,12 +1022,19 @@
         scratch = [
             pltpu.VMEM((2, 2, 2, 4, 2, 16, HALF), BF16),
             pltpu.VMEM(block, BF16),
+            pltpu.VMEM(weights.shape, BF16),
+            pltpu.VMEM(block, BF16),
+            *[pltpu.SemaphoreType.DMA((2, 3)) for _ in range(2)],
             pltpu.SemaphoreType.DMA((2,)),
-            pltpu.SemaphoreType.DMA((2,)),
+            pltpu.SemaphoreType.DMA((2, 3)),
         ]
         params = dict(collective_id=3, has_side_effects=True)
+    vmem = pl.BlockSpec(memory_space=pltpu.VMEM)
+    large = pl.BlockSpec(memory_space=pl.ANY) if paired else vmem
     return pl.pallas_call(
         functools.partial(heads_kernel, atoms, acts, paired),
+        in_specs=[vmem, large, vmem, vmem, vmem],
+        out_specs=[large, vmem, vmem, vmem],
         out_shape=[
             jax.ShapeDtypeStruct(block if paired else weights.shape, BF16),
             jax.ShapeDtypeStruct(feats.shape, BF16),

time: 166 us -> 147 us (0.89)
  Pallas kernels: 164 us -> 146 us
    pallas_call x1, Pallas kernels: 71.4 us -> 62.1 us  [torso_backward(): pl.pallas_call(functools.partial(backward_kernel, summed is not None), gr...]
    pallas_call x1, Pallas kernels: 68 us -> 58.9 us  [torso_forward(): pl.pallas_call(functools.partial(forward_kernel, shared is not None), gri...]
where the time goes in v4:
time: 147 us
  Pallas kernels  146 us (99%)
    pallas_call x1, Pallas kernels, torso_backward(): pl.pallas_call(functools.partial(backward_kernel, summed is not None), gr...  62.1 us
    pallas_call x1, Pallas kernels, torso_forward(): pl.pallas_call(functools.partial(forward_kernel, shared is not None), gri...  58.9 us
    pallas_call x1, Pallas kernels, heads(): pl.pallas_call(functools.partial(heads_kernel, atoms, acts, paired), in_s...  22.7 us

profile of v4, /device:TPU:0, one launch (start us, length us, event | category | flops | bytes accessed | tf_op | source)
XLA Modules:
  0.0 147.2 jit_solution(12364175807251908037)
XLA Ops:
  0.7 58.9 %torso_forward.1 = (bf16[10,2,272,768]{3,2,1,0:T(8,128)(2,1)}, bf16[10,2,272,768]{3,2,1,0:T(8,128)(2,1)}, bf16[9,272,640]{2,1,0:T(8,128)(2,1)}, bf16[9,272,640]{...) custom-call(bf16[21,4,272,336]{3,2,1,0:T(8,128)(2,1)} %bitcast.21, ...), custom_call_target="tpu_custom_call" | custom-call | tf_op jit(solution)/shard_map/torso_forward/pallas_call | solution.py:598
  59.6 22.7 %heads.1 = (bf16[2,2,4,2,16,3712]{5,4,3,2,1,0:T(8,128)(2,1)}, bf16[272,3200]{1,0:T(8,128)(2,1)}, f32[1,512]{1,0:T(1,128)}, f32[16,128]{1,0:T(8,128)}) custom-call(bf16[272,3200]{1,0:T(8,128)(2,1)} %get-tuple-element.51.f_ref, bf16[2,512,3712]{2,1,0:T(8,128)(2,1)} %bitcast.23, f32[1,969]{1,0:T(1,128)} %bitcast.31, f32[512,128]{1,0:T(8,128)} %bitcast.26, ...), custom_call_target="tpu_custom_call" | custom-call | tf_op jit(solution)/shard_map/heads/pallas_call | solution.py:1034
  82.2 0.0 copy-start
  82.3 62.1 %torso_backward.1 = (f32[2,16,3712]{2,1,0:T(8,128)}, f32[16,128]{1,0:T(8,128)}, f32[80,128]{1,0:T(8,128)}) custom-call(bf16[20,3,272,512]{3,2,1,0:T(8,128)(2,1)} %get-tuple-element.44.refs_0_, bf16[10,2,272,768]{3,2,1,0:T(8,128)(2,1)} %get-tuple-element.45.refs_1_, bf16[10,2,272,768]{3,2,1,0:T(8,128)(2,1)} %get-tuple-element.46.refs_2_, ...), custom_call_target="tpu_custom_call" | custom-call | tf_op jit(solution)/shard_map/torso_backward/pallas_call | solution.py:874
  144.4 2.2 %outputs.1 = (f32[1,1]{1,0:T(1,128)}, f32[32,32]{1,0:T(8,128)}, f32[64,64]{1,0:T(8,128)}, f32[64,72]{1,0:T(8,128)}, f32[2,16,3136]{2,1,0:T(8,128)}, /*index=5*/f...) custom-call(f32[2,16,3712]{2,1,0:T(8,128)} %get-tuple-element.59.dsu, ...), custom_call_target="tpu_custom_call" | custom-call | tf_op jit(solution)/shard_map/outputs/pallas_call | solution.py:1082
  146.6 0.0 copy-done
  146.6 0.6 copy.34
Async XLA Ops:
  82.2 64.4 %copy-start = (f32[1,512]{1,0:T(1,128)S(1)}, f32[1,512]{1,0:T(1,128)}, u32[]{:S(2)}) copy-start(f32[1,512]{1,0:T(1,128)} %get-tuple-element.74) | copy-start | bytes 6148

commit v5 on v4

--- a/solution.py
+++ b/solution.py
@@ -103,7 +103,8 @@
                 h = col // 4
                 total = total + jnp.where(lane + 4 * h == col, d1[at : at + 16, 128 * h : 128 * h + 128], 0.0)
             at = ((u // 4) * 2 + v) * 64 + (u % 4) * 16
-            out[at : at + 16, :] = fold_lanes(total, 32)
+            out[at : at + 16, :] = total
+    out[...] = fold_lanes(out[...], 32)
 
 
 def take_band_two(blocks, out):
@@ -118,7 +119,8 @@
                     piece = ref[u, at : at + 32, 128 * (c // 2) : 128 * (c // 2) + 128]
                     total = total + jnp.where((lane < 64) == (c % 2 == 0), piece, 0.0)
             at = ((u // 2) * 2 + v // 2) * 128 + ((u % 2) * 2 + v % 2) * 32
-            out[at : at + 32, :] = fold_lanes(total, 64)
+            out[at : at + 32, :] = total
+    out[...] = fold_lanes(out[...], 64)
 
 
 def take_band_three(d3, out):
@@ -130,7 +132,8 @@
                 piece = d3[u, 64 * (c + v) : 64 * (c + v) + 64, 128 * (c // 2) : 128 * (c // 2) + 128]
                 total = total + jnp.where((lane < 64) == (c % 2 == 0), piece, 0.0)
             at = (u * 3 + v) * 64
-            out[at : at + 64, :] = fold_lanes(total, 64)
+            out[at : at + 64, :] = total
+    out[...] = fold_lanes(out[...], 64)
 
 
 def coordinates():
@@ -360,13 +363,27 @@
         (sw,), refs = refs[:1], refs[1:]
     else:
         (x_ref, xn_ref, k1_ref, k2_ref, k3_ref), refs = refs[:5], refs[5:]
-    (a1_ref, s1_ref, *whole_out, y_ref, y0_ref), refs = refs[:8], refs[8:]
+    (a1_out, s1_out, *whole_out, y_out, y0_ref), refs = refs[:8], refs[8:]
     if shared:
         (w_out, slot_out, k2_ref, k3_ref), refs = refs[:4], refs[4:]
-    (carry, a1s, b1_ref, b2_ref, b3_ref, *whole, whole_sem), refs = refs[:10], refs[10:]
+    (carry, a1s, b1_ref, b2_ref, b3_ref, *whole, whole_sem, slopes_one, shifted, step_sem), refs = refs[:13], refs[13:]
     a2_ref, s2_ref, f_ref, s3_ref = whole
     i = pl.program_id(0)
     rows = x_ref.shape[2]
+    s1_ref, y_ref = slopes_one.at[lax.rem(i, 2)], shifted.at[lax.rem(i, 2)]
+
+    def step_copies(step):
+        slot, two = lax.rem(step, 2), pl.ds(2 * step, 2)
+        return [
+            pltpu.make_async_copy(a1s.at[two], a1_out.at[two], step_sem.at[slot, 0]),
+            pltpu.make_async_copy(slopes_one.at[slot], s1_out.at[two], step_sem.at[slot, 1]),
+            pltpu.make_async_copy(shifted.at[slot], y_out.at[pl.ds(4 * step, 4)], step_sem.at[slot, 2]),
+        ]
+
+    @pl.when(i >= 2)
+    def _():
+        finish(step_copies(i - 2))
+
     if shared:
         k1_ref, shard, kern_own, kern_buf, staged, slot_src, slot_buf, kern_s, kern_r, slot_s, slot_r, own_sem, sems, core_sems = refs
         flow_stage = {
@@ -474,12 +491,12 @@
             lhs = jnp.concatenate([carry[j] if pp == 0 else y_ref[pp - 1, j], y_ref[pp, j]], axis=1)
             act, slope = silu_and_slope(dot(lhs, b1_ref[...]))
             act = act.astype(BF16)
-            a1_ref[pp // 2, pp % 2, :, 256 * j : 256 * j + 256] = act
             a1s[2 * i + pp // 2, pp % 2, :, 256 * j : 256 * j + 256] = act
             s1_ref[pp // 2, pp % 2, :, 256 * j : 256 * j + 256] = slope.astype(BF16)
         if shared:
             point(i, pp)
     carry[...] = y_ref[3]
+    start(step_copies(i))
 
     def second(p):
         for lo, hi, n0, n1 in ((0, 384, 0, 256), (256, 640, 256, 512), (512, 768, 512, 640)):
@@ -541,6 +558,8 @@
         if shared:
             end()
         finish(leaving)
+        for step in (i - 1, i):
+            finish(step_copies(step))
 
 
 def full(shape):
@@ -559,9 +578,8 @@
     shapes = [(10, 2, rows, 768)] * 2 + [(9, rows, 640)] * 2 + [(rows, 3200)] * 2 + [(20, 3, rows, 512), (3, rows, 512)]
     args = [x, x, *kernels]
     out_specs = (
-        [pl.BlockSpec((2, 2, rows, 768), lambda i: (i, 0, 0, 0))] * 2
-        + [pl.BlockSpec(memory_space=pl.ANY)] * 4
-        + [pl.BlockSpec((4, 3, rows, 512), lambda i: (i, 0, 0, 0)), once((3, rows, 512))]
+        [pl.BlockSpec(memory_space=pl.ANY)] * 7
+        + [once((3, rows, 512))]
     )
     out_shape = [jax.ShapeDtypeStruct(s, BF16) for s in shapes]
     scratch = [
@@ -570,6 +588,9 @@
         *[pltpu.VMEM(s, BF16) for s in BANDS],
         *[pltpu.VMEM(s, BF16) for s in shapes[2:6]],
         pltpu.SemaphoreType.DMA((4,)),
+        pltpu.VMEM((2, 2, 2, rows, 768), BF16),
+        pltpu.VMEM((2, 4, 3, rows, 512), BF16),
+        pltpu.SemaphoreType.DMA((2, 3)),
     ]
     params = {}
     if shared is not None:
@@ -611,30 +632,41 @@
     )(*args)
 
 
-def pack_kernels(d, o1, o2, o3):
+KERNEL_ROWS = [(72, 8, 16), (0, 72, 80)]
+
+
+def pack_first(d, o1):
+    lane = lax.broadcasted_iota(jnp.int32, (8, 128), 1) // 32
+    one = jnp.zeros((8, 128), F32)
+    for k in range(4):
+        one = jnp.where(lane == k, o1[32 * d + 8 * k : 32 * d + 8 * k + 8, :], one)
+    return jnp.concatenate([one, jnp.zeros((8, 128), F32)], axis=0)
+
+
+def pack_others(d, o2, o3):
     lane = lax.broadcasted_iota(jnp.int32, (32, 128), 1)
     two = jnp.where(lane < 64, o2[64 * d : 64 * d + 32, :], o2[64 * d + 32 : 64 * d + 64, :])
     three = jnp.where(lane < 64, o3[72 * d : 72 * d + 32, :], o3[72 * d + 32 : 72 * d + 64, :])
-    lane = lane[:8] // 32
-    one = jnp.zeros((8, 128), F32)
-    for k in range(4):
-        one = jnp.where(lane == k, o1[32 * d + 8 * k : 32 * d + 8 * k + 8, :], one)
-    return jnp.concatenate([two, three, o3[72 * d + 64 : 72 * d + 72, :], one], axis=0)
+    return jnp.concatenate([two, three, o3[72 * d + 64 : 72 * d + 72, :], jnp.zeros((8, 128), F32)], axis=0)
 
 
 BACK_LANES = ((0, 256), (128, 512), (384, 640))
 
 
 def backward_kernel(summed, *refs):
-    (y_ref, a1_ref, s1_ref, *whole_in, k2_ref, k3_ref), refs = refs[:10], refs[10:]
+    (*streams, y0_in, a2_in, s2_in, s3_in, fg_in, k2_ref, k3_ref), refs = refs[:10], refs[10:]
+    whole_in = (y0_in, a2_in, s2_in, s3_in, fg_in)
     if summed:
         (dw_ref, stat_ref, dsum_ref, stat_out, kern_out), refs = refs[:5], refs[5:]
     (o1_ref, o2_ref, o3_ref), refs = refs[:3], refs[3:]
-    (carry, *whole, whole_sem, back, grad, g3, g2, b2_ref, b3_ref, d1_ref, d2a_ref, d2b_ref, d2c_ref, d3_ref), refs = refs[:17], refs[17:]
+    (carry, *whole, whole_sem), refs = refs[:6], refs[6:]
+    slots, step_sem, refs = refs[:3], refs[3], refs[4:]
+    (back, grad, g3, g2, b2_ref, b3_ref, d1_ref, d2a_ref, d2b_ref, d2c_ref, d3_ref), refs = refs[:11], refs[11:]
     a2_ref, s2_ref, s3_ref, fg_ref = whole
     coming = [pltpu.make_async_copy(whole_in[k], (carry, *whole)[k], whole_sem.at[k]) for k in range(5)]
     if summed:
-        (acc, stat_dp, stat_mp, kern_send, kern_dp, kern_mp, load_sem, sems, send_s, recv_s), bufs = refs[:10], refs[10:]
+        (acc, stat_dp, stat_mp, load_sem, sems, send_s, recv_s), bufs = refs[:7], refs[7:]
+        kern_bufs, bufs = bufs[:6], bufs[6:]
         me = coordinates()
         stages = {}
         at = 0
@@ -654,10 +686,13 @@
             src = stat_ref if k == 0 else stat_mp.at[lax.axis_index("mp")]
             return share(axis, count, lambda _: src, (stat_dp, stat_mp)[k], send_s.at[k], recv_s.at[k])
 
-        def kern_copies(axis, count, k):
+        def kern_copies(group, k):
+            kern_send, kern_dp, kern_mp = kern_bufs[3 * group : 3 * group + 3]
+            sem = 2 + 2 * group + k
+            if k == 1:
+                return share("mp", 4, lambda _: kern_mp.at[lax.axis_index("mp")], kern_mp, send_s.at[sem], recv_s.at[sem])
             ids = [lax.rem(lax.axis_index("dp") + j, 8) for j in range(1, 8)]
-            src = (lambda j: kern_send.at[ids[j]]) if k == 0 else (lambda _: kern_mp.at[lax.axis_index("mp")])
-            return share(axis, count, src, (kern_dp, kern_mp)[k], send_s.at[2 + k], recv_s.at[2 + k])
+            return share("dp", 8, lambda j: kern_send.at[ids[j]], kern_dp, send_s.at[sem], recv_s.at[sem])
 
         def first():
             start(list(loaded.values()))
@@ -692,7 +727,8 @@
                         for f, s in entries:
                             enter(f, s)
 
-            for at, where, what in ((0, 5, stats_over), (1, 6, stats_done)):
+            extra = [(0, 5, stats_over), (1, 6, stats_done), (4, 3, lambda: kernel_out(1))]
+            for at, where, what in extra:
                 if where == k:
 
                     @pl.when(step == at)
@@ -703,29 +739,50 @@
             finish(stat_copies("mp", 4, 1))
             stat_out[...] = in_order(stat_mp, 4)
 
-        def kernels_out():
+        def kernel_out(group):
+            kern_send, kern_dp, _ = kern_bufs[3 * group : 3 * group + 3]
+            if group == 0:
+                take_band_one(d1_ref, o1_ref)
+            else:
+                take_band_two(((d2a_ref, 0, 0, 4), (d2b_ref, 8, 4, 4), (d2c_ref, 16, 8, 1)), o2_ref)
+                take_band_three(d3_ref, o3_ref)
             for d in range(8):
-                kern_send[d] = pack_kernels(d, o1_ref, o2_ref, o3_ref).astype(BF16)
+                rows_out = pack_first(d, o1_ref) if group == 0 else pack_others(d, o2_ref, o3_ref)
+                kern_send[d] = rows_out.astype(BF16)
             kern_dp[lax.axis_index("dp")] = kern_send[lax.axis_index("dp")]
-            start(kern_copies("dp", 8, 0))
-
-        def kernels_over():
-            finish(kern_copies("dp", 8, 0))
+            start(kern_copies(group, 0))
+
+        def kernel_over(group):
+            _, kern_dp, kern_mp = kern_bufs[3 * group : 3 * group + 3]
+            finish(kern_copies(group, 0))
             kern_mp[lax.axis_index("mp")] = in_order(kern_dp, 8)
-            start(kern_copies("mp", 4, 1))
-
-        def kernels_done():
-            finish(kern_copies("mp", 4, 1))
-            kern_out[...] = in_order(kern_mp, 4) / stat_out[9:10, :]
+            start(kern_copies(group, 1))
+
+        def kernel_done(group):
+            at, count, _ = KERNEL_ROWS[group]
+            finish(kern_copies(group, 1))
+            total = in_order(kern_bufs[3 * group + 2], 4) / stat_out[9:10, :]
+            kern_out[at : at + count, :] = total[:count]
 
     i = pl.program_id(0)
-    rows = y_ref.shape[2]
+    rows = g3.shape[1]
+    y_ref, a1_ref, s1_ref = (slot.at[lax.rem(i, 2)] for slot in slots)
+
+    def step_copies(step):
+        return [
+            pltpu.make_async_copy(
+                streams[k].at[pl.ds(count * step, count)], slots[k].at[lax.rem(step, 2)], step_sem.at[lax.rem(step, 2), k]
+            )
+            for k, count in enumerate((4, 2, 2))
+        ]
+
 
     @pl.when(i == 0)
     def _():
         if summed:
             greet()
         start(coming[::-1])
+        start(step_copies(i))
         b2_ref[...] = jnp.zeros_like(b2_ref)
         b3_ref[...] = jnp.zeros_like(b3_ref)
         fill_band_two(k2_ref, b2_ref)
@@ -776,6 +833,12 @@
             if summed:
                 point(i, "a%d" % (4 + at))
 
+    finish(step_copies(i))
+
+    @pl.when(i < 4)
+    def _():
+        start(step_copies(i + 1))
+
     for r in range(2):
         for ref, lo, hi, n0, n1 in ((d2a_ref, 0, 384, 0, 256), (d2b_ref, 256, 640, 256, 512), (d2c_ref, 512, 768, 512, 640)):
             lhs = a1_ref[:, r, :, lo:hi].reshape(2 * rows, hi - lo)
@@ -813,17 +876,20 @@
 
     @pl.when(i == 4)
     def _():
-        take_band_one(d1_ref, o1_ref)
-        take_band_two(((d2a_ref, 0, 0, 4), (d2b_ref, 8, 4, 4), (d2c_ref, 16, 8, 1)), o2_ref)
-        take_band_three(d3_ref, o3_ref)
         if summed:
-            kernels_out()
+            kernel_out(0)
             for f, s in SUM_LAST:
                 enter(f, s)
-            kernels_over()
+            kernel_over(1)
+            kernel_over(0)
             for f in SUM_DONE:
                 leave(f, 2)
-            kernels_done()
+            kernel_done(1)
+            kernel_done(0)
+        else:
+            take_band_one(d1_ref, o1_ref)
+            take_band_two(((d2a_ref, 0, 0, 4), (d2b_ref, 8, 4, 4), (d2c_ref, 16, 8, 1)), o2_ref)
+            take_band_three(d3_ref, o3_ref)
 
 
 def torso_backward(y, y0, a1, s1, a2, s2, s3, fg, kern2, kern3, summed=None):
@@ -832,15 +898,16 @@
     own = [(256, 128), (512, 128), (576, 128)]
     args = [y, a1, s1, y0, a2, s2, s3, fg, kern2, kern3]
     in_specs = [
-        pl.BlockSpec((4, 3, rows, 512), lambda i: (i, 0, 0, 0)),
-        pl.BlockSpec((2, 2, rows, 768), lambda i: (i, 0, 0, 0)),
-        pl.BlockSpec((2, 2, rows, 768), lambda i: (i, 0, 0, 0)),
-        *[pl.BlockSpec(memory_space=pl.ANY)] * 5,
+        *[pl.BlockSpec(memory_space=pl.ANY)] * 8,
         *[once(v.shape) for v in args[8:]],
     ]
     scratch = [
         *[pltpu.VMEM(v.shape, BF16) for v in args[3:8]],
         pltpu.SemaphoreType.DMA((5,)),
+        pltpu.VMEM((2, 4, 3, rows, 512), BF16),
+        pltpu.VMEM((2, 2, 2, rows, 768), BF16),
+        pltpu.VMEM((2, 2, 2, rows, 768), BF16),
+        pltpu.SemaphoreType.DMA((2, 3)),
         pltpu.VMEM((3, 2, 768, 256), BF16),
         pltpu.VMEM((4, rows, 768), BF16),
         pltpu.VMEM((11, rows, 512), BF16),
@@ -861,13 +928,15 @@
             pltpu.VMEM(block, BF16),
             pltpu.VMEM((8, 16, 128), F32),
             pltpu.VMEM((4, 16, 128), F32),
-            pltpu.VMEM((8, 80, 128), BF16),
-            pltpu.VMEM((8, 80, 128), BF16),
-            pltpu.VMEM((4, 80, 128), F32),
             pltpu.SemaphoreType.DMA((len(SUM_FLOWS),)),
             pltpu.SemaphoreType.DMA((2, len(buffers), 3)),
-            pltpu.SemaphoreType.DMA((4, 7)),
-            pltpu.SemaphoreType.DMA((4, 7)),
+            pltpu.SemaphoreType.DMA((6, 7)),
+            pltpu.SemaphoreType.DMA((6, 7)),
+            *[
+                pltpu.VMEM((count, padded, 128), kind)
+                for _, _, padded in KERNEL_ROWS
+                for count, kind in ((8, BF16), (8, BF16), (4, F32))
+            ],
             *[pltpu.VMEM(s, BF16) for s in buffers],
         ]
         params = dict(collective_id=1, has_side_effects=True)
@@ -895,8 +964,12 @@
     if paired:
         dw_ref, arrived, w_hbm, w_ref, summed, dw_hbm = *refs[:2], w_ref, refs[2], refs[3], dw_out
         send, recv, load, save = refs[4:]
-        loads = [pltpu.make_async_copy(w_hbm.at[h], w_ref.at[h], load.at[h]) for h in range(2)]
-        start(loads)
+        loads = {
+            (h, k): pltpu.make_async_copy(w_hbm.at[h, :, lo:hi], w_ref.at[h, :, lo:hi], load.at[h, k])
+            for h in range(2)
+            for k, (lo, hi) in enumerate(HEAD_COLUMNS)
+        }
+        start(list(loads.values()))
         me = coordinates()
         other = device_at({**me, "c": 1 - me["c"]})
         barrier = pltpu.get_barrier_semaphore()
@@ -942,12 +1015,15 @@
     coeff = jnp.where(which == -1.0, 1.0, 0.0) + jnp.where(which == action, 1.0, 0.0) - jnp.where(which >= 0.0, 1.0 / acts, 0.0)
     atom = jnp.where(which >= -1.0, lane - atoms * (which.astype(jnp.int32) + 1), -1)
     fold = jnp.where(lax.broadcasted_iota(jnp.int32, (128, wide), 0) == atom, 1.0, 0.0).astype(BF16)
-    feats = f_ref[...]
     pre = []
-    for k in range(2):
-        if paired:
-            loads[k].wait()
-        pre.append(dot_nt(feats, w_ref[k, :, :3200]))
+    for h in range(2):
+        total = 0.0
+        for k, (lo, hi) in enumerate(HEAD_COLUMNS):
+            if paired:
+                loads[h, k].wait()
+            hi = min(hi, 3200)
+            total = total + dot_nt(f_ref[:, lo:hi], w_ref[h, :, lo:hi])
+        pre.append(total)
     hidden, slope = [], []
     for k in range(2):
         a, s = silu_and_slope(pre[k])
@@ -1024,9 +1100,7 @@
             pltpu.VMEM(block, BF16),
             pltpu.VMEM(weights.shape, BF16),
             pltpu.VMEM(block, BF16),
-            *[pltpu.SemaphoreType.DMA((2, 3)) for _ in range(2)],
-            pltpu.SemaphoreType.DMA((2,)),
-            pltpu.SemaphoreType.DMA((2, 3)),
+            *[pltpu.SemaphoreType.DMA((2, 3))] * 4,
         ]
         params = dict(collective_id=3, has_side_effects=True)
     vmem = pl.BlockSpec(memory_space=pltpu.VMEM)

time: 147 us -> 143 us (0.973)
  Pallas kernels: 146 us -> 141 us
    pallas_call x1, Pallas kernels: 58.9 us -> 56.6 us  [torso_forward(): pl.pallas_call(functools.partial(forward_kernel, shared is not None), gri...]
    pallas_call x1, Pallas kernels: 62.1 us -> 60 us  [torso_backward(): pl.pallas_call(functools.partial(backward_kernel, summed is not None), gr...]
where the time goes in v5:
time: 143 us; the launch traced here: 142 us
  Pallas kernels  141 us (99%)
    pallas_call x1, Pallas kernels, torso_backward(): pl.pallas_call(functools.partial(backward_kernel, summed is not None), gr...  60 us
    pallas_call x1, Pallas kernels, torso_forward(): pl.pallas_call(functools.partial(forward_kernel, shared is not None), gri...  56.6 us
    pallas_call x1, Pallas kernels, heads(): pl.pallas_call(functools.partial(heads_kernel, atoms, acts, paired), in_s...  22.4 us

profile of v5, /device:TPU:0, one launch (start us, length us, event | category | flops | bytes accessed | tf_op | source)
XLA Modules:
  0.0 142.5 jit_solution(15911645174578780606)
XLA Ops:
  0.7 56.6 %torso_forward.1 = (bf16[10,2,272,768]{3,2,1,0:T(8,128)(2,1)}, bf16[10,2,272,768]{3,2,1,0:T(8,128)(2,1)}, bf16[9,272,640]{2,1,0:T(8,128)(2,1)}, bf16[9,272,640]{...) custom-call(bf16[21,4,272,336]{3,2,1,0:T(8,128)(2,1)} %bitcast.21, ...), custom_call_target="tpu_custom_call" | custom-call | tf_op jit(solution)/shard_map/torso_forward/pallas_call | solution.py:619
  57.3 22.4 %heads.1 = (bf16[2,2,4,2,16,3712]{5,4,3,2,1,0:T(8,128)(2,1)}, bf16[272,3200]{1,0:T(8,128)(2,1)}, f32[1,512]{1,0:T(1,128)}, f32[16,128]{1,0:T(8,128)}) custom-call(bf16[272,3200]{1,0:T(8,128)(2,1)} %get-tuple-element.51.f_ref, bf16[2,512,3712]{2,1,0:T(8,128)(2,1)} %bitcast.23, f32[1,969]{1,0:T(1,128)} %bitcast.31, f32[512,128]{1,0:T(8,128)} %bitcast.26, ...), custom_call_target="tpu_custom_call" | custom-call | tf_op jit(solution)/shard_map/heads/pallas_call | solution.py:1108
  79.7 0.0 copy-start
  79.7 60.0 %torso_backward.1 = (f32[2,16,3712]{2,1,0:T(8,128)}, f32[16,128]{1,0:T(8,128)}, f32[80,128]{1,0:T(8,128)}) custom-call(bf16[20,3,272,512]{3,2,1,0:T(8,128)(2,1)} %get-tuple-element.44.refs_0_, bf16[10,2,272,768]{3,2,1,0:T(8,128)(2,1)} %get-tuple-element.45.refs_1_, bf16[10,2,272,768]{3,2,1,0:T(8,128)(2,1)} %get-tuple-element.46.refs_2_, ...), custom_call_target="tpu_custom_call" | custom-call | tf_op jit(solution)/shard_map/torso_backward/pallas_call | solution.py:943
  139.7 2.2 %outputs.1 = (f32[1,1]{1,0:T(1,128)}, f32[32,32]{1,0:T(8,128)}, f32[64,64]{1,0:T(8,128)}, f32[64,72]{1,0:T(8,128)}, f32[2,16,3136]{2,1,0:T(8,128)}, /*index=5*/f...) custom-call(f32[2,16,3712]{2,1,0:T(8,128)} %get-tuple-element.59.dsu, ...), custom_call_target="tpu_custom_call" | custom-call | tf_op jit(solution)/shard_map/outputs/pallas_call | solution.py:1156
  141.9 0.0 copy-done
  141.9 0.6 copy.34
Async XLA Ops:
  79.7 62.2 %copy-start = (f32[1,512]{1,0:T(1,128)S(1)}, f32[1,512]{1,0:T(1,128)}, u32[]{:S(2)}) copy-start(f32[1,512]{1,0:T(1,128)} %get-tuple-element.74) | copy-start | bytes 6148

commit v6 on v5

--- a/solution.py
+++ b/solution.py
@@ -358,18 +358,19 @@
 
 def forward_kernel(shared, *refs):
     if shared:
-        ins, refs = refs[:18], refs[18:]
-        (x_ref, xn_ref, c1, c2, c3t, hm, hs, hb, fn, hn, vm, vs, am, adv_s, on, tt, cnt, act), refs = ins, refs
+        ins, refs = refs[:17], refs[17:]
+        (x_in, c1, c2, c3t, hm, hs, hb, fn, hn, vm, vs, am, adv_s, on, tt, cnt, act), refs = ins, refs
         (sw,), refs = refs[:1], refs[1:]
     else:
-        (x_ref, xn_ref, k1_ref, k2_ref, k3_ref), refs = refs[:5], refs[5:]
+        (x_in, k1_ref, k2_ref, k3_ref), refs = refs[:4], refs[4:]
     (a1_out, s1_out, *whole_out, y_out, y0_ref), refs = refs[:8], refs[8:]
     if shared:
         (w_out, slot_out, k2_ref, k3_ref), refs = refs[:4], refs[4:]
-    (carry, a1s, b1_ref, b2_ref, b3_ref, *whole, whole_sem, slopes_one, shifted, step_sem), refs = refs[:13], refs[13:]
+    (carry, a1s, b1_ref, b2_ref, b3_ref, *whole, whole_sem, slopes_one, shifted, step_sem, x_first, x_slots, x_sem), refs = refs[:16], refs[16:]
     a2_ref, s2_ref, f_ref, s3_ref = whole
     i = pl.program_id(0)
-    rows = x_ref.shape[2]
+    rows = x_first.shape[1]
+    x_ref = x_slots.at[lax.rem(i, 2)]
     s1_ref, y_ref = slopes_one.at[lax.rem(i, 2)], shifted.at[lax.rem(i, 2)]
 
     def step_copies(step):
@@ -379,6 +380,16 @@
             pltpu.make_async_copy(slopes_one.at[slot], s1_out.at[two], step_sem.at[slot, 1]),
             pltpu.make_async_copy(shifted.at[slot], y_out.at[pl.ds(4 * step, 4)], step_sem.at[slot, 2]),
         ]
+
+    def frame_copy(step):
+        slot = lax.rem(step, 2)
+        return pltpu.make_async_copy(x_in.at[pl.ds(4 * step + 1, 4)], x_slots.at[slot], x_sem.at[slot])
+
+    first_frames = pltpu.make_async_copy(x_in.at[0], x_first, x_sem.at[2])
+
+    @pl.when(i == 0)
+    def _():
+        start([first_frames, frame_copy(i)])
 
     @pl.when(i >= 2)
     def _():
@@ -467,8 +478,9 @@
     def prepare():
         b2_ref[...] = jnp.zeros_like(b2_ref)
         b3_ref[...] = jnp.zeros_like(b3_ref)
+        finish([first_frames])
         for r in range(4):
-            for j, blk in enumerate(shifted_blocks(x_ref[0, r])):
+            for j, blk in enumerate(shifted_blocks(x_first[r])):
                 carry[j, :, 128 * r : 128 * r + 128] = blk
         y0_ref[...] = carry[...]
 
@@ -482,10 +494,15 @@
         fill_band_two(k2_ref, b2_ref)
         fill_band_three(k3_ref, b3_ref)
 
+    finish([frame_copy(i)])
+
+    @pl.when(i < 4)
+    def _():
+        start([frame_copy(i + 1)])
+
     for pp in range(4):
         for r in range(4):
-            src = x_ref[pp + 1, r] if pp < 3 else xn_ref[0, r]
-            for j, blk in enumerate(shifted_blocks(src)):
+            for j, blk in enumerate(shifted_blocks(x_ref[pp, r])):
                 y_ref[pp, j, :, 128 * r : 128 * r + 128] = blk
         for j in range(3):
             lhs = jnp.concatenate([carry[j] if pp == 0 else y_ref[pp - 1, j], y_ref[pp, j]], axis=1)
@@ -576,7 +593,7 @@
 def torso_forward(x, kernels, shared=None):
     rows = x.shape[2]
     shapes = [(10, 2, rows, 768)] * 2 + [(9, rows, 640)] * 2 + [(rows, 3200)] * 2 + [(20, 3, rows, 512), (3, rows, 512)]
-    args = [x, x, *kernels]
+    args = [x, *kernels]
     out_specs = (
         [pl.BlockSpec(memory_space=pl.ANY)] * 7
         + [once((3, rows, 512))]
@@ -591,6 +608,9 @@
         pltpu.VMEM((2, 2, 2, rows, 768), BF16),
         pltpu.VMEM((2, 4, 3, rows, 512), BF16),
         pltpu.SemaphoreType.DMA((2, 3)),
+        pltpu.VMEM((4, rows, 336), BF16),
+        pltpu.VMEM((2, 4, 4, rows, 336), BF16),
+        pltpu.SemaphoreType.DMA((3,)),
     ]
     params = {}
     if shared is not None:
@@ -620,9 +640,8 @@
         functools.partial(forward_kernel, shared is not None),
         grid=(5,),
         in_specs=[
-            pl.BlockSpec((4, 4, rows, 336), lambda i: (i, 0, 0, 0)),
-            pl.BlockSpec((1, 4, rows, 336), lambda i: (4 * i + 4, 0, 0, 0)),
-            *[once(v.shape) for v in args[2:]],
+            pl.BlockSpec(memory_space=pl.ANY),
+            *[once(v.shape) for v in args[1:]],
         ],
         out_specs=out_specs,
         out_shape=out_shape,

time: 143 us -> 141 us (0.986)
    pallas_call x1, Pallas kernels: 56.6 us -> 54.9 us  [torso_forward(): pl.pallas_call(functools.partial(forward_kernel, shared is not None), gri...]
where the time goes in v6:
time: 141 us
  Pallas kernels  140 us (99%)
    pallas_call x1, Pallas kernels, torso_backward(): pl.pallas_call(functools.partial(backward_kernel, summed is not None), gr...  60 us
    pallas_call x1, Pallas kernels, torso_forward(): pl.pallas_call(functools.partial(forward_kernel, shared is not None), gri...  54.9 us
    pallas_call x1, Pallas kernels, heads(): pl.pallas_call(functools.partial(heads_kernel, atoms, acts, paired), in_s...  22.4 us

profile of v6, /device:TPU:0, one launch (start us, length us, event | category | flops | bytes accessed | tf_op | source)
XLA Modules:
  0.0 140.8 jit_solution(10802682662362889061)
XLA Ops:
  0.7 54.9 %torso_forward.1 = (bf16[10,2,272,768]{3,2,1,0:T(8,128)(2,1)}, bf16[10,2,272,768]{3,2,1,0:T(8,128)(2,1)}, bf16[9,272,640]{2,1,0:T(8,128)(2,1)}, bf16[9,272,640]{...) custom-call(bf16[21,4,272,336]{3,2,1,0:T(8,128)(2,1)} %bitcast.21, ...), custom_call_target="tpu_custom_call" | custom-call | tf_op jit(solution)/shard_map/torso_forward/pallas_call | solution.py:639
  55.6 22.4 %heads.1 = (bf16[2,2,4,2,16,3712]{5,4,3,2,1,0:T(8,128)(2,1)}, bf16[272,3200]{1,0:T(8,128)(2,1)}, f32[1,512]{1,0:T(1,128)}, f32[16,128]{1,0:T(8,128)}) custom-call(bf16[272,3200]{1,0:T(8,128)(2,1)} %get-tuple-element.51.f_ref, bf16[2,512,3712]{2,1,0:T(8,128)(2,1)} %bitcast.22, f32[1,969]{1,0:T(1,128)} %bitcast.30, f32[512,128]{1,0:T(8,128)} %bitcast.25, ...), custom_call_target="tpu_custom_call" | custom-call | tf_op jit(solution)/shard_map/heads/pallas_call | solution.py:1127
  78.0 0.0 copy-start
  78.0 60.0 %torso_backward.1 = (f32[2,16,3712]{2,1,0:T(8,128)}, f32[16,128]{1,0:T(8,128)}, f32[80,128]{1,0:T(8,128)}) custom-call(bf16[20,3,272,512]{3,2,1,0:T(8,128)(2,1)} %get-tuple-element.44.refs_0_, bf16[10,2,272,768]{3,2,1,0:T(8,128)(2,1)} %get-tuple-element.45.refs_1_, bf16[10,2,272,768]{3,2,1,0:T(8,128)(2,1)} %get-tuple-element.46.refs_2_, ...), custom_call_target="tpu_custom_call" | custom-call | tf_op jit(solution)/shard_map/torso_backward/pallas_call | solution.py:962
  138.0 2.2 %outputs.1 = (f32[1,1]{1,0:T(1,128)}, f32[32,32]{1,0:T(8,128)}, f32[64,64]{1,0:T(8,128)}, f32[64,72]{1,0:T(8,128)}, f32[2,16,3136]{2,1,0:T(8,128)}, /*index=5*/f...) custom-call(f32[2,16,3712]{2,1,0:T(8,128)} %get-tuple-element.59.dsu, ...), custom_call_target="tpu_custom_call" | custom-call | tf_op jit(solution)/shard_map/outputs/pallas_call | solution.py:1175
  140.2 0.0 copy-done
  140.2 0.6 copy.34
Async XLA Ops:
  78.0 62.2 %copy-start = (f32[1,512]{1,0:T(1,128)S(1)}, f32[1,512]{1,0:T(1,128)}, u32[]{:S(2)}) copy-start(f32[1,512]{1,0:T(1,128)} %get-tuple-element.74) | copy-start | bytes 6148

commit v7 on v6

--- a/solution.py
+++ b/solution.py
@@ -1008,12 +1008,12 @@
             to_core(h, k).wait()
 
             def one(j, _):
-                x, z, y = j // 8, (j // 2) % 4, j % 2
-                own = dw_ref[h, x, me["c"], z, y, :, lo:hi]
-                summed[h, x, z, y, :, lo:hi] = own + arrived[h, x, z, y, :, lo:hi]
+                x, z = j // 4, j % 4
+                own = dw_ref[h, x, me["c"], z, :, :, lo:hi]
+                summed[h, x, z, :, :, lo:hi] = own + arrived[h, x, z, :, :, lo:hi]
                 return 0
 
-            lax.fori_loop(0, 16, one, 0)
+            lax.fori_loop(0, 8, one, 0)
             saving(h, k).start()
 
 

time: 141 us -> 140 us (level)
  no operation moved by 1% of the time
where the time goes in v7:
time: 140 us
  Pallas kernels  139 us (99%)
    pallas_call x1, Pallas kernels, torso_backward(): pl.pallas_call(functools.partial(backward_kernel, summed is not None), gr...  60 us
    pallas_call x1, Pallas kernels, torso_forward(): pl.pallas_call(functools.partial(forward_kernel, shared is not None), gri...  54.9 us
    pallas_call x1, Pallas kernels, heads(): pl.pallas_call(functools.partial(heads_kernel, atoms, acts, paired), in_s...  21.5 us

profile of v7, /device:TPU:0, one launch (start us, length us, event | category | flops | bytes accessed | tf_op | source)
XLA Modules:
  0.0 139.9 jit_solution(9731508937215196052)
XLA Ops:
  0.7 54.9 %torso_forward.1 = (bf16[10,2,272,768]{3,2,1,0:T(8,128)(2,1)}, bf16[10,2,272,768]{3,2,1,0:T(8,128)(2,1)}, bf16[9,272,640]{2,1,0:T(8,128)(2,1)}, bf16[9,272,640]{...) custom-call(bf16[21,4,272,336]{3,2,1,0:T(8,128)(2,1)} %bitcast.21, ...), custom_call_target="tpu_custom_call" | custom-call | tf_op jit(solution)/shard_map/torso_forward/pallas_call | solution.py:639
  55.6 21.5 %heads.1 = (bf16[2,2,4,2,16,3712]{5,4,3,2,1,0:T(8,128)(2,1)}, bf16[272,3200]{1,0:T(8,128)(2,1)}, f32[1,512]{1,0:T(1,128)}, f32[16,128]{1,0:T(8,128)}) custom-call(bf16[272,3200]{1,0:T(8,128)(2,1)} %get-tuple-element.51.f_ref, bf16[2,512,3712]{2,1,0:T(8,128)(2,1)} %bitcast.22, f32[1,969]{1,0:T(1,128)} %bitcast.30, f32[512,128]{1,0:T(8,128)} %bitcast.25, ...), custom_call_target="tpu_custom_call" | custom-call | tf_op jit(solution)/shard_map/heads/pallas_call | solution.py:1127
  77.1 0.0 copy-start
  77.2 60.0 %torso_backward.1 = (f32[2,16,3712]{2,1,0:T(8,128)}, f32[16,128]{1,0:T(8,128)}, f32[80,128]{1,0:T(8,128)}) custom-call(bf16[20,3,272,512]{3,2,1,0:T(8,128)(2,1)} %get-tuple-element.44.refs_0_, bf16[10,2,272,768]{3,2,1,0:T(8,128)(2,1)} %get-tuple-element.45.refs_1_, bf16[10,2,272,768]{3,2,1,0:T(8,128)(2,1)} %get-tuple-element.46.refs_2_, ...), custom_call_target="tpu_custom_call" | custom-call | tf_op jit(solution)/shard_map/torso_backward/pallas_call | solution.py:962
  137.1 2.2 %outputs.1 = (f32[1,1]{1,0:T(1,128)}, f32[32,32]{1,0:T(8,128)}, f32[64,64]{1,0:T(8,128)}, f32[64,72]{1,0:T(8,128)}, f32[2,16,3136]{2,1,0:T(8,128)}, /*index=5*/f...) custom-call(f32[2,16,3712]{2,1,0:T(8,128)} %get-tuple-element.59.dsu, ...), custom_call_target="tpu_custom_call" | custom-call | tf_op jit(solution)/shard_map/outputs/pallas_call | solution.py:1175
  139.3 0.0 copy-done
  139.3 0.6 copy.34
Async XLA Ops:
  77.1 62.2 %copy-start = (f32[1,512]{1,0:T(1,128)S(1)}, f32[1,512]{1,0:T(1,128)}, u32[]{:S(2)}) copy-start(f32[1,512]{1,0:T(1,128)} %get-tuple-element.74) | copy-start | bytes 6148
